TPU v7x, 32 devices: a whole 2x2x4 slice. The times are simulated.
32 devices in a mesh: groups: 2 (over y), seq: 8 (over z, x), head: 2 (over core).
Axes of the slice: x: 2, y: 2, z: 4, core: 2. Of those that a mesh axis runs over, the one named last changes fastest.
Arguments:
- text_query_rows: bfloat16 [2048, 8192], P(('groups', 'seq'), 'head'), parts along dimension 0, may hold values from -40 to 40, as said below
- text_key_value: bfloat16 [2, 2048, 1024], P(None, ('groups', 'seq'), 'head'), parts along dimension 1, may hold values from -4 to 4, as said below
- doc_ids: int32 [2048], P(('groups', 'seq')), parts along dimension 0, may hold values from 0 to 3, never falling along the last dimension, each value on 1 to 512 neighbouring positions
- tile_span: int32 [2048, 2], P(('groups', 'seq')), parts along dimension 0, may hold values from 0 to 8, as said below
- vision_hidden: bfloat16 [4096, 1280], P(('groups', 'seq')), parts along dimension 0, may hold values from -6 to 6
- vision_qkv: bfloat16 [3, 4096, 1280], P(None, ('groups', 'seq'), 'head'), parts along dimension 1, may hold values from -6 to 6, as said below
- vision_out_weight: bfloat16 [1280, 1280], P('head'), may hold values from -0.625 to 0.625
- cross_keyvalue_weight: bfloat16 [1280, 2, 1024], P('seq', None, 'head'), may hold values from -0.15625 to 0.15625
- cross_gate: float32 [64], P('head'), may hold values from -1.5 to 1.5
Outputs:
- attention_out: bfloat16 [2048, 8192], P(('groups', 'seq'), 'head'), parts along dimension 0
There are 2 independent parts, one for each index of `groups`. A program takes and returns all parts, laid end to end along the dimension named above; an argument that names none is the same for every part. Nothing has to cross between parts.
Inputs may be any that keep to these rules, and one draw needn't show every extreme that they name: `tile_span`: each text token's span is an interval of the tiles of its own block b = p // 128 and of block b - 1 (first <= second, both between b - 1 and b + 1, never below 0); it may be empty. `doc_ids`: never falling along the document; each segment holds 1 to 512 tokens. `text_query_rows`: real values. `text_key_value`: real values. `vision_qkv`: real values.
All inputs are finite; a program needn't handle non-finite values.
Results may differ from a plain program's by a relative error of at most 0.024.
Values may be sent and summed in bfloat16 or wider, within the bound.
No kernel may reach another device: no remote copies, remote signals or barrier semaphores. Data moves between devices by JAX's collectives and lax.ppermute only.
A program may use at most 64 MiB of HBM per device.

v0:
```python
import math

import jax
import jax.numpy as jnp
from jax import lax
from jax.sharding import PartitionSpec as P

HEAD_SIZE = 128
VHD = 80
WINDOW_BLOCKS = 2


def passed_along(block, axis, distance):
    devices = range(lax.axis_size(axis))
    route = [(i - distance, i) for i in devices if i - distance in devices]
    return lax.ppermute(block, axis, route)


def attend_heads(query_rows, keys, allowed_mask):
    scores = jnp.einsum(
        "tgrd,kgd->grtk", query_rows, keys, preferred_element_type=jnp.float32
    ) / math.sqrt(HEAD_SIZE)
    scores = jnp.where(allowed_mask[None, None], scores, -1e30)
    return jax.nn.softmax(scores, axis=-1)


def per_device(
    text_query_rows,
    text_key_value,
    doc_ids,
    tile_span,
    vision_hidden,
    vision_qkv,
    vision_out_weight,
    cross_keyvalue_weight,
    cross_gate,
):
    text_rows = text_query_rows.shape[0]
    tile_rows = vision_hidden.shape[0]
    kv_cols = text_key_value.shape[2]
    kv_heads = kv_cols // HEAD_SIZE
    query_group_ratio = text_query_rows.shape[1] // HEAD_SIZE // kv_heads
    seq_index = lax.axis_index("seq")
    vision_query = vision_qkv[0].reshape(tile_rows, -1, VHD)
    vision_key = vision_qkv[1].reshape(tile_rows, -1, VHD)
    vision_value = vision_qkv[2].reshape(tile_rows, -1, VHD)
    vision_scores = jnp.einsum(
        "qhd,khd->hqk", vision_query, vision_key, preferred_element_type=jnp.float32
    ) / math.sqrt(VHD)
    vision_weights = jax.nn.softmax(vision_scores, axis=-1).astype(jnp.bfloat16)
    vision_attn = jnp.einsum(
        "hqk,khd->qhd", vision_weights, vision_value, preferred_element_type=jnp.float32
    )
    vision_attn = vision_attn.astype(jnp.bfloat16).reshape(tile_rows, -1)
    partial_mix = jnp.dot(vision_attn, vision_out_weight, preferred_element_type=jnp.float32)
    mixed_sum = lax.psum(partial_mix, "head") + vision_hidden.astype(jnp.float32)
    image_norm = (
        mixed_sum * lax.rsqrt(jnp.mean(mixed_sum * mixed_sum, axis=-1, keepdims=True) + 1e-05)
    ).astype(jnp.bfloat16)
    image_key_value = jnp.einsum(
        "ic,cjf->ijf",
        image_norm,
        lax.all_gather(cross_keyvalue_weight, "seq", axis=0, tiled=True),
        preferred_element_type=jnp.float32,
    ).astype(jnp.bfloat16)
    earlier_tile = passed_along(image_key_value, "seq", 1)
    blocks = [(text_key_value, doc_ids)]
    current_kv, current_docs = (text_key_value, doc_ids)
    for repeat_count in range(WINDOW_BLOCKS):
        current_kv, current_docs = passed_along((current_kv, current_docs), "seq", 1)
        blocks.insert(0, (current_kv, current_docs))
    all_keyval = jnp.concatenate([member[0] for member in blocks], axis=1)
    all_docs = jnp.concatenate([member[1] for member in blocks], axis=0)
    key_pos = (seq_index - WINDOW_BLOCKS) * text_rows + jnp.arange(
        (WINDOW_BLOCKS + 1) * text_rows, dtype=jnp.int32
    )
    query_pos = seq_index * text_rows + jnp.arange(text_rows, dtype=jnp.int32)
    allowed_mask = (
        (all_docs[None, :] == doc_ids[:, None])
        & (key_pos[None, :] <= query_pos[:, None])
        & (key_pos[None, :] >= 0)
    )
    query_rows = text_query_rows.reshape(text_rows, kv_heads, query_group_ratio, HEAD_SIZE)
    self_attention_weights = attend_heads(
        query_rows, all_keyval[0].reshape(-1, kv_heads, HEAD_SIZE), allowed_mask
    ).astype(jnp.bfloat16)
    self_output = jnp.einsum(
        "ycmq,qyb->mycb",
        self_attention_weights,
        all_keyval[1].reshape(-1, kv_heads, HEAD_SIZE),
        preferred_element_type=jnp.float32,
    )
    self_output = self_output.reshape(text_rows, -1)
    image_all = jnp.concatenate([earlier_tile, image_key_value], axis=0)
    tile_ids = seq_index - 1 + jnp.arange(2 * tile_rows, dtype=jnp.int32) // tile_rows
    low_tile = tile_span[:, 0]
    high_tile = tile_span[:, 1]
    visible_mask = (tile_ids[None, :] >= low_tile[:, None]) & (
        tile_ids[None, :] < high_tile[:, None]
    )
    image_present = (high_tile > low_tile).astype(jnp.float32)
    cross_probabilities = (
        attend_heads(query_rows, image_all[:, 0].reshape(-1, kv_heads, HEAD_SIZE), visible_mask)
        * image_present[None, None, :, None]
    )
    cross_probabilities = cross_probabilities.astype(jnp.bfloat16)
    cross_output = jnp.einsum(
        "ycmq,qyb->mycb",
        cross_probabilities,
        image_all[:, 1].reshape(-1, kv_heads, HEAD_SIZE),
        preferred_element_type=jnp.float32,
    )
    cross_output = cross_output.reshape(text_rows, -1)
    gate_cols = jnp.repeat(jnp.tanh(cross_gate), HEAD_SIZE)
    return (self_output + gate_cols[None, :] * cross_output).astype(jnp.bfloat16)


def solution(mesh):
    placed = (
        P(("groups", "seq"), "head"),
        P(None, ("groups", "seq"), "head"),
        P(("groups", "seq")),
        P(("groups", "seq"), None),
        P(("groups", "seq"), None),
        P(None, ("groups", "seq"), "head"),
        P("head", None),
        P("seq", None, "head"),
        P("head"),
    )
    return jax.shard_map(
        per_device,
        mesh=mesh,
        in_specs=placed,
        out_specs=P(("groups", "seq"), "head"),
        check_vma=False,
    )
```

profile of v0, /device:TPU:0, one launch (start us, length us, event | category | flops | bytes accessed | tf_op | source)
XLA Modules:
  0.0 129.1 jit_solution(16018390959418832903)
XLA Ops:
  7.4 0.0 copy-start
  7.4 0.0 all-reduce.2.cloned.1.call-start
  7.4 1.4 %fusion.35 = (bf16[1,256,640]{2,1,0:T(8,128)(2,1)S(1)}, bf16[1,256,640]{2,1,0:T(8,128)(2,1)S(1)}, bf16[1,256,640]{2,1,0:T(8,128)(2,1)S(1)}) fusion(bf16[3,256,640]{2,1,0:T(8,128)(2,1)} %param.14), kind=kLoop, calls=%fused_computation.67 | loop fusion | bytes 1966080 | tf_op jit(solution)/shard_map/slice | solution.py:45
  8.8 0.2 copy.30
  8.9 0.2 copy.29
  9.1 0.2 copy.31
  9.3 2.2 %fusion.38 = (f32[8,256]{1,0:T(8,128)S(1)}, f32[8,256,256]{1,2,0:T(8,128)}) fusion(bf16[256,8,80]{0,2,1:T(8,128)(2,1)S(1)} %bitcast.88, bf16[256,8,80]{0,2,1:T(8,128)(2,1)S(1)} %bitcast.87), kind=kOutput, calls=%fused_computation.70 | convolution fusion | flops 85459200 | bytes 2760704 | tf_op jit(solution)/shard_map/sub | solution.py:50
  11.5 1.9 %convolution_convert_fusion.1 = bf16[8,256,80]{1,2,0:T(8,128)(2,1)S(1)} fusion(bf16[256,8,80]{0,2,1:T(8,128)(2,1)S(1)} %bitcast.89, f32[8,256,256]{1,2,0:T(8,128)} %get-tuple-element.17, f32[8,256]{1,0:T(8,128)S(1)} %get-tuple-element.16), kind=kOutput, calls=%fused_computation.28 | convolution fusion | flops 85098496 | bytes 2760704 | tf_op jit(solution)/shard_map/hqk,khd->qhd/dot_general | solution.py:51
  13.4 0.0 copy-start.3
  13.4 0.0 copy-done
  13.4 0.0 copy-start.5
  13.4 0.0 copy-start.4
  13.4 0.0 copy-start.7
  13.4 0.0 copy-start.6
  13.4 1.8 %fusion.40 = f32[256,1280]{1,0:T(8,128)} fusion(bf16[256,640]{0,1:T(8,128)(2,1)S(1)} %bitcast.86, bf16[640,1280]{1,0:T(8,128)(2,1)S(1)} %copy-done), kind=kOutput, calls=%fused_computation.72 | convolution fusion | flops 419430400 | bytes 3276800 | tf_op jit(solution)/shard_map/dot_general | solution.py:55
  15.2 0.0 all-reduce.2.cloned.1.call-update
  15.2 0.0 all-gather.2.cloned.1.call-start
  15.3 0.0 copy-done.3
  15.3 0.8 copy.33
  16.1 0.0 all-gather.2.cloned.1.call-update
  16.1 0.0 copy-done.5
  16.1 4.8 %collective-permute-start.2 = (s32[128]{0:T(128)S(1)}, s32[128]{0:T(128)S(1)}, u32[]{:S(2)}, u32[]{:S(2)}) collective-permute-start(s32[128]{0:T(128)S(1)} %copy-done.5), channel_id=1, source_target_pairs={{0,2},{2,4},{4,6},{6,8},{8,10},{10,12},{12,14},{1,3},{3,5},{5,7},{... | collective-permute-start | bytes 1544 | tf_op jit(solution)/shard_map/ppermute | solution.py:16
  20.9 0.0 copy-done.4
  21.0 0.2 copy.24
  21.1 3.5 %collective-permute-start = (bf16[2,128,512]{1,2,0:T(8,128)(2,1)S(1)}, bf16[2,128,512]{1,2,0:T(8,128)(2,1)S(1)}, u32[]{:S(2)}, u32[]{:S(2)}) collective-permute-start(bf16[2,128,512]{1,2,0:T(8,128)(2,1)S(1)} %copy.24), channel_id=1, source_target_pairs={{0,2},{2,4},{4,6},{6,8},{8,10},{10,12},{12,14},{1,3},{3,5},{5,7},{... | collective-permute-start | bytes 786440 | tf_op jit(solution)/shard_map/ppermute | solution.py:16
  24.6 0.0 copy-done.7
  24.6 0.0 copy-done.6
  24.7 0.1 broadcast_bitcast_fusion
  24.8 0.1 compare_and_fusion
  24.9 0.0 collective-permute-done.2
  24.9 3.4 %collective-permute-start.3 = (s32[128]{0:T(128)S(1)}, s32[128]{0:T(128)S(1)}, u32[]{:S(2)}, u32[]{:S(2)}) collective-permute-start(s32[128]{0:T(128)S(1)} %collective-permute-done.2), channel_id=1, source_target_pairs={{0,2},{2,4},{4,6},{6,8},{8,10},{10,12},{12,14},{1,3},{3,5},{5,7},{... | collective-permute-start | bytes 1544 | tf_op jit(solution)/shard_map/ppermute | solution.py:16
  28.3 1.5 %copy.52 = bf16[16,8,32,128]{3,2,1,0:T(8,128)(2,1)S(1)} copy(bf16[16,8,32,128]{3,1,2,0:T(8,128)(2,1)} %bitcast.83) | data formatting | bytes 2097152
  29.8 1.5 %collective-permute-done = bf16[2,128,512]{1,2,0:T(8,128)(2,1)S(1)} collective-permute-done((bf16[2,128,512]{1,2,0:T(8,128)(2,1)S(1)}, bf16[2,128,512]{1,2,0:T(8,128)(2,1)S(1)}, u32[]{:S(2)}, u32[]{:S(2)}) %collective-permute-start) | collective-permute-done | bytes 262176 | tf_op jit(solution)/shard_map/ppermute | solution.py:16
  31.4 4.4 %collective-permute-start.1 = (bf16[2,128,512]{1,2,0:T(8,128)(2,1)S(1)}, bf16[2,128,512]{1,2,0:T(8,128)(2,1)S(1)}, u32[]{:S(2)}, u32[]{:S(2)}) collective-permute-start(bf16[2,128,512]{1,2,0:T(8,128)(2,1)S(1)} %collective-permute-done), channel_id=1, source_target_pairs={{0,2},{2,4},{4,6},{6,8},{8,10},{10,12},{12,14},{1,3},{3,5},{5,7},{... | collective-permute-start | bytes 786440 | tf_op jit(solution)/shard_map/ppermute | solution.py:16
  35.8 0.0 collective-permute-done.3
  35.8 0.2 and_and_fusion
  36.0 3.6 %collective-permute-done.1 = bf16[2,128,512]{1,2,0:T(8,128)(2,1)S(1)} collective-permute-done((bf16[2,128,512]{1,2,0:T(8,128)(2,1)S(1)}, bf16[2,128,512]{1,2,0:T(8,128)(2,1)S(1)}, u32[]{:S(2)}, u32[]{:S(2)}) %collective-permute-start.1) | collective-permute-done | bytes 262176 | tf_op jit(solution)/shard_map/ppermute | solution.py:16
  39.6 0.1 pad_maximum_fusion
  39.7 0.8 fusion.36
  40.6 1.0 fusion.17
  41.6 0.0 copy-start.1
  41.6 3.6 %fusion.37 = (f32[4,8,128]{2,1,0:T(8,128)S(1)}, f32[4,8,128,384]{2,3,1,0:T(8,128)}) fusion(f32[4,384,128,8]{2,1,3,0:T(8,128)S(1)} %fusion.17, pred[128,384]{0,1:T(8,128)(4,1)S(1)} %and_and_fusion), kind=kOutput, calls=%fused_computation.69 | output fusion | flops 9437567 | bytes 12648448 | tf_op jit(solution)/shard_map/sub | solution.py:24
  45.2 0.0 all-reduce.2.cloned.1.call-done
  45.2 0.0 copy-done.1
  45.2 1.6 %multiply_reduce_fusion.1 = f32[256]{0:T(256)S(1)} fusion(f32[256,1280]{1,0:T(8,128)} %all-reduce.2.cloned.1.call-done, bf16[256,1280]{1,0:T(8,128)(2,1)S(1)} %copy-done.1), kind=kLoop, calls=%fused_computation.25 | loop fusion | flops 1310464 | bytes 1967104 | tf_op jit(solution)/shard_map/reduce_sum | solution.py:58
  46.8 31.8 %all-gather.2.cloned.1.call-done = bf16[1280,2,512]{2,0,1:T(8,128)(2,1)} async-done(((bf16[160,2,512]{2,0,1:T(8,128)(2,1)}), bf16[1280,2,512]{2,0,1:T(8,128)(2,1)}) %all-gather.2.cloned.1.call-update) | async-done | bytes 2621456 | tf_op jit(solution)/shard_map/all_gather | solution.py:63
  78.6 0.0 copy-start.2
  78.6 3.9 %convolution_convert_fusion = bf16[256,2,512]{2,0,1:T(8,128)(2,1)} fusion(bf16[1280,2,512]{2,0,1:T(8,128)(2,1)} %all-gather.2.cloned.1.call-done, f32[256,1280]{1,0:T(8,128)} %all-reduce.2.cloned.1.call-done, bf16[256,1280]{1,0:T(8,128)(2,1)S(1)} %copy-done.1, f32[256]{0:T(256)S(1)} %add_rsqrt_fusion), kind=kOutput, calls=%fused_computation.27 | convolution fusion | flops 672661504 | bytes 5112832 | tf_op jit(solution)/shard_map/ic,cjf->ijf/dot_general | solution.py:60
  82.5 2.7 %collective-permute-start.4 = (bf16[256,2,512]{2,0,1:T(8,128)(2,1)}, bf16[256,2,512]{2,0,1:T(8,128)(2,1)S(1)}, u32[]{:S(2)}, u32[]{:S(2)}) collective-permute-start(bf16[256,2,512]{2,0,1:T(8,128)(2,1)} %convolution_convert_fusion), channel_id=1, source_target_pairs={{0,2},{2,4},{4,6},{6,8},{8,10},{10,12},{12,14},{1,3},{3,5},{5,7},{... | collective-permute-start | bytes 1572872 | tf_op jit(solution)/shard_map/ppermute | solution.py:16
  85.2 0.0 copy-done.2
  85.2 4.9 %fusion.11 = f32[4,128,8,128]{3,1,2,0:T(8,128)} fusion(bf16[384,4,128,1]{0,2,3,1:T(8,128)(2,1)S(1)} %bitcast.85, f32[4,8,128,384]{2,3,1,0:T(8,128)} %get-tuple-element.15, f32[4,8,128]{2,1,0:T(8,128)S(1)} %get-tuple-element.14), kind=kOutput, calls=%fused_computation.17 | convolution fusion | flops 405798912 | bytes 8798208 | tf_op jit(solution)/shard_map/ycmq,qyb->mycb/dot_general | solution.py:87
  90.1 2.9 %copy.39 = f32[128,4096]{1,0:T(8,128)} copy(f32[128,4096]{0,1:T(8,128)} %bitcast.81) | data formatting | bytes 4194304 | tf_op jit(solution)/shard_map/reshape | solution.py:93
  93.0 2.0 %collective-permute-done.4 = bf16[256,2,512]{2,0,1:T(8,128)(2,1)S(1)} collective-permute-done((bf16[256,2,512]{2,0,1:T(8,128)(2,1)}, bf16[256,2,512]{2,0,1:T(8,128)(2,1)S(1)}, u32[]{:S(2)}, u32[]{:S(2)}) %collective-permute-start.4) | collective-permute-done | bytes 524320 | tf_op jit(solution)/shard_map/ppermute | solution.py:16
  95.0 2.1 %pad_maximum_fusion.1 = (bf16[512,1,512]{2,0,1:T(8,128)(2,1)}, bf16[512,1,512]{2,0,1:T(8,128)(2,1)}) fusion(bf16[256,2,512]{2,0,1:T(8,128)(2,1)} %convolution_convert_fusion, bf16[256,2,512]{2,0,1:T(8,128)(2,1)S(1)} %collective-permute-done.4), kind=kLoop, calls=%fused_computation.40 | loop fusion | flops 2097152 | bytes 2097152 | tf_op jit(solution)/shard_map/concatenate | solution.py:94
  97.1 1.2 reshape_squeeze.27
  98.3 4.5 %fusion.15 = f32[4,512,128,8]{2,1,3,0:T(8,128)} fusion(bf16[128,4,8,128]{3,2,1,0:T(8,128)(2,1)S(1)} %bitcast.78, bf16[512,4,128,1]{2,1,0,3:T(4,128)(2,1)S(1)} %bitcast.79), kind=kOutput, calls=%fused_computation.32 | convolution fusion | flops 536870912 | bytes 9961472 | tf_op jit(solution)/shard_map/tgrd,kgd->grtk/dot_general | solution.py:20
  102.8 1.3 copy.49
  104.0 8.9 %fusion.39 = (f32[4,8,128]{2,1,0:T(8,128)S(1)}, f32[4,8,128,512]{2,3,1,0:T(8,128)S(1)}) fusion(f32[4,512,128,8]{2,1,3,0:T(8,128)} %fusion.15, pred[128,512]{0,1:T(8,128)(4,1)S(1)} %compare_and_fusion), kind=kOutput, calls=%fused_computation.71 | output fusion | flops 12583423 | bytes 16859136 | tf_op jit(solution)/shard_map/sub | solution.py:24
  112.9 2.3 %fusion.8 = f32[4,128,8,128]{3,1,2,0:T(8,128)} fusion(bf16[512,4,128,1]{0,2,3,1:T(8,128)(2,1)S(1)} %bitcast.84, f32[4,8,128,512]{2,3,1,0:T(8,128)S(1)} %get-tuple-element.19, f32[128]{0:T(128)S(1)} %compare_convert_fusion, f32[4,8,128]{2,1,0:T(8,128)S(1)} %get-tuple-element.18), kind=kOutput, calls=%fused_computation.14 | convolution fusion | flops 543162368 | bytes 11026944 | tf_op jit(solution)/shard_map/ycmq,qyb->mycb/dot_general | solution.py:107
  115.2 2.9 %copy.38 = f32[128,4096]{1,0:T(8,128)} copy(f32[128,4096]{0,1:T(8,128)} %bitcast.80) | data formatting | bytes 4194304 | tf_op jit(solution)/shard_map/reshape | solution.py:113
  118.2 3.5 %add_convert_fusion = bf16[128,4096]{1,0:T(8,128)(2,1)} fusion(f32[128,4096]{1,0:T(8,128)} %copy.39, f32[128,4096]{1,0:T(8,128)} %copy.38, f32[4096]{0:T(1024)S(1)} %broadcast_bitcast_fusion), kind=kLoop, calls=%fused_computation.19 | loop fusion | flops 1572864 | bytes 5259264 | tf_op jit(solution)/shard_map/convert_element_type | solution.py:115
  (9 shorter events, 0.1 us)
Async XLA Ops:
  7.4 6.0 %copy-start = (bf16[640,1280]{1,0:T(8,128)(2,1)S(1)}, bf16[640,1280]{1,0:T(8,128)(2,1)}, u32[]{:S(2)}) copy-start(bf16[640,1280]{1,0:T(8,128)(2,1)} %param.15) | copy-start | bytes 4915204
  7.4 37.9 %all-reduce.2.cloned.1.call-start = ((), (), s32[]{:S(2)}) async-start(), calls=%async_computation | async-start | bytes 2621440 | tf_op jit(solution)/shard_map/psum | solution.py:56
  13.4 1.9 %copy-start.3 = (bf16[160,2,512]{2,1,0:T(2,128)(2,1)S(1)}, bf16[160,2,512]{2,1,0:T(2,128)(2,1)}, u32[]{:S(2)}) copy-start(bf16[160,2,512]{2,1,0:T(2,128)(2,1)} %param.16) | copy-start | bytes 983044
  13.4 2.7 %copy-start.5 = (s32[128]{0:T(128)S(1)}, s32[128]{0:T(128)}, u32[]{:S(2)}) copy-start(s32[128]{0:T(128)} %param.11) | copy-start | bytes 1540
  13.4 7.5 %copy-start.4 = (bf16[2,128,512]{2,1,0:T(8,128)(2,1)S(1)}, bf16[2,128,512]{2,1,0:T(8,128)(2,1)}, u32[]{:S(2)}) copy-start(bf16[2,128,512]{2,1,0:T(8,128)(2,1)} %param.10) | copy-start | bytes 786436
  13.4 11.2 %copy-start.7 = (f32[32]{0:T(128)S(1)}, f32[32]{0:T(128)}, u32[]{:S(2)}) copy-start(f32[32]{0:T(128)} %param.17) | copy-start | bytes 388
  13.4 11.2 %copy-start.6 = (s32[128,2]{0,1:T(2,128)S(1)}, s32[128,2]{0,1:T(2,128)}, u32[]{:S(2)}) copy-start(s32[128,2]{0,1:T(2,128)} %param.12) | copy-start | bytes 3076
  15.2 63.4 %all-gather.2.cloned.1.call-start = ((), (), s32[]{:S(2)}) async-start(), calls=%async_computation.1 | async-start | bytes 2949120 | tf_op jit(solution)/shard_map/all_gather | solution.py:63
  16.1 8.8 %collective-permute-start.2 = (s32[128]{0:T(128)S(1)}, s32[128]{0:T(128)S(1)}, u32[]{:S(2)}, u32[]{:S(2)}) collective-permute-start(s32[128]{0:T(128)S(1)} %copy-done.5), channel_id=1, source_target_pairs={{0,2},{2,4},{4,6},{6,8},{8,10},{10,12},{12,14},{1,3},{3,5},{5,7},{... | collective-permute-start | bytes 1544 | tf_op jit(solution)/shard_map/ppermute | solution.py:16
  21.1 10.2 %collective-permute-start = (bf16[2,128,512]{1,2,0:T(8,128)(2,1)S(1)}, bf16[2,128,512]{1,2,0:T(8,128)(2,1)S(1)}, u32[]{:S(2)}, u32[]{:S(2)}) collective-permute-start(bf16[2,128,512]{1,2,0:T(8,128)(2,1)S(1)} %copy.24), channel_id=1, source_target_pairs={{0,2},{2,4},{4,6},{6,8},{8,10},{10,12},{12,14},{1,3},{3,5},{5,7},{... | collective-permute-start | bytes 786440 | tf_op jit(solution)/shard_map/ppermute | solution.py:16
  24.9 10.8 %collective-permute-start.3 = (s32[128]{0:T(128)S(1)}, s32[128]{0:T(128)S(1)}, u32[]{:S(2)}, u32[]{:S(2)}) collective-permute-start(s32[128]{0:T(128)S(1)} %collective-permute-done.2), channel_id=1, source_target_pairs={{0,2},{2,4},{4,6},{6,8},{8,10},{10,12},{12,14},{1,3},{3,5},{5,7},{... | collective-permute-start | bytes 1544 | tf_op jit(solution)/shard_map/ppermute | solution.py:16
  31.4 8.3 %collective-permute-start.1 = (bf16[2,128,512]{1,2,0:T(8,128)(2,1)S(1)}, bf16[2,128,512]{1,2,0:T(8,128)(2,1)S(1)}, u32[]{:S(2)}, u32[]{:S(2)}) collective-permute-start(bf16[2,128,512]{1,2,0:T(8,128)(2,1)S(1)} %collective-permute-done), channel_id=1, source_target_pairs={{0,2},{2,4},{4,6},{6,8},{8,10},{10,12},{12,14},{1,3},{3,5},{5,7},{... | collective-permute-start | bytes 786440 | tf_op jit(solution)/shard_map/ppermute | solution.py:16
  41.6 3.6 %copy-start.1 = (bf16[256,1280]{1,0:T(8,128)(2,1)S(1)}, bf16[256,1280]{1,0:T(8,128)(2,1)}, u32[]{:S(2)}) copy-start(bf16[256,1280]{1,0:T(8,128)(2,1)} %param.13) | copy-start | bytes 1966084
  78.6 6.5 %copy-start.2 = (bf16[1,384,512]{1,2,0:T(8,128)(2,1)S(1)}, bf16[1,384,512]{1,2,0:T(8,128)(2,1)}, u32[]{:S(2)}) copy-start(bf16[1,384,512]{1,2,0:T(8,128)(2,1)} %get-tuple-element.11) | copy-start | bytes 1179652
  82.5 12.5 %collective-permute-start.4 = (bf16[256,2,512]{2,0,1:T(8,128)(2,1)}, bf16[256,2,512]{2,0,1:T(8,128)(2,1)S(1)}, u32[]{:S(2)}, u32[]{:S(2)}) collective-permute-start(bf16[256,2,512]{2,0,1:T(8,128)(2,1)} %convolution_convert_fusion), channel_id=1, source_target_pairs={{0,2},{2,4},{4,6},{6,8},{8,10},{10,12},{12,14},{1,3},{3,5},{5,7},{... | collective-permute-start | bytes 1572872 | tf_op jit(solution)/shard_map/ppermute | solution.py:16
Sparse Core Ops, SparseCore 0:
  15.4 22.6 all-reduce.1
Sparse Core Ops, SparseCore 1:
  17.9 60.7 all-gather.1
where the time goes:
time: 131 us; the launch traced here: 129 us
  waiting for transfers between devices  39 us (30%)
  matrix products  22.5 us (17%)
  other arithmetic  20.1 us (15%)
  starting transfers between devices  18.8 us (14%)
  between operations  15.1 us (12%)
  local copies, waits for them, and re-layouts  13.5 us (10%)
    all_gather x1, waiting for transfers between devices, per_device(): lax.all_gather(cross_keyvalue_weight, 'seq', axis=0, tiled=True)  31.8 us
    ppermute x5, starting transfers between devices, passed_along(): return lax.ppermute(block, axis, route)  18.7 us
    sub x2, other arithmetic, attend_heads(): return jax.nn.softmax(scores, axis=-1)  12.5 us
    ppermute x5, waiting for transfers between devices, passed_along(): return lax.ppermute(block, axis, route)  7.12 us
    dot_general x2, matrix products, attend_heads(): jnp.einsum('tgrd,kgd->grtk', query_rows, keys, preferred_element_type=jnp...  5.54 us
    dot_general x1, matrix products, per_device(): jnp.einsum('ycmq,qyb->mycb', self_attention_weights, all_keyval[1].reshap...  4.89 us
    dot_general x1, matrix products, per_device(): jnp.einsum('ic,cjf->ijf', image_norm, lax.all_gather(cross_keyvalue_weigh...  3.87 us
    convert_element_type x1, other arithmetic, per_device(): (self_output + gate_cols[None, :] * cross_output).astype(jnp.bfloat16)  3.46 us
  transfers between devices with their start and end apart: 7, of which 4 were waited for; matrix products, arithmetic and copies ran while one was open for 14% of the time, Pallas kernels for 0%

commit v1 on v0

v1 whole, which is shorter than its diff:
```python
import functools
import math

import jax
import jax.numpy as jnp
from jax import lax
from jax.experimental import pallas as pl
from jax.experimental.pallas import tpu as pltpu
from jax.sharding import PartitionSpec as P

HEAD_SIZE = 128
VHD = 80
LANES = 128
WINDOW_BLOCKS = 2
ID_ROWS = 16
NEG = -1e30
LOG2E = math.log2(math.e)
F32 = jnp.float32
BF16 = jnp.bfloat16
VMEM_LIMIT = 40 * 1024 * 1024


def dot_t(a, b):
    return lax.dot_general(a, b, (((1,), (1,)), ((), ())), preferred_element_type=F32)


def dot_n(a, b):
    return lax.dot_general(a, b, (((1,), (0,)), ((), ())), preferred_element_type=F32)


def column_of(row):
    n = row.shape[1]
    at = lax.broadcasted_iota(jnp.int32, (n, n), 0) == lax.broadcasted_iota(jnp.int32, (n, n), 1)
    return jnp.sum(jnp.where(at, row, 0.0), axis=1, keepdims=True)


def call(kernel, out_shape, args, smem=0, scratch=(), flops=0, transcendentals=0):
    outs = out_shape if isinstance(out_shape, (tuple, list)) else (out_shape,)
    moved = sum(a.size * a.dtype.itemsize for a in args) + sum(
        math.prod(o.shape) * jnp.dtype(o.dtype).itemsize for o in outs
    )
    single = not isinstance(out_shape, (tuple, list))
    vmem = pl.BlockSpec(memory_space=pltpu.VMEM)
    return pl.pallas_call(
        kernel,
        out_shape=out_shape,
        in_specs=[pl.BlockSpec(memory_space=pltpu.SMEM)] * smem + [vmem] * (len(args) - smem),
        out_specs=vmem if single else [vmem] * len(outs),
        scratch_shapes=list(scratch),
        compiler_params=pltpu.CompilerParams(vmem_limit_bytes=VMEM_LIMIT),
        cost_estimate=pl.CostEstimate(
            flops=flops, bytes_accessed=moved, transcendentals=transcendentals
        ),
    )(*args)


def vision_kernel(qkv, out):
    rows, cols = out.shape
    tiles = cols // LANES
    acc = [None] * tiles
    scale = LOG2E / math.sqrt(VHD)
    for head in range(cols // VHD):
        first, last = head * VHD, (head + 1) * VHD
        t0, t1 = first // LANES, -(-last // LANES)
        lanes = slice(t0 * LANES, t1 * LANES)
        lane = lax.broadcasted_iota(jnp.int32, (rows, (t1 - t0) * LANES), 1) + t0 * LANES
        mine = (lane >= first) & (lane < last)
        q = jnp.where(mine, qkv[0, :, lanes], jnp.zeros((), BF16))
        v = jnp.where(mine, qkv[2, :, lanes], jnp.zeros((), BF16))
        s = dot_t(q, qkv[1, :, lanes])
        p = jnp.exp2((s - jnp.max(s, axis=1, keepdims=True)) * scale)
        total = jnp.sum(p, axis=1, keepdims=True)
        o = dot_n(p.astype(BF16), v) * (1.0 / total)
        for t in range(t0, t1):
            part = o[:, (t - t0) * LANES : (t - t0 + 1) * LANES]
            acc[t] = part if acc[t] is None else acc[t] + part
    for t in range(tiles):
        out[:, t * LANES : (t + 1) * LANES] = acc[t].astype(BF16)


def norm_kernel(core, hidden, attn_own, attn_other, w_own, w_other, out, half):
    mixed = (
        hidden[...].astype(F32)
        + dot_n(attn_own[...], w_own[...])
        + dot_n(attn_other[...], w_other[...])
    )
    mean = jnp.mean(mixed * mixed, axis=1, keepdims=True)
    out[...] = (mixed * lax.rsqrt(mean + 1e-05)).astype(BF16)
    n = half.shape[0]
    half[...] = out[pl.ds(pl.multiple_of(core[0] * n, n), n), :]


def stacked_queries(q, group, ratio):
    first = group * ratio * HEAD_SIZE
    return jnp.concatenate(
        [q[:, first + i * HEAD_SIZE : first + (i + 1) * HEAD_SIZE] for i in range(ratio)], axis=0
    )


def self_kernel(seq, q, own, back1, back2, out):
    rows = q.shape[0]
    groups = own.shape[1] // HEAD_SIZE
    ratio = q.shape[1] // HEAD_SIZE // groups
    scale = LOG2E / math.sqrt(HEAD_SIZE)
    blocks = (back2, back1, own)
    ids = [b[2 * rows : 2 * rows + ID_ROWS, 0:rows][0:1].astype(F32) for b in blocks]
    own_ids = column_of(ids[2])
    t = lax.broadcasted_iota(jnp.int32, (rows, rows), 0)
    k = lax.broadcasted_iota(jnp.int32, (rows, rows), 1)
    ok = [
        (ids[0] == own_ids) & (seq[0] >= 2),
        (ids[1] == own_ids) & (seq[0] >= 1),
        (ids[2] == own_ids) & (k <= t),
    ]
    bias = jnp.concatenate([jnp.where(m, 0.0, NEG) for m in ok], axis=1)
    bias = jnp.concatenate([bias] * ratio, axis=0)
    ones = jnp.ones((len(blocks) * rows, HEAD_SIZE), BF16)
    for g in range(groups):
        cols = slice(g * HEAD_SIZE, (g + 1) * HEAD_SIZE)
        keys = jnp.concatenate([b[0:rows, cols] for b in blocks], axis=0)
        values = jnp.concatenate([b[rows : 2 * rows, cols] for b in blocks], axis=0)
        s = dot_t(stacked_queries(q, g, ratio), keys) + bias
        p = jnp.exp2((s - jnp.max(s, axis=1, keepdims=True)) * scale).astype(BF16)
        o = dot_n(p, jnp.concatenate([values, ones], axis=1))
        o = o[:, :HEAD_SIZE] * (1.0 / o[:, HEAD_SIZE:])
        for i in range(ratio):
            j = g * ratio + i
            out[:, j * HEAD_SIZE : (j + 1) * HEAD_SIZE] = o[i * rows : (i + 1) * rows]


def cross_kernel(pieces, place, q, self_out, span, gate, norm_own, before_a, before_b, *refs):
    weights, out, w, kv = refs[:pieces], refs[pieces], refs[pieces + 1], refs[pieces + 2]
    rows = q.shape[0]
    tile = norm_own.shape[0]
    part = before_a.shape[0]
    kv_cols = w.shape[1] // 2
    groups = kv_cols // HEAD_SIZE
    ratio = q.shape[1] // HEAD_SIZE // groups
    scale = LOG2E / math.sqrt(HEAD_SIZE)
    for i, piece in enumerate(weights):
        n = piece.shape[0]
        start = place[2 + i]
        w[pl.ds(pl.multiple_of(start, ID_ROWS), n), :] = piece[...]
    before = jnp.concatenate([before_a[...], before_b[...]], axis=0)
    kv[0:tile, :] = dot_n(before, w[...]).astype(BF16)
    kv[tile : 2 * tile, :] = dot_n(norm_own[...], w[...]).astype(BF16)
    seq = place[0]
    low = column_of(span[0:1, :].astype(F32))
    high = column_of(span[1:2, :].astype(F32))
    this = seq.astype(F32)
    see_own = (low <= this) & (this < high)
    see_before = (low <= this - 1.0) & (this - 1.0 < high)
    see_own = jnp.concatenate([see_own.astype(F32)] * ratio, axis=0) > 0.5
    see_before = jnp.concatenate([see_before.astype(F32)] * ratio, axis=0) > 0.5
    ones = jnp.ones((tile, HEAD_SIZE), BF16)
    for g in range(groups):
        cols = slice(g * HEAD_SIZE, (g + 1) * HEAD_SIZE)
        vcols = slice(kv_cols + g * HEAD_SIZE, kv_cols + (g + 1) * HEAD_SIZE)
        queries = stacked_queries(q, g, ratio)
        s_before = dot_t(queries, kv[0:tile, cols])
        s_own = dot_t(queries, kv[tile : 2 * tile, cols])
        m = jnp.maximum(
            jnp.where(see_before, jnp.max(s_before, axis=1, keepdims=True), NEG),
            jnp.where(see_own, jnp.max(s_own, axis=1, keepdims=True), NEG),
        )
        p_before = jnp.exp2((s_before - jnp.where(see_before, m, -NEG)) * scale).astype(BF16)
        p_own = jnp.exp2((s_own - jnp.where(see_own, m, -NEG)) * scale).astype(BF16)
        o = dot_n(p_before, jnp.concatenate([kv[0:tile, vcols], ones], axis=1))
        o = o + dot_n(p_own, jnp.concatenate([kv[tile : 2 * tile, vcols], ones], axis=1))
        total = o[:, HEAD_SIZE:]
        o = o[:, :HEAD_SIZE] * jnp.where(total > 0.0, 1.0 / total, 0.0)
        for i in range(ratio):
            at = slice((g * ratio + i) * HEAD_SIZE, (g * ratio + i + 1) * HEAD_SIZE)
            out[:, at] = (self_out[:, at] + gate[:, at] * o[i * rows : (i + 1) * rows]).astype(BF16)


def shifted(block, axis, distance):
    n = lax.axis_size(axis)
    return lax.ppermute(block, axis, [(i, i + distance) for i in range(n - distance)])


def flipped(block, axis, bits):
    return lax.ppermute(block, axis, [(i, i ^ bits) for i in range(lax.axis_size(axis))])


def gathered_weights(w):
    n, rows = lax.axis_size("seq"), w.shape[0]
    me = lax.axis_index("seq")
    if n != 8 or lax.axis_size("groups") != 2 or rows % 32:
        return [(lax.all_gather(w, "seq", axis=0, tiled=True), 0)]
    group = lax.axis_index("groups")
    half = rows // 2
    mine, other = group * half, (1 - group) * half
    part = lax.dynamic_slice_in_dim(w, mine, half, 0)
    pieces = [(w, me * rows), (flipped(w, "seq", 1), (me ^ 1) * rows)]
    for z in (2, 4, 6):
        near = flipped(part, "seq", z)
        across = flipped(near, "seq", 1)
        pieces += [
            (near, (me ^ z) * rows + mine),
            (flipped(near, "groups", 1), (me ^ z) * rows + other),
            (across, (me ^ z ^ 1) * rows + mine),
            (flipped(across, "groups", 1), (me ^ z ^ 1) * rows + other),
        ]
    return pieces


def per_device(
    text_query_rows,
    text_key_value,
    doc_ids,
    tile_span,
    vision_hidden,
    vision_qkv,
    vision_out_weight,
    cross_keyvalue_weight,
    cross_gate,
):
    text_rows = text_query_rows.shape[0]
    tile_rows, width = vision_hidden.shape
    kv_cols = text_key_value.shape[2]
    kv_heads = kv_cols // HEAD_SIZE
    q_heads = text_query_rows.shape[1] // HEAD_SIZE
    seq = lax.axis_index("seq")
    core = lax.axis_index("head")
    other_core = functools.partial(flipped, axis="head", bits=1)
    sds = jax.ShapeDtypeStruct

    w = cross_keyvalue_weight.reshape(cross_keyvalue_weight.shape[0], -1)
    pieces = gathered_weights(w)
    out_weight_other = other_core(vision_out_weight)

    attn = call(
        vision_kernel,
        sds((tile_rows, vision_qkv.shape[2]), BF16),
        (vision_qkv,),
        flops=4 * tile_rows * tile_rows * vision_qkv.shape[2],
        transcendentals=tile_rows * tile_rows * vision_qkv.shape[2] // VHD,
    )
    attn_other = other_core(attn)
    norm, norm_half = call(
        norm_kernel,
        (sds((tile_rows, width), BF16), sds((tile_rows // 2, width), BF16)),
        (
            core.reshape(1),
            vision_hidden,
            attn,
            attn_other,
            vision_out_weight,
            out_weight_other,
        ),
        smem=1,
        flops=2 * tile_rows * width * width,
    )
    before_mine = shifted(norm_half, "seq", 1)
    before_other = other_core(before_mine)
    before_a = jnp.where(core == 0, before_mine, before_other)
    before_b = jnp.where(core == 0, before_other, before_mine)

    ids = jnp.broadcast_to(doc_ids.astype(BF16), (ID_ROWS, text_rows))
    ids = jnp.pad(ids, ((0, 0), (0, kv_cols - text_rows)))
    text = jnp.concatenate([text_key_value.reshape(-1, kv_cols), ids], axis=0)
    back1 = shifted(text, "seq", 1)
    back2 = shifted(text, "seq", 2)
    self_out = call(
        self_kernel,
        sds(text_query_rows.shape, F32),
        (seq.reshape(1), text_query_rows, text, back1, back2),
        smem=1,
        flops=4 * text_rows * q_heads * (WINDOW_BLOCKS + 1) * text_rows * HEAD_SIZE,
        transcendentals=text_rows * q_heads * (WINDOW_BLOCKS + 1) * text_rows,
    )

    gate = jnp.repeat(jnp.tanh(cross_gate), HEAD_SIZE)[None, :]
    place = jnp.stack([seq, core] + [jnp.asarray(p[1], jnp.int32) for p in pieces])
    return call(
        functools.partial(cross_kernel, len(pieces)),
        sds(text_query_rows.shape, BF16),
        (
            place,
            text_query_rows,
            self_out,
            tile_span.T,
            gate,
            norm,
            before_a,
            before_b,
            *[p[0] for p in pieces],
        ),
        smem=1,
        scratch=(
            pltpu.VMEM((width, 2 * kv_cols), BF16),
            pltpu.VMEM((2 * tile_rows, 2 * kv_cols), BF16),
        ),
        flops=4 * tile_rows * width * 2 * kv_cols
        + 4 * text_rows * q_heads * 2 * tile_rows * HEAD_SIZE,
        transcendentals=text_rows * q_heads * 2 * tile_rows,
    )


def solution(mesh):
    placed = (
        P(("groups", "seq"), "head"),
        P(None, ("groups", "seq"), "head"),
        P(("groups", "seq")),
        P(("groups", "seq"), None),
        P(("groups", "seq"), None),
        P(None, ("groups", "seq"), "head"),
        P("head", None),
        P("seq", None, "head"),
        P("head"),
    )
    return jax.shard_map(
        per_device,
        mesh=mesh,
        in_specs=placed,
        out_specs=P(("groups", "seq"), "head"),
        check_vma=False,
    )
```

time: 131 us -> 83.5 us (0.64)
  the two profiles are of different devices: /device:TPU:0 before, /device:TPU:18 now
where the time goes in v1:
time: 83.5 us; the launch traced here: 83.1 us
  waiting for transfers between devices  40.1 us (48%)
  Pallas kernels  18.7 us (22%)
  starting transfers between devices  18.5 us (22%)
  local copies, waits for them, and re-layouts  5.6 us (7%)
    ppermute x16, waiting for transfers between devices, flipped(): lax.ppermute(block, axis, [(i, i ^ bits) for i in range(lax.axis_size(axi...  40.1 us
    pallas_call x4, Pallas kernels, call(): pl.pallas_call(kernel, out_shape=out_shape, in_specs=[pl.BlockSpec(memory...  18.7 us
    ppermute x16, starting transfers between devices, flipped(): lax.ppermute(block, axis, [(i, i ^ bits) for i in range(lax.axis_size(axi...  10.6 us
    ppermute x3, starting transfers between devices, shifted(): lax.ppermute(block, axis, [(i, i + distance) for i in range(n - distance)])  7.84 us
    unnamed x25, local copies, waits for them, and re-layouts  5.39 us
  transfers between devices with their start and end apart: 19, of which 8 were waited for; matrix products, arithmetic and copies ran while one was open for 2% of the time, Pallas kernels for 5%

profile of v1, /device:TPU:18, one launch (start us, length us, event | category | flops | bytes accessed | tf_op | source)
XLA Modules:
  0.0 83.1 jit_solution(14474679879443489008)
XLA Ops:
  0.0 0.0 copy-start
  0.0 0.0 collective-permute-start.3
  0.0 0.0 copy-start.2
  0.0 1.3 %copy-done.2 = bf16[3,256,640]{2,1,0:T(8,128)(2,1)S(1)} copy-done((bf16[3,256,640]{2,1,0:T(8,128)(2,1)S(1)}, bf16[3,256,640]{2,1,0:T(8,128)(2,1)}, u32[]{:S(2)}) %copy-start.2) | copy-done | bytes 983064
  1.3 1.9 %shard_map.92.attn_own = bf16[256,640]{1,0:T(8,128)(2,1)} custom-call(bf16[3,256,640]{2,1,0:T(8,128)(2,1)S(1)} %copy-done.2), custom_call_target="tpu_custom_call" | custom-call | flops 167772160 | bytes 1310720 | tf_op jit(solution)/shard_map/pallas_call | solution.py:44
  3.2 0.4 collective-permute-start.2
  3.6 1.7 %copy.10 = bf16[20,8,2,512]{3,1,2,0:T(8,128)(2,1)} copy(bf16[20,8,2,512]{3,2,1,0:T(2,128)(2,1)} %bitcast.26) | data formatting | bytes 655360
  5.3 0.0 collective-permute-done.2.attn_other
  5.3 0.0 collective-permute-done.3.w_other
  5.3 0.0 copy-done
  5.3 0.0 copy-start.5
  5.3 1.1 %copy-done.5 = bf16[256,1280]{1,0:T(8,128)(2,1)S(1)} copy-done((bf16[256,1280]{1,0:T(8,128)(2,1)S(1)}, bf16[256,1280]{1,0:T(8,128)(2,1)}, u32[]{:S(2)}) %copy-start.5) | copy-done | bytes 655384
  6.4 0.0 copy-start.3
  6.4 0.0 copy-start.10
  6.4 2.5 %shard_map.93 = (bf16[256,1280]{1,0:T(8,128)(2,1)S(1)}, bf16[128,1280]{1,0:T(8,128)(2,1)S(1)}) custom-call(s32[1]{0:T(128)} %bitcast.1.core, bf16[256,1280]{1,0:T(8,128)(2,1)S(1)} %copy-done.5, bf16[256,640]{1,0:T(8,128)(2,1)} %shard_map.92.attn_own, bf16[256,640]{1,0:T(8,128)(2,1)} %collective-permute-done.2.attn_other, bf16[640,1280]{1,0:T(8,128)(2,1)S(1)} %copy-done, ...), custom_call_target="tpu_custom_call" | custom-call | flops 838860800 | bytes 5570564 | tf_op jit(solution)/shard_map/pallas_call | solution.py:44
  8.9 0.0 copy-start.6
  8.9 3.5 %collective-permute-start.4 = (bf16[128,1280]{1,0:T(8,128)(2,1)S(1)}, bf16[128,1280]{1,0:T(8,128)(2,1)S(1)}, u32[]{:S(2)}, u32[]{:S(2)}) collective-permute-start(bf16[128,1280]{1,0:T(8,128)(2,1)S(1)} %get-tuple-element.8), channel_id=1, source_target_pairs={{0,2},{2,4},{4,6},{6,8},{8,10},{10,12},{12,14},{1,3},{3,5},{5,7},{... | collective-permute-start | bytes 983048 | tf_op jit(solution)/shard_map/ppermute | solution.py:179
  12.4 0.0 copy-done.3
  12.4 0.1 collective-permute-start.7
  12.5 1.9 %collective-permute-start.11 = (bf16[80,1024]{1,0:T(8,128)(2,1)S(1)}, bf16[80,1024]{1,0:T(8,128)(2,1)S(1)}, u32[]{:S(2)}, u32[]{:S(2)}) collective-permute-start(bf16[80,1024]{1,0:T(8,128)(2,1)S(1)} %constant_dynamic-slice_fusion), channel_id=1, source_target_pairs={{0,8},{2,10},{4,12},{6,14},{8,0},{10,2},{12,4},{14,6},{1,9},{3,11}... | collective-permute-start | bytes 491528 | tf_op jit(solution)/shard_map/ppermute | solution.py:183
  14.4 0.0 copy-done.10
  14.4 0.0 copy-done.9
  14.5 2.3 %collective-permute-start = (bf16[272,512]{1,0:T(8,128)(2,1)S(1)}, bf16[272,512]{1,0:T(8,128)(2,1)S(1)}, u32[]{:S(2)}, u32[]{:S(2)}) collective-permute-start(bf16[272,512]{1,0:T(8,128)(2,1)S(1)} %pad_maximum_fusion.own), channel_id=1, source_target_pairs={{0,2},{2,4},{4,6},{6,8},{8,10},{10,12},{12,14},{1,3},{3,5},{5,7},{... | collective-permute-start | bytes 835592 | tf_op jit(solution)/shard_map/ppermute | solution.py:179
  16.8 2.1 %collective-permute-start.1 = (bf16[272,512]{1,0:T(8,128)(2,1)S(1)}, bf16[272,512]{1,0:T(8,128)(2,1)S(1)}, u32[]{:S(2)}, u32[]{:S(2)}) collective-permute-start(bf16[272,512]{1,0:T(8,128)(2,1)S(1)} %pad_maximum_fusion.own), channel_id=1, source_target_pairs={{0,4},{2,6},{4,8},{6,10},{8,12},{10,14},{1,5},{3,7},{5,9},{7,11},{... | collective-permute-start | bytes 835592 | tf_op jit(solution)/shard_map/ppermute | solution.py:179
  18.9 8.3 %collective-permute-done.7.refs_2_ = bf16[80,1024]{1,0:T(8,128)(2,1)S(1)} collective-permute-done((bf16[80,1024]{1,0:T(8,128)(2,1)S(1)}, bf16[80,1024]{1,0:T(8,128)(2,1)S(1)}, u32[]{:S(2)}, u32[]{:S(2)}) %collective-permute-start.7) | collective-permute-done | bytes 163872 | tf_op jit(solution)/shard_map/ppermute | solution.py:183
  27.2 0.0 collective-permute-start.15
  27.2 1.1 %collective-permute-done.11.refs_6_ = bf16[80,1024]{1,0:T(8,128)(2,1)S(1)} collective-permute-done((bf16[80,1024]{1,0:T(8,128)(2,1)S(1)}, bf16[80,1024]{1,0:T(8,128)(2,1)S(1)}, u32[]{:S(2)}, u32[]{:S(2)}) %collective-permute-start.11) | collective-permute-done | bytes 163872 | tf_op jit(solution)/shard_map/ppermute | solution.py:183
  28.3 0.0 collective-permute-start.9
  28.3 0.0 collective-permute-done.4
  28.3 0.0 collective-permute-start.5
  28.3 18.4 %collective-permute-done.15.refs_10_ = bf16[80,1024]{1,0:T(8,128)(2,1)S(1)} collective-permute-done((bf16[80,1024]{1,0:T(8,128)(2,1)S(1)}, bf16[80,1024]{1,0:T(8,128)(2,1)S(1)}, u32[]{:S(2)}, u32[]{:S(2)}) %collective-permute-start.15) | collective-permute-done | bytes 163872 | tf_op jit(solution)/shard_map/ppermute | solution.py:183
  46.7 0.0 collective-permute-start.13
  46.7 0.0 collective-permute-done.back1
  46.7 2.0 %collective-permute-start.17 = (bf16[80,1024]{1,0:T(8,128)(2,1)S(1)}, bf16[80,1024]{1,0:T(8,128)(2,1)S(1)}, u32[]{:S(2)}, u32[]{:S(2)}) collective-permute-start(bf16[80,1024]{1,0:T(8,128)(2,1)S(1)} %collective-permute-done.15.refs_10_), channel_id=1, source_target_pairs={{0,2},{2,0},{4,6},{6,4},{8,10},{10,8},{12,14},{14,12},{1,3},{3,1},... | collective-permute-start | bytes 491528 | tf_op jit(solution)/shard_map/ppermute | solution.py:183
  48.7 0.0 collective-permute-done.1.back2
  48.7 0.0 copy-done.6
  48.7 1.5 %collective-permute-start.12 = (bf16[80,1024]{1,0:T(8,128)(2,1)S(1)}, bf16[80,1024]{1,0:T(8,128)(2,1)S(1)}, u32[]{:S(2)}, u32[]{:S(2)}) collective-permute-start(bf16[80,1024]{1,0:T(8,128)(2,1)S(1)} %collective-permute-done.11.refs_6_), channel_id=1, source_target_pairs={{0,16},{16,0},{1,17},{17,1},{2,18},{18,2},{3,19},{19,3},{4,20},{20... | collective-permute-start | bytes 491528 | tf_op jit(solution)/shard_map/ppermute | solution.py:183
  50.3 0.0 collective-permute-done.9.refs_4_
  50.3 0.5 collective-permute-start.16
  50.8 0.0 copy-done.11
  50.8 0.1 stack.67.place
  50.9 0.0 copy-start.1
  50.9 1.2 %copy-done.1 = bf16[128,4096]{1,0:T(8,128)(2,1)S(1)} copy-done((bf16[128,4096]{1,0:T(8,128)(2,1)S(1)}, bf16[128,4096]{1,0:T(8,128)(2,1)}, u32[]{:S(2)}) %copy-start.1) | copy-done | bytes 1048600
  52.1 2.6 %shard_map.91.self_out = f32[128,4096]{1,0:T(8,128)S(1)} custom-call(s32[1]{0:T(128)} %bitcast.seq, bf16[128,4096]{1,0:T(8,128)(2,1)S(1)} %copy-done.1, bf16[272,512]{1,0:T(8,128)(2,1)S(1)} %pad_maximum_fusion.own, bf16[272,512]{1,0:T(8,128)(2,1)S(1)} %collective-permute-done.back1, bf16[272,512]{1,0:T(8,128)(2,1)S(1)} %collective-permute-done.1.back2), custom_call_target="tpu_custom_call" | custom-call | flops 805306368 | bytes 3981316 | tf_op jit(solution)/shard_map/pallas_call | solution.py:44
  54.7 0.0 collective-permute-done.13.refs_8_
  54.7 0.0 copy-done.4
  54.7 0.2 collective-permute-start.6
  54.9 0.9 %collective-permute-done.17.refs_12_ = bf16[80,1024]{1,0:T(8,128)(2,1)S(1)} collective-permute-done((bf16[80,1024]{1,0:T(8,128)(2,1)S(1)}, bf16[80,1024]{1,0:T(8,128)(2,1)S(1)}, u32[]{:S(2)}, u32[]{:S(2)}) %collective-permute-start.17) | collective-permute-done | bytes 163872 | tf_op jit(solution)/shard_map/ppermute | solution.py:183
  55.7 1.5 %collective-permute-start.8 = (bf16[80,1024]{1,0:T(8,128)(2,1)S(1)}, bf16[80,1024]{1,0:T(8,128)(2,1)S(1)}, u32[]{:S(2)}, u32[]{:S(2)}) collective-permute-start(bf16[80,1024]{1,0:T(8,128)(2,1)S(1)} %collective-permute-done.7.refs_2_), channel_id=1, source_target_pairs={{0,16},{16,0},{1,17},{17,1},{2,18},{18,2},{3,19},{19,3},{4,20},{20... | collective-permute-start | bytes 491528 | tf_op jit(solution)/shard_map/ppermute | solution.py:183
  57.2 0.0 collective-permute-done.12.refs_7_
  57.2 0.5 collective-permute-start.10
  57.8 0.0 collective-permute-done.16.refs_11_
  57.8 1.5 %collective-permute-start.14 = (bf16[80,1024]{1,0:T(8,128)(2,1)S(1)}, bf16[80,1024]{1,0:T(8,128)(2,1)S(1)}, u32[]{:S(2)}, u32[]{:S(2)}) collective-permute-start(bf16[80,1024]{1,0:T(8,128)(2,1)S(1)} %collective-permute-done.13.refs_8_), channel_id=1, source_target_pairs={{0,16},{16,0},{1,17},{17,1},{2,18},{18,2},{3,19},{19,3},{4,20},{20... | collective-permute-start | bytes 491528 | tf_op jit(solution)/shard_map/ppermute | solution.py:183
  59.3 0.0 collective-permute-done.5
  59.3 0.5 collective-permute-start.18
  59.8 3.0 %collective-permute-done.8.refs_3_ = bf16[80,1024]{1,0:T(8,128)(2,1)S(1)} collective-permute-done((bf16[80,1024]{1,0:T(8,128)(2,1)S(1)}, bf16[80,1024]{1,0:T(8,128)(2,1)S(1)}, u32[]{:S(2)}, u32[]{:S(2)}) %collective-permute-start.8) | collective-permute-done | bytes 163872 | tf_op jit(solution)/shard_map/ppermute | solution.py:183
  62.9 0.0 collective-permute-done.6.refs_1_
  62.9 3.5 %collective-permute-done.10.refs_5_ = bf16[80,1024]{1,0:T(8,128)(2,1)S(1)} collective-permute-done((bf16[80,1024]{1,0:T(8,128)(2,1)S(1)}, bf16[80,1024]{1,0:T(8,128)(2,1)S(1)}, u32[]{:S(2)}, u32[]{:S(2)}) %collective-permute-start.10) | collective-permute-done | bytes 163872 | tf_op jit(solution)/shard_map/ppermute | solution.py:183
  66.4 3.1 %collective-permute-done.14.refs_9_ = bf16[80,1024]{1,0:T(8,128)(2,1)S(1)} collective-permute-done((bf16[80,1024]{1,0:T(8,128)(2,1)S(1)}, bf16[80,1024]{1,0:T(8,128)(2,1)S(1)}, u32[]{:S(2)}, u32[]{:S(2)}) %collective-permute-start.14) | collective-permute-done | bytes 163872 | tf_op jit(solution)/shard_map/ppermute | solution.py:183
  69.5 1.8 %collective-permute-done.18.refs_13_ = bf16[80,1024]{1,0:T(8,128)(2,1)S(1)} collective-permute-done((bf16[80,1024]{1,0:T(8,128)(2,1)S(1)}, bf16[80,1024]{1,0:T(8,128)(2,1)S(1)}, u32[]{:S(2)}, u32[]{:S(2)}) %collective-permute-start.18) | collective-permute-done | bytes 163872 | tf_op jit(solution)/shard_map/ppermute | solution.py:183
  71.2 0.1 broadcast_in_dim.4
  71.3 0.0 copy-done.7
  71.3 0.0 copy-done.8
  71.3 11.8 %shard_map.94 = bf16[128,4096]{1,0:T(8,128)(2,1)} custom-call(s32[16]{0:T(128)S(1)} %stack.67.place, bf16[128,4096]{1,0:T(8,128)(2,1)S(1)} %copy-done.1, f32[128,4096]{1,0:T(8,128)S(1)} %shard_map.91.self_out, s32[2,128]{1,0:T(2,128)S(1)} %bitcast.25, f32[1,4096]{1,0:T(1,128)S(1)} %bitcast.24, bf16[256,1280]{1,0:T(8,128)(2,1)S(1)} %copy-done.7, ...), custom_call_target="tpu_custom_call" | custom-call | flops 2415919104 | bytes 8143936 | tf_op jit(solution)/shard_map/pallas_call | solution.py:44
  (12 shorter events, 0.1 us)
Async XLA Ops:
  0.0 5.3 %copy-start = (bf16[640,1280]{1,0:T(8,128)(2,1)S(1)}, bf16[640,1280]{1,0:T(8,128)(2,1)}, u32[]{:S(2)}) copy-start(bf16[640,1280]{1,0:T(8,128)(2,1)} %w_own.1) | copy-start | bytes 4915204
  0.0 5.3 %collective-permute-start.3 = (bf16[640,1280]{1,0:T(8,128)(2,1)}, bf16[640,1280]{1,0:T(8,128)(2,1)S(1)}, u32[]{:S(2)}, u32[]{:S(2)}) collective-permute-start(bf16[640,1280]{1,0:T(8,128)(2,1)} %w_own.1), channel_id=1, source_target_pairs={{0,1},{1,0},{2,3},{3,2},{4,5},{5,4},{6,7},{7,6},{8,9},{9,8},{10,11... | collective-permute-start | bytes 4915208 | tf_op jit(solution)/shard_map/ppermute | solution.py:183
  0.0 1.3 %copy-start.2 = (bf16[3,256,640]{2,1,0:T(8,128)(2,1)S(1)}, bf16[3,256,640]{2,1,0:T(8,128)(2,1)}, u32[]{:S(2)}) copy-start(bf16[3,256,640]{2,1,0:T(8,128)(2,1)} %qkv.1) | copy-start | bytes 2949124
  3.2 2.1 %collective-permute-start.2 = (bf16[256,640]{1,0:T(8,128)(2,1)}, bf16[256,640]{1,0:T(8,128)(2,1)}, u32[]{:S(2)}, u32[]{:S(2)}) collective-permute-start(bf16[256,640]{1,0:T(8,128)(2,1)} %shard_map.92.attn_own), channel_id=1, source_target_pairs={{0,1},{1,0},{2,3},{3,2},{4,5},{5,4},{6,7},{7,6},{8,9},{9,8},{10,11... | collective-permute-start | bytes 983048 | tf_op jit(solution)/shard_map/ppermute | solution.py:183
  5.3 1.1 %copy-start.5 = (bf16[256,1280]{1,0:T(8,128)(2,1)S(1)}, bf16[256,1280]{1,0:T(8,128)(2,1)}, u32[]{:S(2)}) copy-start(bf16[256,1280]{1,0:T(8,128)(2,1)} %hidden.1) | copy-start | bytes 1966084
  6.4 6.0 %copy-start.3 = (bf16[20,8,2,512]{3,1,2,0:T(8,128)(2,1)S(1)}, bf16[20,8,2,512]{3,1,2,0:T(8,128)(2,1)}, u32[]{:S(2)}) copy-start(bf16[20,8,2,512]{3,1,2,0:T(8,128)(2,1)} %copy.10) | copy-start | bytes 983044
  6.4 8.0 %copy-start.10 = (s32[128]{0:T(128)S(1)}, s32[128]{0:T(128)}, u32[]{:S(2)}) copy-start(s32[128]{0:T(128)} %param.11) | copy-start | bytes 1540
  6.4 8.0 %copy-start.9 = (bf16[2,128,512]{2,1,0:T(8,128)(2,1)S(1)}, bf16[2,128,512]{2,1,0:T(8,128)(2,1)}, u32[]{:S(2)}) copy-start(bf16[2,128,512]{2,1,0:T(8,128)(2,1)} %param.10) | copy-start | bytes 786436
  6.4 44.3 %copy-start.11 = (f32[32]{0:T(128)S(1)}, f32[32]{0:T(128)}, u32[]{:S(2)}) copy-start(f32[32]{0:T(128)} %param.17) | copy-start | bytes 388
  8.9 39.8 %copy-start.6 = (bf16[256,1280]{1,0:T(8,128)(2,1)}, bf16[256,1280]{1,0:T(8,128)(2,1)S(1)}, u32[]{:S(2)}) copy-start(bf16[256,1280]{1,0:T(8,128)(2,1)S(1)} %get-tuple-element.7.norm_own) | copy-start | bytes 1966084
  8.9 19.4 %collective-permute-start.4 = (bf16[128,1280]{1,0:T(8,128)(2,1)S(1)}, bf16[128,1280]{1,0:T(8,128)(2,1)S(1)}, u32[]{:S(2)}, u32[]{:S(2)}) collective-permute-start(bf16[128,1280]{1,0:T(8,128)(2,1)S(1)} %get-tuple-element.8), channel_id=1, source_target_pairs={{0,2},{2,4},{4,6},{6,8},{8,10},{10,12},{12,14},{1,3},{3,5},{5,7},{... | collective-permute-start | bytes 983048 | tf_op jit(solution)/shard_map/ppermute | solution.py:179
  12.4 14.7 %collective-permute-start.7 = (bf16[80,1024]{1,0:T(8,128)(2,1)S(1)}, bf16[80,1024]{1,0:T(8,128)(2,1)S(1)}, u32[]{:S(2)}, u32[]{:S(2)}) collective-permute-start(bf16[80,1024]{1,0:T(8,128)(2,1)S(1)} %constant_dynamic-slice_fusion), channel_id=1, source_target_pairs={{0,4},{2,6},{4,0},{6,2},{8,12},{10,14},{12,8},{14,10},{1,5},{3,7},... | collective-permute-start | bytes 491528 | tf_op jit(solution)/shard_map/ppermute | solution.py:183
  12.5 15.8 %collective-permute-start.11 = (bf16[80,1024]{1,0:T(8,128)(2,1)S(1)}, bf16[80,1024]{1,0:T(8,128)(2,1)S(1)}, u32[]{:S(2)}, u32[]{:S(2)}) collective-permute-start(bf16[80,1024]{1,0:T(8,128)(2,1)S(1)} %constant_dynamic-slice_fusion), channel_id=1, source_target_pairs={{0,8},{2,10},{4,12},{6,14},{8,0},{10,2},{12,4},{14,6},{1,9},{3,11}... | collective-permute-start | bytes 491528 | tf_op jit(solution)/shard_map/ppermute | solution.py:183
  14.5 32.2 %collective-permute-start = (bf16[272,512]{1,0:T(8,128)(2,1)S(1)}, bf16[272,512]{1,0:T(8,128)(2,1)S(1)}, u32[]{:S(2)}, u32[]{:S(2)}) collective-permute-start(bf16[272,512]{1,0:T(8,128)(2,1)S(1)} %pad_maximum_fusion.own), channel_id=1, source_target_pairs={{0,2},{2,4},{4,6},{6,8},{8,10},{10,12},{12,14},{1,3},{3,5},{5,7},{... | collective-permute-start | bytes 835592 | tf_op jit(solution)/shard_map/ppermute | solution.py:179
  16.8 32.0 %collective-permute-start.1 = (bf16[272,512]{1,0:T(8,128)(2,1)S(1)}, bf16[272,512]{1,0:T(8,128)(2,1)S(1)}, u32[]{:S(2)}, u32[]{:S(2)}) collective-permute-start(bf16[272,512]{1,0:T(8,128)(2,1)S(1)} %pad_maximum_fusion.own), channel_id=1, source_target_pairs={{0,4},{2,6},{4,8},{6,10},{8,12},{10,14},{1,5},{3,7},{5,9},{7,11},{... | collective-permute-start | bytes 835592 | tf_op jit(solution)/shard_map/ppermute | solution.py:179
  27.2 19.5 %collective-permute-start.15 = (bf16[80,1024]{1,0:T(8,128)(2,1)S(1)}, bf16[80,1024]{1,0:T(8,128)(2,1)S(1)}, u32[]{:S(2)}, u32[]{:S(2)}) collective-permute-start(bf16[80,1024]{1,0:T(8,128)(2,1)S(1)} %constant_dynamic-slice_fusion), channel_id=1, source_target_pairs={{0,12},{2,14},{4,8},{6,10},{8,4},{10,6},{12,0},{14,2},{1,13},{3,15... | collective-permute-start | bytes 491528 | tf_op jit(solution)/shard_map/ppermute | solution.py:183
  28.3 22.0 %collective-permute-start.9 = (bf16[80,1024]{1,0:T(8,128)(2,1)S(1)}, bf16[80,1024]{1,0:T(8,128)(2,1)S(1)}, u32[]{:S(2)}, u32[]{:S(2)}) collective-permute-start(bf16[80,1024]{1,0:T(8,128)(2,1)S(1)} %collective-permute-done.7.refs_2_), channel_id=1, source_target_pairs={{0,2},{2,0},{4,6},{6,4},{8,10},{10,8},{12,14},{14,12},{1,3},{3,1},... | collective-permute-start | bytes 491528 | tf_op jit(solution)/shard_map/ppermute | solution.py:183
  28.3 31.0 %collective-permute-start.5 = (bf16[128,1280]{1,0:T(8,128)(2,1)S(1)}, bf16[128,1280]{1,0:T(8,128)(2,1)S(1)}, u32[]{:S(2)}, u32[]{:S(2)}) collective-permute-start(bf16[128,1280]{1,0:T(8,128)(2,1)S(1)} %collective-permute-done.4), channel_id=1, source_target_pairs={{0,1},{1,0},{2,3},{3,2},{4,5},{5,4},{6,7},{7,6},{8,9},{9,8},{10,11... | collective-permute-start | bytes 983048 | tf_op jit(solution)/shard_map/ppermute | solution.py:183
  46.7 8.0 %collective-permute-start.13 = (bf16[80,1024]{1,0:T(8,128)(2,1)S(1)}, bf16[80,1024]{1,0:T(8,128)(2,1)S(1)}, u32[]{:S(2)}, u32[]{:S(2)}) collective-permute-start(bf16[80,1024]{1,0:T(8,128)(2,1)S(1)} %collective-permute-done.11.refs_6_), channel_id=1, source_target_pairs={{0,2},{2,0},{4,6},{6,4},{8,10},{10,8},{12,14},{14,12},{1,3},{3,1},... | collective-permute-start | bytes 491528 | tf_op jit(solution)/shard_map/ppermute | solution.py:183
  46.7 9.0 %collective-permute-start.17 = (bf16[80,1024]{1,0:T(8,128)(2,1)S(1)}, bf16[80,1024]{1,0:T(8,128)(2,1)S(1)}, u32[]{:S(2)}, u32[]{:S(2)}) collective-permute-start(bf16[80,1024]{1,0:T(8,128)(2,1)S(1)} %collective-permute-done.15.refs_10_), channel_id=1, source_target_pairs={{0,2},{2,0},{4,6},{6,4},{8,10},{10,8},{12,14},{14,12},{1,3},{3,1},... | collective-permute-start | bytes 491528 | tf_op jit(solution)/shard_map/ppermute | solution.py:183
  48.7 8.5 %collective-permute-start.12 = (bf16[80,1024]{1,0:T(8,128)(2,1)S(1)}, bf16[80,1024]{1,0:T(8,128)(2,1)S(1)}, u32[]{:S(2)}, u32[]{:S(2)}) collective-permute-start(bf16[80,1024]{1,0:T(8,128)(2,1)S(1)} %collective-permute-done.11.refs_6_), channel_id=1, source_target_pairs={{0,16},{16,0},{1,17},{17,1},{2,18},{18,2},{3,19},{19,3},{4,20},{20... | collective-permute-start | bytes 491528 | tf_op jit(solution)/shard_map/ppermute | solution.py:183
  50.3 7.5 %collective-permute-start.16 = (bf16[80,1024]{1,0:T(8,128)(2,1)S(1)}, bf16[80,1024]{1,0:T(8,128)(2,1)S(1)}, u32[]{:S(2)}, u32[]{:S(2)}) collective-permute-start(bf16[80,1024]{1,0:T(8,128)(2,1)S(1)} %collective-permute-done.15.refs_10_), channel_id=1, source_target_pairs={{0,16},{16,0},{1,17},{17,1},{2,18},{18,2},{3,19},{19,3},{4,20},{20... | collective-permute-start | bytes 491528 | tf_op jit(solution)/shard_map/ppermute | solution.py:183
  50.9 1.2 %copy-start.1 = (bf16[128,4096]{1,0:T(8,128)(2,1)S(1)}, bf16[128,4096]{1,0:T(8,128)(2,1)}, u32[]{:S(2)}) copy-start(bf16[128,4096]{1,0:T(8,128)(2,1)} %q.3) | copy-start | bytes 3145732
  52.1 2.6 %copy-start.4 = (bf16[20,8,2,512]{3,1,2,0:T(8,128)(2,1)S(1)}, bf16[20,8,2,512]{3,1,2,0:T(8,128)(2,1)}, u32[]{:S(2)}) copy-start(bf16[20,8,2,512]{3,1,2,0:T(8,128)(2,1)} %copy.10) | copy-start | bytes 983044
  52.1 19.2 %copy-start.7 = (bf16[256,1280]{1,0:T(8,128)(2,1)S(1)}, bf16[256,1280]{1,0:T(8,128)(2,1)}, u32[]{:S(2)}) copy-start(bf16[256,1280]{1,0:T(8,128)(2,1)} %copy-done.6) | copy-start | bytes 1966084
  52.1 19.2 %copy-start.8 = (s32[128,2]{0,1:T(2,128)S(1)}, s32[128,2]{0,1:T(2,128)}, u32[]{:S(2)}) copy-start(s32[128,2]{0,1:T(2,128)} %param.12) | copy-start | bytes 3076
  54.7 8.2 %collective-permute-start.6 = (bf16[160,1024]{1,0:T(8,128)(2,1)S(1)}, bf16[160,1024]{1,0:T(8,128)(2,1)S(1)}, u32[]{:S(2)}, u32[]{:S(2)}) collective-permute-start(bf16[160,1024]{1,0:T(8,128)(2,1)S(1)} %bitcast.22), channel_id=1, source_target_pairs={{0,2},{2,0},{4,6},{6,4},{8,10},{10,8},{12,14},{14,12},{1,3},{3,1},... | collective-permute-start | bytes 983048 | tf_op jit(solution)/shard_map/ppermute | solution.py:183
  55.7 7.1 %collective-permute-start.8 = (bf16[80,1024]{1,0:T(8,128)(2,1)S(1)}, bf16[80,1024]{1,0:T(8,128)(2,1)S(1)}, u32[]{:S(2)}, u32[]{:S(2)}) collective-permute-start(bf16[80,1024]{1,0:T(8,128)(2,1)S(1)} %collective-permute-done.7.refs_2_), channel_id=1, source_target_pairs={{0,16},{16,0},{1,17},{17,1},{2,18},{18,2},{3,19},{19,3},{4,20},{20... | collective-permute-start | bytes 491528 | tf_op jit(solution)/shard_map/ppermute | solution.py:183
  57.2 9.1 %collective-permute-start.10 = (bf16[80,1024]{1,0:T(8,128)(2,1)S(1)}, bf16[80,1024]{1,0:T(8,128)(2,1)S(1)}, u32[]{:S(2)}, u32[]{:S(2)}) collective-permute-start(bf16[80,1024]{1,0:T(8,128)(2,1)S(1)} %collective-permute-done.9.refs_4_), channel_id=1, source_target_pairs={{0,16},{16,0},{1,17},{17,1},{2,18},{18,2},{3,19},{19,3},{4,20},{20... | collective-permute-start | bytes 491528 | tf_op jit(solution)/shard_map/ppermute | solution.py:183
  57.8 11.7 %collective-permute-start.14 = (bf16[80,1024]{1,0:T(8,128)(2,1)S(1)}, bf16[80,1024]{1,0:T(8,128)(2,1)S(1)}, u32[]{:S(2)}, u32[]{:S(2)}) collective-permute-start(bf16[80,1024]{1,0:T(8,128)(2,1)S(1)} %collective-permute-done.13.refs_8_), channel_id=1, source_target_pairs={{0,16},{16,0},{1,17},{17,1},{2,18},{18,2},{3,19},{19,3},{4,20},{20... | collective-permute-start | bytes 491528 | tf_op jit(solution)/shard_map/ppermute | solution.py:183
  59.3 12.0 %collective-permute-start.18 = (bf16[80,1024]{1,0:T(8,128)(2,1)S(1)}, bf16[80,1024]{1,0:T(8,128)(2,1)S(1)}, u32[]{:S(2)}, u32[]{:S(2)}) collective-permute-start(bf16[80,1024]{1,0:T(8,128)(2,1)S(1)} %collective-permute-done.17.refs_12_), channel_id=1, source_target_pairs={{0,16},{16,0},{1,17},{17,1},{2,18},{18,2},{3,19},{19,3},{4,20},{20... | collective-permute-start | bytes 491528 | tf_op jit(solution)/shard_map/ppermute | solution.py:183

commit v2 on v1

--- a/solution.py
+++ b/solution.py
@@ -17,6 +17,7 @@
 LOG2E = math.log2(math.e)
 F32 = jnp.float32
 BF16 = jnp.bfloat16
+PLANNED_FLOPS = 20_000_000_000
 VMEM_LIMIT = 40 * 1024 * 1024
 
 
@@ -34,23 +35,19 @@
     return jnp.sum(jnp.where(at, row, 0.0), axis=1, keepdims=True)
 
 
-def call(kernel, out_shape, args, smem=0, scratch=(), flops=0, transcendentals=0):
-    outs = out_shape if isinstance(out_shape, (tuple, list)) else (out_shape,)
-    moved = sum(a.size * a.dtype.itemsize for a in args) + sum(
-        math.prod(o.shape) * jnp.dtype(o.dtype).itemsize for o in outs
-    )
-    single = not isinstance(out_shape, (tuple, list))
+def call(kernel, out_shape, args, smem=0, scratch=()):
+    many = isinstance(out_shape, (tuple, list))
     vmem = pl.BlockSpec(memory_space=pltpu.VMEM)
+    outs = out_shape if many else (out_shape,)
+    moved = sum(math.prod(a.shape) * jnp.dtype(a.dtype).itemsize for a in (*args, *outs))
     return pl.pallas_call(
         kernel,
         out_shape=out_shape,
         in_specs=[pl.BlockSpec(memory_space=pltpu.SMEM)] * smem + [vmem] * (len(args) - smem),
-        out_specs=vmem if single else [vmem] * len(outs),
+        out_specs=[vmem] * len(out_shape) if many else vmem,
         scratch_shapes=list(scratch),
         compiler_params=pltpu.CompilerParams(vmem_limit_bytes=VMEM_LIMIT),
-        cost_estimate=pl.CostEstimate(
-            flops=flops, bytes_accessed=moved, transcendentals=transcendentals
-        ),
+        cost_estimate=pl.CostEstimate(flops=PLANNED_FLOPS, bytes_accessed=moved, transcendentals=0),
     )(*args)
 
 
@@ -76,6 +73,12 @@
             acc[t] = part if acc[t] is None else acc[t] + part
     for t in range(tiles):
         out[:, t * LANES : (t + 1) * LANES] = acc[t].astype(BF16)
+
+
+def rows_kernel(w, out):
+    cols = w.shape[2]
+    out[:, 0:cols] = w[:, 0, :]
+    out[:, cols : 2 * cols] = w[:, 1, :]
 
 
 def norm_kernel(core, hidden, attn_own, attn_other, w_own, w_other, out, half):
@@ -132,7 +135,6 @@
     weights, out, w, kv = refs[:pieces], refs[pieces], refs[pieces + 1], refs[pieces + 2]
     rows = q.shape[0]
     tile = norm_own.shape[0]
-    part = before_a.shape[0]
     kv_cols = w.shape[1] // 2
     groups = kv_cols // HEAD_SIZE
     ratio = q.shape[1] // HEAD_SIZE // groups
@@ -141,37 +143,42 @@
         n = piece.shape[0]
         start = place[2 + i]
         w[pl.ds(pl.multiple_of(start, ID_ROWS), n), :] = piece[...]
-    before = jnp.concatenate([before_a[...], before_b[...]], axis=0)
-    kv[0:tile, :] = dot_n(before, w[...]).astype(BF16)
-    kv[tile : 2 * tile, :] = dot_n(norm_own[...], w[...]).astype(BF16)
-    seq = place[0]
+    norms = jnp.concatenate([before_a[...], before_b[...], norm_own[...]], axis=0)
+    kv[...] = dot_n(norms, w[...]).astype(BF16)
+    this = place[0].astype(F32)
     low = column_of(span[0:1, :].astype(F32))
     high = column_of(span[1:2, :].astype(F32))
-    this = seq.astype(F32)
     see_own = (low <= this) & (this < high)
     see_before = (low <= this - 1.0) & (this - 1.0 < high)
-    see_own = jnp.concatenate([see_own.astype(F32)] * ratio, axis=0) > 0.5
-    see_before = jnp.concatenate([see_before.astype(F32)] * ratio, axis=0) > 0.5
-    ones = jnp.ones((tile, HEAD_SIZE), BF16)
+    present = jnp.broadcast_to(jnp.where(low < high, 1.0, 0.0), (rows, HEAD_SIZE))
+    bias = jnp.concatenate(
+        [
+            jnp.broadcast_to(jnp.where(see, 0.0, NEG), (rows, tile))
+            for see in (see_before, see_own)
+        ],
+        axis=1,
+    )
+    ones = jnp.ones((2 * tile, HEAD_SIZE), BF16)
     for g in range(groups):
-        cols = slice(g * HEAD_SIZE, (g + 1) * HEAD_SIZE)
-        vcols = slice(kv_cols + g * HEAD_SIZE, kv_cols + (g + 1) * HEAD_SIZE)
-        queries = stacked_queries(q, g, ratio)
-        s_before = dot_t(queries, kv[0:tile, cols])
-        s_own = dot_t(queries, kv[tile : 2 * tile, cols])
-        m = jnp.maximum(
-            jnp.where(see_before, jnp.max(s_before, axis=1, keepdims=True), NEG),
-            jnp.where(see_own, jnp.max(s_own, axis=1, keepdims=True), NEG),
-        )
-        p_before = jnp.exp2((s_before - jnp.where(see_before, m, -NEG)) * scale).astype(BF16)
-        p_own = jnp.exp2((s_own - jnp.where(see_own, m, -NEG)) * scale).astype(BF16)
-        o = dot_n(p_before, jnp.concatenate([kv[0:tile, vcols], ones], axis=1))
-        o = o + dot_n(p_own, jnp.concatenate([kv[tile : 2 * tile, vcols], ones], axis=1))
-        total = o[:, HEAD_SIZE:]
-        o = o[:, :HEAD_SIZE] * jnp.where(total > 0.0, 1.0 / total, 0.0)
+        keys = kv[:, g * HEAD_SIZE : (g + 1) * HEAD_SIZE]
+        values = kv[:, kv_cols + g * HEAD_SIZE : kv_cols + (g + 1) * HEAD_SIZE]
+        values = jnp.concatenate([values, ones], axis=1)
         for i in range(ratio):
             at = slice((g * ratio + i) * HEAD_SIZE, (g * ratio + i + 1) * HEAD_SIZE)
-            out[:, at] = (self_out[:, at] + gate[:, at] * o[i * rows : (i + 1) * rows]).astype(BF16)
+            s = dot_t(q[:, at], keys) + bias
+            p = jnp.exp2((s - jnp.max(s, axis=1, keepdims=True)) * scale).astype(BF16)
+            o = dot_n(p, values)
+            o = o[:, :HEAD_SIZE] * (1.0 / o[:, HEAD_SIZE:])
+            out[:, at] = (self_out[:, at] + gate[:, at] * present * o).astype(BF16)
+
+
+def mark_kernel(x, out):
+    out[...] = x[...]
+
+
+def marker(*done):
+    x = after(jnp.zeros((8, LANES), F32), *done)
+    return call(mark_kernel, jax.ShapeDtypeStruct(x.shape, F32), (x,))
 
 
 def shifted(block, axis, distance):
@@ -183,26 +190,8 @@
     return lax.ppermute(block, axis, [(i, i ^ bits) for i in range(lax.axis_size(axis))])
 
 
-def gathered_weights(w):
-    n, rows = lax.axis_size("seq"), w.shape[0]
-    me = lax.axis_index("seq")
-    if n != 8 or lax.axis_size("groups") != 2 or rows % 32:
-        return [(lax.all_gather(w, "seq", axis=0, tiled=True), 0)]
-    group = lax.axis_index("groups")
-    half = rows // 2
-    mine, other = group * half, (1 - group) * half
-    part = lax.dynamic_slice_in_dim(w, mine, half, 0)
-    pieces = [(w, me * rows), (flipped(w, "seq", 1), (me ^ 1) * rows)]
-    for z in (2, 4, 6):
-        near = flipped(part, "seq", z)
-        across = flipped(near, "seq", 1)
-        pieces += [
-            (near, (me ^ z) * rows + mine),
-            (flipped(near, "groups", 1), (me ^ z) * rows + other),
-            (across, (me ^ z ^ 1) * rows + mine),
-            (flipped(across, "groups", 1), (me ^ z ^ 1) * rows + other),
-        ]
-    return pieces
+def after(x, *done):
+    return lax.optimization_barrier((x, *done))[0]
 
 
 def per_device(
@@ -226,50 +215,78 @@
     other_core = functools.partial(flipped, axis="head", bits=1)
     sds = jax.ShapeDtypeStruct
 
-    w = cross_keyvalue_weight.reshape(cross_keyvalue_weight.shape[0], -1)
-    pieces = gathered_weights(w)
+    rows = cross_keyvalue_weight.shape[0]
+    n = lax.axis_size("seq")
+    half = rows // 2
+    ring = [i for i in range(0, n, 2)] + [i for i in range(n - 1, 0, -2)]
+    rings = n == 8 and rows % 32 == 0
+    even = seq % 2 == 0
+
+    def around(blocks):
+        if not rings:
+            return ()
+        up, down = blocks
+        return (
+            lax.ppermute(up, "seq", [(ring[i - 1], ring[i]) for i in range(n)]),
+            lax.ppermute(down, "seq", [(ring[i], ring[i - 1]) for i in range(n)]),
+        )
+
+    (w,) = call(
+        rows_kernel,
+        (sds((rows, 2 * kv_cols), BF16),),
+        (cross_keyvalue_weight,),
+    )
     out_weight_other = other_core(vision_out_weight)
-
+    ids = jnp.broadcast_to(doc_ids.astype(BF16), (ID_ROWS, text_rows))
+    ids = jnp.pad(ids, ((0, 0), (0, kv_cols - text_rows)))
+    text = jnp.concatenate([text_key_value.reshape(-1, kv_cols), ids], axis=0)
+    step1 = around((w, w))
     attn = call(
         vision_kernel,
         sds((tile_rows, vision_qkv.shape[2]), BF16),
-        (vision_qkv,),
-        flops=4 * tile_rows * tile_rows * vision_qkv.shape[2],
-        transcendentals=tile_rows * tile_rows * vision_qkv.shape[2] // VHD,
+        (after(vision_qkv, w),),
     )
     attn_other = other_core(attn)
+    back2 = shifted(after(text, attn), "seq", 2)
+    mark = marker(attn)
+    step2 = around([after(block, mark) for block in step1])
     norm, norm_half = call(
         norm_kernel,
         (sds((tile_rows, width), BF16), sds((tile_rows // 2, width), BF16)),
         (
             core.reshape(1),
-            vision_hidden,
+            after(vision_hidden, back2, *step1),
             attn,
             attn_other,
             vision_out_weight,
             out_weight_other,
         ),
         smem=1,
-        flops=2 * tile_rows * width * width,
-    )
+    )
+    mark = marker(norm)
+    step3 = around([after(block, mark) for block in step2])
+    back1 = flipped(after(jnp.where(even, text, back2), norm), "seq", 1)
     before_mine = shifted(norm_half, "seq", 1)
     before_other = other_core(before_mine)
     before_a = jnp.where(core == 0, before_mine, before_other)
     before_b = jnp.where(core == 0, before_other, before_mine)
-
-    ids = jnp.broadcast_to(doc_ids.astype(BF16), (ID_ROWS, text_rows))
-    ids = jnp.pad(ids, ((0, 0), (0, kv_cols - text_rows)))
-    text = jnp.concatenate([text_key_value.reshape(-1, kv_cols), ids], axis=0)
-    back1 = shifted(text, "seq", 1)
-    back2 = shifted(text, "seq", 2)
     self_out = call(
         self_kernel,
         sds(text_query_rows.shape, F32),
-        (seq.reshape(1), text_query_rows, text, back1, back2),
+        (seq.reshape(1), after(text_query_rows, before_mine), text, back1, back2),
         smem=1,
-        flops=4 * text_rows * q_heads * (WINDOW_BLOCKS + 1) * text_rows * HEAD_SIZE,
-        transcendentals=text_rows * q_heads * (WINDOW_BLOCKS + 1) * text_rows,
-    )
+    )
+    if rings:
+        up, down = [after(block, self_out) for block in step3]
+        step4 = around((up[:half], down[half:]))
+        at = lambda p: jnp.where(p % n < n // 2, 2 * (p % n), 2 * (n - 1 - p % n) + 1) * rows
+        place = jnp.where(even, seq // 2, n - 1 - seq // 2)
+        pieces = [(w, seq * rows)]
+        for k, (up, down) in ((1, step1), (2, step2), (3, step3)):
+            pieces += [(up, at(place + n - k)), (down, at(place + k))]
+        pieces += [(step4[0], at(place + n // 2)), (step4[1], at(place + n // 2) + half)]
+    else:
+        pieces = [(lax.all_gather(w, "seq", axis=0, tiled=True), 0)]
 
     gate = jnp.repeat(jnp.tanh(cross_gate), HEAD_SIZE)[None, :]
     place = jnp.stack([seq, core] + [jnp.asarray(p[1], jnp.int32) for p in pieces])
@@ -292,9 +309,6 @@
             pltpu.VMEM((width, 2 * kv_cols), BF16),
             pltpu.VMEM((2 * tile_rows, 2 * kv_cols), BF16),
         ),
-        flops=4 * tile_rows * width * 2 * kv_cols
-        + 4 * text_rows * q_heads * 2 * tile_rows * HEAD_SIZE,
-        transcendentals=text_rows * q_heads * 2 * tile_rows,
     )
 
 

time: 83.5 us -> 61.7 us (0.74)
  the two profiles are of different devices: /device:TPU:18 before, /device:TPU:0 now
where the time goes in v2:
time: 61.7 us; the launch traced here: 61.4 us
  waiting for transfers between devices  25.9 us (42%)
  starting transfers between devices  18.5 us (30%)
  Pallas kernels  14.3 us (23%)
  local copies, waits for them, and re-layouts  1.3 us (2%)
  other arithmetic  1.09 us (2%)
    ppermute x2, waiting for transfers between devices, shifted(): lax.ppermute(block, axis, [(i, i + distance) for i in range(n - distance)])  14.4 us
    pallas_call x5, Pallas kernels, call(): pl.pallas_call(kernel, out_shape=out_shape, in_specs=[pl.BlockSpec(memory...  14.3 us
    ppermute x4, starting transfers between devices, around(): lax.ppermute(down, 'seq', [(ring[i], ring[i - 1]) for i in range(n)])  9.02 us
    ppermute x2, starting transfers between devices, shifted(): lax.ppermute(block, axis, [(i, i + distance) for i in range(n - distance)])  6.6 us
    ppermute x4, waiting for transfers between devices, around(): lax.ppermute(down, 'seq', [(ring[i], ring[i - 1]) for i in range(n)])  6.32 us
    ppermute x4, waiting for transfers between devices, around(): lax.ppermute(up, 'seq', [(ring[i - 1], ring[i]) for i in range(n)])  5.22 us
    ppermute x4, starting transfers between devices, flipped(): lax.ppermute(block, axis, [(i, i ^ bits) for i in range(lax.axis_size(axi...  1.58 us
    ppermute x4, starting transfers between devices, around(): lax.ppermute(up, 'seq', [(ring[i - 1], ring[i]) for i in range(n)])  1.28 us
  transfers between devices with their start and end apart: 14, of which 7 were waited for; matrix products, arithmetic and copies ran while one was open for 2% of the time, Pallas kernels for 12%

profile of v2, /device:TPU:0, one launch (start us, length us, event | category | flops | bytes accessed | tf_op | source)
XLA Modules:
  0.0 61.4 jit_solution(8021873024234468290)
XLA Ops:
  0.0 0.0 copy-start.2
  0.0 0.0 copy-start.4
  0.0 1.1 %copy-done.4 = bf16[160,2,512]{2,1,0:T(2,128)(2,1)S(1)} copy-done((bf16[160,2,512]{2,1,0:T(2,128)(2,1)S(1)}, bf16[160,2,512]{2,1,0:T(2,128)(2,1)}, u32[]{:S(2)}) %copy-start.4) | copy-done | bytes 327704
  1.1 0.7 %shard_map.91.refs_0_ = bf16[160,1024]{1,0:T(8,128)(2,1)S(1)} custom-call(bf16[160,2,512]{2,1,0:T(2,128)(2,1)S(1)} %copy-done.4), custom_call_target="tpu_custom_call" | custom-call | flops 20000000000 | bytes 655360 | tf_op jit(solution)/shard_map/pallas_call | solution.py:43
  1.8 0.0 copy-start.7
  1.8 0.0 copy-start.6
  1.8 0.0 copy-start
  1.8 0.0 copy-start.8
  1.8 3.0 %collective-permute-start.2 = (bf16[160,1024]{1,0:T(8,128)(2,1)S(1)}, bf16[160,1024]{1,0:T(8,128)(2,1)S(1)}, u32[]{:S(2)}, u32[]{:S(2)}) collective-permute-start(bf16[160,1024]{1,0:T(8,128)(2,1)S(1)} %shard_map.91.refs_0_), channel_id=1, source_target_pairs={{0,2},{4,0},{8,4},{12,8},{14,12},{10,14},{6,10},{2,6},{1,3},{5,1},... | collective-permute-start | bytes 983048 | tf_op jit(solution)/shard_map/ppermute | solution.py:231
  4.8 0.2 collective-permute-start.1
  4.9 0.0 copy-done.2
  4.9 1.9 %shard_map.92.attn_own = bf16[256,640]{1,0:T(8,128)(2,1)} custom-call(bf16[3,256,640]{2,1,0:T(8,128)(2,1)S(1)} %copy-done.2), custom_call_target="tpu_custom_call" | custom-call | flops 20000000000 | bytes 1310720 | tf_op jit(solution)/shard_map/pallas_call | solution.py:43
  6.8 0.0 copy-start.3
  6.8 0.0 collective-permute-start.3
  6.8 0.0 copy-done.7
  6.9 0.0 copy-done.6
  6.9 4.0 %collective-permute-start = (bf16[272,512]{1,0:T(8,128)(2,1)S(1)}, bf16[272,512]{1,0:T(8,128)(2,1)S(1)}, u32[]{:S(2)}, u32[]{:S(2)}) collective-permute-start(bf16[272,512]{1,0:T(8,128)(2,1)S(1)} %pad_maximum_fusion.own), channel_id=1, source_target_pairs={{0,4},{2,6},{4,8},{6,10},{8,12},{10,14},{1,5},{3,7},{5,9},{7,11},{... | collective-permute-start | bytes 835592 | tf_op jit(solution)/shard_map/ppermute | solution.py:186
  10.9 0.0 copy-done
  10.9 0.1 collective-permute-start.4
  11.2 0.0 copy-done.8
  11.2 0.1 stack.47.place
  11.3 6.6 %collective-permute-done.back2 = bf16[272,512]{1,0:T(8,128)(2,1)S(1)} collective-permute-done((bf16[272,512]{1,0:T(8,128)(2,1)S(1)}, bf16[272,512]{1,0:T(8,128)(2,1)S(1)}, u32[]{:S(2)}, u32[]{:S(2)}) %collective-permute-start) | collective-permute-done | bytes 278560 | tf_op jit(solution)/shard_map/ppermute | solution.py:186
  17.9 1.0 %broadcast_select_fusion.2 = bf16[272,512]{1,0:T(8,128)(2,1)S(1)} fusion(bf16[272,512]{1,0:T(8,128)(2,1)S(1)} %collective-permute-done.back2, pred[]{:T(512)S(6)} %eq.33, bf16[16,512]{1,0:T(8,128)(2,1)S(1)} %pad.7, bf16[256,512]{1,0:T(8,128)(2,1)} %bitcast.16), kind=kLoop, calls=%fused_computation.3 | loop fusion | flops 696320 | bytes 835585 | tf_op jit(solution)/shard_map/jit(_where)/select_n | solution.py:268
  18.9 0.0 copy-start.1
  18.9 0.0 collective-permute-done.2.refs_2_
  18.9 1.5 %collective-permute-start.9 = (bf16[160,1024]{1,0:T(8,128)(2,1)S(1)}, bf16[160,1024]{1,0:T(8,128)(2,1)S(1)}, u32[]{:S(2)}, u32[]{:S(2)}) collective-permute-start(bf16[160,1024]{1,0:T(8,128)(2,1)S(1)} %collective-permute-done.2.refs_2_), channel_id=1, source_target_pairs={{0,2},{4,0},{8,4},{12,8},{14,12},{10,14},{6,10},{2,6},{1,3},{5,1},... | collective-permute-start | bytes 983048 | tf_op jit(solution)/shard_map/ppermute | solution.py:231
  20.4 0.0 collective-permute-done.1.refs_1_
  20.4 1.1 %collective-permute-start.8 = (bf16[160,1024]{1,0:T(8,128)(2,1)}, bf16[160,1024]{1,0:T(8,128)(2,1)S(1)}, u32[]{:S(2)}, u32[]{:S(2)}) collective-permute-start(bf16[160,1024]{1,0:T(8,128)(2,1)} %collective-permute-done.1.refs_1_), channel_id=1, source_target_pairs={{2,0},{0,4},{4,8},{8,12},{12,14},{14,10},{10,6},{6,2},{3,1},{1,5},... | collective-permute-start | bytes 983048 | tf_op jit(solution)/shard_map/ppermute | solution.py:230
  21.5 0.0 collective-permute-done.3.attn_other
  21.5 0.0 collective-permute-done.4.w_other
  21.5 0.0 copy-done.3
  21.5 3.0 %shard_map.93 = (bf16[256,1280]{1,0:T(8,128)(2,1)S(1)}, bf16[128,1280]{1,0:T(8,128)(2,1)S(1)}) custom-call(s32[1]{0:T(128)} %bitcast.1.core, bf16[256,1280]{1,0:T(8,128)(2,1)S(1)} %copy-done.3, bf16[256,640]{1,0:T(8,128)(2,1)} %shard_map.92.attn_own, bf16[256,640]{1,0:T(8,128)(2,1)} %collective-permute-done.3.attn_other, bf16[640,1280]{1,0:T(8,128)(2,1)S(1)} %copy-done, ...), custom_call_target="tpu_custom_call" | custom-call | flops 20000000000 | bytes 5570564 | tf_op jit(solution)/shard_map/pallas_call | solution.py:43
  24.5 1.4 %collective-permute-start.6 = (bf16[272,512]{1,0:T(8,128)(2,1)S(1)}, bf16[272,512]{1,0:T(8,128)(2,1)S(1)}, u32[]{:S(2)}, u32[]{:S(2)}) collective-permute-start(bf16[272,512]{1,0:T(8,128)(2,1)S(1)} %broadcast_select_fusion.2), channel_id=1, source_target_pairs={{0,2},{2,0},{4,6},{6,4},{8,10},{10,8},{12,14},{14,12},{1,3},{3,1},... | collective-permute-start | bytes 835592 | tf_op jit(solution)/shard_map/ppermute | solution.py:190
  26.0 2.6 %collective-permute-start.5 = (bf16[128,1280]{1,0:T(8,128)(2,1)S(1)}, bf16[128,1280]{1,0:T(8,128)(2,1)S(1)}, u32[]{:S(2)}, u32[]{:S(2)}) collective-permute-start(bf16[128,1280]{1,0:T(8,128)(2,1)S(1)} %get-tuple-element.23), channel_id=1, source_target_pairs={{0,2},{2,4},{4,6},{6,8},{8,10},{10,12},{12,14},{1,3},{3,5},{5,7},{... | collective-permute-start | bytes 983048 | tf_op jit(solution)/shard_map/ppermute | solution.py:186
  28.5 0.4 collective-permute-done.9.refs_4_
  29.0 2.7 %collective-permute-done.8.refs_3_ = bf16[160,1024]{1,0:T(8,128)(2,1)S(1)} collective-permute-done((bf16[160,1024]{1,0:T(8,128)(2,1)}, bf16[160,1024]{1,0:T(8,128)(2,1)S(1)}, u32[]{:S(2)}, u32[]{:S(2)}) %collective-permute-start.8) | collective-permute-done | bytes 327712 | tf_op jit(solution)/shard_map/ppermute | solution.py:230
  31.7 0.0 collective-permute-start.10
  31.7 2.0 %collective-permute-start.11 = (bf16[160,1024]{1,0:T(8,128)(2,1)S(1)}, bf16[160,1024]{1,0:T(8,128)(2,1)S(1)}, u32[]{:S(2)}, u32[]{:S(2)}) collective-permute-start(bf16[160,1024]{1,0:T(8,128)(2,1)S(1)} %collective-permute-done.9.refs_4_), channel_id=1, source_target_pairs={{0,2},{4,0},{8,4},{12,8},{14,12},{10,14},{6,10},{2,6},{1,3},{5,1},... | collective-permute-start | bytes 983048 | tf_op jit(solution)/shard_map/ppermute | solution.py:231
  33.7 7.8 %collective-permute-done.5 = bf16[128,1280]{1,0:T(8,128)(2,1)S(1)} collective-permute-done((bf16[128,1280]{1,0:T(8,128)(2,1)S(1)}, bf16[128,1280]{1,0:T(8,128)(2,1)S(1)}, u32[]{:S(2)}, u32[]{:S(2)}) %collective-permute-start.5) | collective-permute-done | bytes 327712 | tf_op jit(solution)/shard_map/ppermute | solution.py:186
  41.5 0.0 collective-permute-start.7
  41.5 0.0 collective-permute-done.6.back1
  41.5 0.0 copy-done.1
  41.5 2.6 %shard_map.94.self_out = f32[128,4096]{1,0:T(8,128)S(1)} custom-call(s32[1]{0:T(128)} %bitcast.seq, bf16[128,4096]{1,0:T(8,128)(2,1)S(1)} %copy-done.1, bf16[272,512]{1,0:T(8,128)(2,1)S(1)} %pad_maximum_fusion.own, bf16[272,512]{1,0:T(8,128)(2,1)S(1)} %collective-permute-done.6.back1, bf16[272,512]{1,0:T(8,128)(2,1)S(1)} %collective-permute-done.back2), custom_call_target="tpu_custom_call" | custom-call | flops 20000000000 | bytes 3981316 | tf_op jit(solution)/shard_map/pallas_call | solution.py:43
  44.1 0.0 copy-start.5
  44.1 3.1 %collective-permute-done.11.refs_6_ = bf16[160,1024]{1,0:T(8,128)(2,1)S(1)} collective-permute-done((bf16[160,1024]{1,0:T(8,128)(2,1)S(1)}, bf16[160,1024]{1,0:T(8,128)(2,1)S(1)}, u32[]{:S(2)}, u32[]{:S(2)}) %collective-permute-start.11) | collective-permute-done | bytes 327712 | tf_op jit(solution)/shard_map/ppermute | solution.py:231
  47.2 0.0 collective-permute-done.10.refs_5_
  47.3 2.5 %collective-permute-start.13 = (bf16[80,1024]{1,0:T(8,128)(2,1)S(1)}, bf16[80,1024]{1,0:T(8,128)(2,1)S(1)}, u32[]{:S(2)}, u32[]{:S(2)}) collective-permute-start(bf16[80,1024]{1,0:T(8,128)(2,1)S(1)} %slice.7), channel_id=1, source_target_pairs={{0,2},{4,0},{8,4},{12,8},{14,12},{10,14},{6,10},{2,6},{1,3},{5,1},... | collective-permute-start | bytes 491528 | tf_op jit(solution)/shard_map/ppermute | solution.py:231
  49.8 0.0 collective-permute-start.12
  49.8 0.0 collective-permute-done.7
  49.9 2.8 %collective-permute-done.13.refs_8_ = bf16[80,1024]{1,0:T(8,128)(2,1)S(1)} collective-permute-done((bf16[80,1024]{1,0:T(8,128)(2,1)S(1)}, bf16[80,1024]{1,0:T(8,128)(2,1)S(1)}, u32[]{:S(2)}, u32[]{:S(2)}) %collective-permute-start.13) | collective-permute-done | bytes 163872 | tf_op jit(solution)/shard_map/ppermute | solution.py:231
  52.7 2.5 %collective-permute-done.12.refs_7_ = bf16[80,1024]{1,0:T(8,128)(2,1)S(1)} collective-permute-done((bf16[80,1024]{1,0:T(8,128)(2,1)S(1)}, bf16[80,1024]{1,0:T(8,128)(2,1)S(1)}, u32[]{:S(2)}, u32[]{:S(2)}) %collective-permute-start.12) | collective-permute-done | bytes 163872 | tf_op jit(solution)/shard_map/ppermute | solution.py:230
  55.1 0.1 broadcast_in_dim.4
  55.2 0.0 copy-done.5
  55.2 6.2 %shard_map.95 = bf16[128,4096]{1,0:T(8,128)(2,1)} custom-call(s32[11]{0:T(128)S(1)} %stack.47.place, bf16[128,4096]{1,0:T(8,128)(2,1)S(1)} %copy-done.1, f32[128,4096]{1,0:T(8,128)S(1)} %shard_map.94.self_out, s32[2,128]{1,0:T(2,128)S(1)} %bitcast.15, f32[1,4096]{1,0:T(1,128)S(1)} %bitcast.14, bf16[256,1280]{1,0:T(8,128)(2,1)S(1)} %get-tuple-element.25.norm_own, ...), custom_call_target="tpu_custom_call" | custom-call | flops 20000000000 | bytes 8143916 | tf_op jit(solution)/shard_map/pallas_call | solution.py:43
  (8 shorter events, 0.1 us)
Async XLA Ops:
  0.0 4.9 %copy-start.2 = (bf16[3,256,640]{2,1,0:T(8,128)(2,1)S(1)}, bf16[3,256,640]{2,1,0:T(8,128)(2,1)}, u32[]{:S(2)}) copy-start(bf16[3,256,640]{2,1,0:T(8,128)(2,1)} %qkv) | copy-start | bytes 2949124
  0.0 1.1 %copy-start.4 = (bf16[160,2,512]{2,1,0:T(2,128)(2,1)S(1)}, bf16[160,2,512]{2,1,0:T(2,128)(2,1)}, u32[]{:S(2)}) copy-start(bf16[160,2,512]{2,1,0:T(2,128)(2,1)} %w.1) | copy-start | bytes 983044
  1.8 5.1 %copy-start.7 = (s32[128]{0:T(128)S(1)}, s32[128]{0:T(128)}, u32[]{:S(2)}) copy-start(s32[128]{0:T(128)} %param.11) | copy-start | bytes 1540
  1.8 5.1 %copy-start.6 = (bf16[2,128,512]{2,1,0:T(8,128)(2,1)S(1)}, bf16[2,128,512]{2,1,0:T(8,128)(2,1)}, u32[]{:S(2)}) copy-start(bf16[2,128,512]{2,1,0:T(8,128)(2,1)} %param.10) | copy-start | bytes 786436
  1.8 9.2 %copy-start = (bf16[640,1280]{1,0:T(8,128)(2,1)S(1)}, bf16[640,1280]{1,0:T(8,128)(2,1)}, u32[]{:S(2)}) copy-start(bf16[640,1280]{1,0:T(8,128)(2,1)} %w_own.1) | copy-start | bytes 4915204
  1.8 9.4 %copy-start.8 = (f32[32]{0:T(128)S(1)}, f32[32]{0:T(128)}, u32[]{:S(2)}) copy-start(f32[32]{0:T(128)} %param.17) | copy-start | bytes 388
  1.8 17.1 %collective-permute-start.2 = (bf16[160,1024]{1,0:T(8,128)(2,1)S(1)}, bf16[160,1024]{1,0:T(8,128)(2,1)S(1)}, u32[]{:S(2)}, u32[]{:S(2)}) collective-permute-start(bf16[160,1024]{1,0:T(8,128)(2,1)S(1)} %shard_map.91.refs_0_), channel_id=1, source_target_pairs={{0,2},{4,0},{8,4},{12,8},{14,12},{10,14},{6,10},{2,6},{1,3},{5,1},... | collective-permute-start | bytes 983048 | tf_op jit(solution)/shard_map/ppermute | solution.py:231
  4.8 15.6 %collective-permute-start.1 = (bf16[160,1024]{1,0:T(8,128)(2,1)S(1)}, bf16[160,1024]{1,0:T(8,128)(2,1)}, u32[]{:S(2)}, u32[]{:S(2)}) collective-permute-start(bf16[160,1024]{1,0:T(8,128)(2,1)S(1)} %shard_map.91.refs_0_), channel_id=1, source_target_pairs={{2,0},{0,4},{4,8},{8,12},{12,14},{14,10},{10,6},{6,2},{3,1},{1,5},... | collective-permute-start | bytes 983048 | tf_op jit(solution)/shard_map/ppermute | solution.py:230
  6.8 14.7 %copy-start.3 = (bf16[256,1280]{1,0:T(8,128)(2,1)S(1)}, bf16[256,1280]{1,0:T(8,128)(2,1)}, u32[]{:S(2)}) copy-start(bf16[256,1280]{1,0:T(8,128)(2,1)} %hidden) | copy-start | bytes 1966084
  6.8 14.7 %collective-permute-start.3 = (bf16[256,640]{1,0:T(8,128)(2,1)}, bf16[256,640]{1,0:T(8,128)(2,1)}, u32[]{:S(2)}, u32[]{:S(2)}) collective-permute-start(bf16[256,640]{1,0:T(8,128)(2,1)} %shard_map.92.attn_own), channel_id=1, source_target_pairs={{0,1},{1,0},{2,3},{3,2},{4,5},{5,4},{6,7},{7,6},{8,9},{9,8},{10,11... | collective-permute-start | bytes 983048 | tf_op jit(solution)/shard_map/ppermute | solution.py:190
  6.9 11.0 %collective-permute-start = (bf16[272,512]{1,0:T(8,128)(2,1)S(1)}, bf16[272,512]{1,0:T(8,128)(2,1)S(1)}, u32[]{:S(2)}, u32[]{:S(2)}) collective-permute-start(bf16[272,512]{1,0:T(8,128)(2,1)S(1)} %pad_maximum_fusion.own), channel_id=1, source_target_pairs={{0,4},{2,6},{4,8},{6,10},{8,12},{10,14},{1,5},{3,7},{5,9},{7,11},{... | collective-permute-start | bytes 835592 | tf_op jit(solution)/shard_map/ppermute | solution.py:186
  10.9 10.6 %collective-permute-start.4 = (bf16[640,1280]{1,0:T(8,128)(2,1)S(1)}, bf16[640,1280]{1,0:T(8,128)(2,1)}, u32[]{:S(2)}, u32[]{:S(2)}) collective-permute-start(bf16[640,1280]{1,0:T(8,128)(2,1)S(1)} %copy-done), channel_id=1, source_target_pairs={{0,1},{1,0},{2,3},{3,2},{4,5},{5,4},{6,7},{7,6},{8,9},{9,8},{10,11... | collective-permute-start | bytes 4915208 | tf_op jit(solution)/shard_map/ppermute | solution.py:190
  18.9 22.6 %copy-start.1 = (bf16[128,4096]{1,0:T(8,128)(2,1)S(1)}, bf16[128,4096]{1,0:T(8,128)(2,1)}, u32[]{:S(2)}) copy-start(bf16[128,4096]{1,0:T(8,128)(2,1)} %q.2) | copy-start | bytes 3145732
  18.9 10.0 %collective-permute-start.9 = (bf16[160,1024]{1,0:T(8,128)(2,1)S(1)}, bf16[160,1024]{1,0:T(8,128)(2,1)S(1)}, u32[]{:S(2)}, u32[]{:S(2)}) collective-permute-start(bf16[160,1024]{1,0:T(8,128)(2,1)S(1)} %collective-permute-done.2.refs_2_), channel_id=1, source_target_pairs={{0,2},{4,0},{8,4},{12,8},{14,12},{10,14},{6,10},{2,6},{1,3},{5,1},... | collective-permute-start | bytes 983048 | tf_op jit(solution)/shard_map/ppermute | solution.py:231
  20.4 11.3 %collective-permute-start.8 = (bf16[160,1024]{1,0:T(8,128)(2,1)}, bf16[160,1024]{1,0:T(8,128)(2,1)S(1)}, u32[]{:S(2)}, u32[]{:S(2)}) collective-permute-start(bf16[160,1024]{1,0:T(8,128)(2,1)} %collective-permute-done.1.refs_1_), channel_id=1, source_target_pairs={{2,0},{0,4},{4,8},{8,12},{12,14},{14,10},{10,6},{6,2},{3,1},{1,5},... | collective-permute-start | bytes 983048 | tf_op jit(solution)/shard_map/ppermute | solution.py:230
  24.5 17.0 %collective-permute-start.6 = (bf16[272,512]{1,0:T(8,128)(2,1)S(1)}, bf16[272,512]{1,0:T(8,128)(2,1)S(1)}, u32[]{:S(2)}, u32[]{:S(2)}) collective-permute-start(bf16[272,512]{1,0:T(8,128)(2,1)S(1)} %broadcast_select_fusion.2), channel_id=1, source_target_pairs={{0,2},{2,0},{4,6},{6,4},{8,10},{10,8},{12,14},{14,12},{1,3},{3,1},... | collective-permute-start | bytes 835592 | tf_op jit(solution)/shard_map/ppermute | solution.py:190
  26.0 15.6 %collective-permute-start.5 = (bf16[128,1280]{1,0:T(8,128)(2,1)S(1)}, bf16[128,1280]{1,0:T(8,128)(2,1)S(1)}, u32[]{:S(2)}, u32[]{:S(2)}) collective-permute-start(bf16[128,1280]{1,0:T(8,128)(2,1)S(1)} %get-tuple-element.23), channel_id=1, source_target_pairs={{0,2},{2,4},{4,6},{6,8},{8,10},{10,12},{12,14},{1,3},{3,5},{5,7},{... | collective-permute-start | bytes 983048 | tf_op jit(solution)/shard_map/ppermute | solution.py:186
  31.7 15.6 %collective-permute-start.10 = (bf16[160,1024]{1,0:T(8,128)(2,1)S(1)}, bf16[160,1024]{1,0:T(8,128)(2,1)S(1)}, u32[]{:S(2)}, u32[]{:S(2)}) collective-permute-start(bf16[160,1024]{1,0:T(8,128)(2,1)S(1)} %collective-permute-done.8.refs_3_), channel_id=1, source_target_pairs={{2,0},{0,4},{4,8},{8,12},{12,14},{14,10},{10,6},{6,2},{3,1},{1,5},... | collective-permute-start | bytes 983048 | tf_op jit(solution)/shard_map/ppermute | solution.py:230
  31.7 15.5 %collective-permute-start.11 = (bf16[160,1024]{1,0:T(8,128)(2,1)S(1)}, bf16[160,1024]{1,0:T(8,128)(2,1)S(1)}, u32[]{:S(2)}, u32[]{:S(2)}) collective-permute-start(bf16[160,1024]{1,0:T(8,128)(2,1)S(1)} %collective-permute-done.9.refs_4_), channel_id=1, source_target_pairs={{0,2},{4,0},{8,4},{12,8},{14,12},{10,14},{6,10},{2,6},{1,3},{5,1},... | collective-permute-start | bytes 983048 | tf_op jit(solution)/shard_map/ppermute | solution.py:231
  41.5 8.3 %collective-permute-start.7 = (bf16[128,1280]{1,0:T(8,128)(2,1)S(1)}, bf16[128,1280]{1,0:T(8,128)(2,1)S(1)}, u32[]{:S(2)}, u32[]{:S(2)}) collective-permute-start(bf16[128,1280]{1,0:T(8,128)(2,1)S(1)} %collective-permute-done.5), channel_id=1, source_target_pairs={{0,1},{1,0},{2,3},{3,2},{4,5},{5,4},{6,7},{7,6},{8,9},{9,8},{10,11... | collective-permute-start | bytes 983048 | tf_op jit(solution)/shard_map/ppermute | solution.py:190
  44.1 11.1 %copy-start.5 = (s32[128,2]{0,1:T(2,128)S(1)}, s32[128,2]{0,1:T(2,128)}, u32[]{:S(2)}) copy-start(s32[128,2]{0,1:T(2,128)} %param.12) | copy-start | bytes 3076
  47.3 5.4 %collective-permute-start.13 = (bf16[80,1024]{1,0:T(8,128)(2,1)S(1)}, bf16[80,1024]{1,0:T(8,128)(2,1)S(1)}, u32[]{:S(2)}, u32[]{:S(2)}) collective-permute-start(bf16[80,1024]{1,0:T(8,128)(2,1)S(1)} %slice.7), channel_id=1, source_target_pairs={{0,2},{4,0},{8,4},{12,8},{14,12},{10,14},{6,10},{2,6},{1,3},{5,1},... | collective-permute-start | bytes 491528 | tf_op jit(solution)/shard_map/ppermute | solution.py:231
  49.8 5.3 %collective-permute-start.12 = (bf16[80,1024]{1,0:T(8,128)(2,1)S(1)}, bf16[80,1024]{1,0:T(8,128)(2,1)S(1)}, u32[]{:S(2)}, u32[]{:S(2)}) collective-permute-start(bf16[80,1024]{1,0:T(8,128)(2,1)S(1)} %slice.6), channel_id=1, source_target_pairs={{2,0},{0,4},{4,8},{8,12},{12,14},{14,10},{10,6},{6,2},{3,1},{1,5},... | collective-permute-start | bytes 491528 | tf_op jit(solution)/shard_map/ppermute | solution.py:230

commit v3 on v2

--- a/solution.py
+++ b/solution.py
@@ -17,7 +17,7 @@
 LOG2E = math.log2(math.e)
 F32 = jnp.float32
 BF16 = jnp.bfloat16
-PLANNED_FLOPS = 20_000_000_000
+PLANNED_FLOPS = 20000000000
 VMEM_LIMIT = 40 * 1024 * 1024
 
 
@@ -131,7 +131,7 @@
             out[:, j * HEAD_SIZE : (j + 1) * HEAD_SIZE] = o[i * rows : (i + 1) * rows]
 
 
-def cross_kernel(pieces, place, q, self_out, span, gate, norm_own, before_a, before_b, *refs):
+def cross_kernel(pieces, place, q, self_out, span, gate, norm_own, before_mine, before_other, *refs):
     weights, out, w, kv = refs[:pieces], refs[pieces], refs[pieces + 1], refs[pieces + 2]
     rows = q.shape[0]
     tile = norm_own.shape[0]
@@ -143,7 +143,9 @@
         n = piece.shape[0]
         start = place[2 + i]
         w[pl.ds(pl.multiple_of(start, ID_ROWS), n), :] = piece[...]
-    norms = jnp.concatenate([before_a[...], before_b[...], norm_own[...]], axis=0)
+    first, mine, other = place[1] == 0, before_mine[...], before_other[...]
+    norms = [jnp.where(first, mine, other), jnp.where(first, other, mine), norm_own[...]]
+    norms = jnp.concatenate(norms, axis=0)
     kv[...] = dot_n(norms, w[...]).astype(BF16)
     this = place[0].astype(F32)
     low = column_of(span[0:1, :].astype(F32))
@@ -222,40 +224,36 @@
     rings = n == 8 and rows % 32 == 0
     even = seq % 2 == 0
 
+    chunks = 1
+    ways = [(ring[i - 1], ring[i]) for i in range(n)], [(ring[i], ring[i - 1]) for i in range(n)]
+
     def around(blocks):
-        if not rings:
-            return ()
-        up, down = blocks
-        return (
-            lax.ppermute(up, "seq", [(ring[i - 1], ring[i]) for i in range(n)]),
-            lax.ppermute(down, "seq", [(ring[i], ring[i - 1]) for i in range(n)]),
-        )
-
+        return [lax.ppermute(block, "seq", ways[way]) for way, block in blocks] if rings else []
+
+    ids = jnp.broadcast_to(doc_ids.astype(BF16), (ID_ROWS, text_rows))
+    ids = jnp.pad(ids, ((0, 0), (0, kv_cols - text_rows)))
+    text = jnp.concatenate([text_key_value.reshape(-1, kv_cols), ids], axis=0)
     (w,) = call(
         rows_kernel,
         (sds((rows, 2 * kv_cols), BF16),),
         (cross_keyvalue_weight,),
     )
     out_weight_other = other_core(vision_out_weight)
-    ids = jnp.broadcast_to(doc_ids.astype(BF16), (ID_ROWS, text_rows))
-    ids = jnp.pad(ids, ((0, 0), (0, kv_cols - text_rows)))
-    text = jnp.concatenate([text_key_value.reshape(-1, kv_cols), ids], axis=0)
-    step1 = around((w, w))
+    step1 = around([(way, w[c * rows // chunks : (c + 1) * rows // chunks]) for c in range(chunks) for way in (0, 1)])
     attn = call(
         vision_kernel,
         sds((tile_rows, vision_qkv.shape[2]), BF16),
-        (after(vision_qkv, w),),
+        (vision_qkv,),
     )
     attn_other = other_core(attn)
-    back2 = shifted(after(text, attn), "seq", 2)
-    mark = marker(attn)
-    step2 = around([after(block, mark) for block in step1])
+    back2 = shifted(text, "seq", 2)
+    step2 = around([(i % 2, block) for i, block in enumerate(step1)])
     norm, norm_half = call(
         norm_kernel,
         (sds((tile_rows, width), BF16), sds((tile_rows // 2, width), BF16)),
         (
             core.reshape(1),
-            after(vision_hidden, back2, *step1),
+            vision_hidden,
             attn,
             attn_other,
             vision_out_weight,
@@ -263,27 +261,27 @@
         ),
         smem=1,
     )
-    mark = marker(norm)
-    step3 = around([after(block, mark) for block in step2])
-    back1 = flipped(after(jnp.where(even, text, back2), norm), "seq", 1)
+    step3 = around([(i % 2, block) for i, block in enumerate(step2)])
+    back1 = flipped(jnp.where(even, text, back2), "seq", 1)
     before_mine = shifted(norm_half, "seq", 1)
     before_other = other_core(before_mine)
-    before_a = jnp.where(core == 0, before_mine, before_other)
-    before_b = jnp.where(core == 0, before_other, before_mine)
     self_out = call(
         self_kernel,
         sds(text_query_rows.shape, F32),
-        (seq.reshape(1), after(text_query_rows, before_mine), text, back1, back2),
+        (seq.reshape(1), text_query_rows, text, back1, back2),
         smem=1,
     )
     if rings:
-        up, down = [after(block, self_out) for block in step3]
-        step4 = around((up[:half], down[half:]))
+        up, down = [block for block in (step3[0], step3[-1])]
+        step4 = around([(0, up[:half]), (1, down[-half:])])
+    if rings:
         at = lambda p: jnp.where(p % n < n // 2, 2 * (p % n), 2 * (n - 1 - p % n) + 1) * rows
         place = jnp.where(even, seq // 2, n - 1 - seq // 2)
         pieces = [(w, seq * rows)]
-        for k, (up, down) in ((1, step1), (2, step2), (3, step3)):
-            pieces += [(up, at(place + n - k)), (down, at(place + k))]
+        for k, step in ((1, step1), (2, step2), (3, step3)):
+            for i, block in enumerate(step):
+                first = at(place + (k if i % 2 else n - k)) + i // 2 * (rows // chunks)
+                pieces += [(block, first)]
         pieces += [(step4[0], at(place + n // 2)), (step4[1], at(place + n // 2) + half)]
     else:
         pieces = [(lax.all_gather(w, "seq", axis=0, tiled=True), 0)]
@@ -300,8 +298,8 @@
             tile_span.T,
             gate,
             norm,
-            before_a,
-            before_b,
+            before_mine,
+            before_other,
             *[p[0] for p in pieces],
         ),
         smem=1,

time: 61.7 us -> 55.1 us (0.89)
  waiting for transfers between devices: 25.9 us -> 18.1 us
  Pallas kernels: 14.3 us -> 15.4 us
  other arithmetic: 1.09 us -> 0.1 us
  local copies, waits for them, and re-layouts: 1.3 us -> 2.23 us
    ppermute x2, waiting for transfers between devices: 14.4 us -> 3.51 us  [shifted(): lax.ppermute(block, axis, [(i, i + distance) for i in range(n - distance)])]
    ppermute x4, waiting for transfers between devices: 0.01 us -> 5.2 us  [flipped(): lax.ppermute(block, axis, [(i, i ^ bits) for i in range(lax.axis_size(axi...]
    ppermute x8, waiting for transfers between devices: 11.5 us -> 9.35 us  [around(): lax.ppermute(block, 'seq', ways[way])]
    pallas_call x5, Pallas kernels: 14.3 us -> 15.4 us  [call(): pl.pallas_call(kernel, out_shape=out_shape, in_specs=[pl.BlockSpec(memory...]
    select_n x2 -> x1, other arithmetic: 1.07 us -> 0.07 us  [per_device(): back1 = flipped(jnp.where(even, text, back2), 'seq', 1)]
    unnamed x18 -> x36, local copies, waits for them, and re-layouts: 1.1 us -> 2.04 us
    ppermute x8, starting transfers between devices: 10.3 us -> 9.62 us  [around(): lax.ppermute(block, 'seq', ways[way])]
  transfers between devices with their start and end apart: 14 -> 14, of which waited for: 7 -> 5; matrix products, arithmetic and copies ran while one was open for 2% -> 0% of each run, Pallas kernels for 12% -> 15%
where the time goes in v3:
time: 55.1 us; the launch traced here: 54.5 us
  starting transfers between devices  18.5 us (34%)
  waiting for transfers between devices  18.1 us (33%)
  Pallas kernels  15.4 us (28%)
  local copies, waits for them, and re-layouts  2.23 us (4%)
    pallas_call x5, Pallas kernels, call(): pl.pallas_call(kernel, out_shape=out_shape, in_specs=[pl.BlockSpec(memory...  15.4 us
    ppermute x8, starting transfers between devices, around(): lax.ppermute(block, 'seq', ways[way])  9.62 us
    ppermute x8, waiting for transfers between devices, around(): lax.ppermute(block, 'seq', ways[way])  9.35 us
    ppermute x2, starting transfers between devices, shifted(): lax.ppermute(block, axis, [(i, i + distance) for i in range(n - distance)])  7.21 us
    ppermute x4, waiting for transfers between devices, flipped(): lax.ppermute(block, axis, [(i, i ^ bits) for i in range(lax.axis_size(axi...  5.2 us
    ppermute x2, waiting for transfers between devices, shifted(): lax.ppermute(block, axis, [(i, i + distance) for i in range(n - distance)])  3.51 us
    unnamed x36, local copies, waits for them, and re-layouts  2.04 us
    ppermute x4, starting transfers between devices, flipped(): lax.ppermute(block, axis, [(i, i ^ bits) for i in range(lax.axis_size(axi...  1.67 us
  transfers between devices with their start and end apart: 14, of which 5 were waited for; matrix products, arithmetic and copies ran while one was open for 0% of the time, Pallas kernels for 15%

profile of v3, /device:TPU:0, one launch (start us, length us, event | category | flops | bytes accessed | tf_op | source)
XLA Modules:
  0.0 54.5 jit_solution(1393897941839080443)
XLA Ops:
  0.0 1.1 %copy-done.4 = bf16[160,2,512]{2,1,0:T(2,128)(2,1)S(1)} copy-done((bf16[160,2,512]{2,1,0:T(2,128)(2,1)S(1)}, bf16[160,2,512]{2,1,0:T(2,128)(2,1)}, u32[]{:S(2)}) %copy-start.4) | copy-done | bytes 327704
  1.1 0.7 %shard_map.94.refs_0_ = bf16[160,1024]{1,0:T(8,128)(2,1)S(1)} custom-call(bf16[160,2,512]{2,1,0:T(2,128)(2,1)S(1)} %copy-done.4), custom_call_target="tpu_custom_call" | custom-call | flops 20000000000 | bytes 655360 | tf_op jit(solution)/shard_map/pallas_call | solution.py:43
  1.8 0.0 copy-start.16
  1.8 0.0 copy-start.14
  1.9 0.0 copy-start.3
  1.9 3.1 %collective-permute-start.6 = (bf16[160,1024]{1,0:T(8,128)(2,1)S(1)}, bf16[160,1024]{1,0:T(8,128)(2,1)S(1)}, u32[]{:S(2)}, u32[]{:S(2)}) collective-permute-start(bf16[160,1024]{1,0:T(8,128)(2,1)S(1)} %shard_map.94.refs_0_), channel_id=1, source_target_pairs={{2,0},{0,4},{4,8},{8,12},{12,14},{14,10},{10,6},{6,2},{3,1},{1,5},... | collective-permute-start | bytes 983048 | tf_op jit(solution)/shard_map/ppermute | solution.py:231
  4.9 0.0 collective-permute-start.7
  4.9 0.0 copy-done
  4.9 0.0 collective-permute-start.3
  5.0 7.6 %collective-permute-done.6.refs_1_ = bf16[160,1024]{1,0:T(8,128)(2,1)S(1)} collective-permute-done((bf16[160,1024]{1,0:T(8,128)(2,1)S(1)}, bf16[160,1024]{1,0:T(8,128)(2,1)S(1)}, u32[]{:S(2)}, u32[]{:S(2)}) %collective-permute-start.6) | collective-permute-done | bytes 327712 | tf_op jit(solution)/shard_map/ppermute | solution.py:231
  12.6 1.8 %collective-permute-start.8 = (bf16[160,1024]{1,0:T(8,128)(2,1)S(1)}, bf16[160,1024]{1,0:T(8,128)(2,1)}, u32[]{:S(2)}, u32[]{:S(2)}) collective-permute-start(bf16[160,1024]{1,0:T(8,128)(2,1)S(1)} %collective-permute-done.6.refs_1_), channel_id=1, source_target_pairs={{2,0},{0,4},{4,8},{8,12},{12,14},{14,10},{10,6},{6,2},{3,1},{1,5},... | collective-permute-start | bytes 983048 | tf_op jit(solution)/shard_map/ppermute | solution.py:231
  14.4 0.0 collective-permute-done.7.refs_2_
  14.4 0.2 collective-permute-start.9
  14.6 0.0 copy-done.2
  14.6 1.9 %shard_map.92.attn_own = bf16[256,640]{1,0:T(8,128)(2,1)} custom-call(bf16[3,256,640]{2,1,0:T(8,128)(2,1)S(1)} %copy-done.2), custom_call_target="tpu_custom_call" | custom-call | flops 20000000000 | bytes 1310720 | tf_op jit(solution)/shard_map/pallas_call | solution.py:43
  16.5 0.0 copy-done.5
  16.5 0.0 copy-done.7
  16.5 0.0 copy-done.9
  16.5 0.1 collective-permute-start.2
  16.6 0.0 copy-done.16
  16.6 0.0 copy-done.14
  16.6 3.7 %collective-permute-start = (bf16[272,512]{1,0:T(8,128)(2,1)S(1)}, bf16[272,512]{1,0:T(8,128)(2,1)S(1)}, u32[]{:S(2)}, u32[]{:S(2)}) collective-permute-start(bf16[272,512]{1,0:T(8,128)(2,1)S(1)} %pad_maximum_fusion.own), channel_id=1, source_target_pairs={{0,4},{2,6},{4,8},{6,10},{8,12},{10,14},{1,5},{3,7},{5,9},{7,11},{... | collective-permute-start | bytes 835592 | tf_op jit(solution)/shard_map/ppermute | solution.py:188
  20.4 1.2 %collective-permute-done.8.refs_3_ = bf16[160,1024]{1,0:T(8,128)(2,1)} collective-permute-done((bf16[160,1024]{1,0:T(8,128)(2,1)S(1)}, bf16[160,1024]{1,0:T(8,128)(2,1)}, u32[]{:S(2)}, u32[]{:S(2)}) %collective-permute-start.8) | collective-permute-done | bytes 327712 | tf_op jit(solution)/shard_map/ppermute | solution.py:231
  21.6 1.5 %collective-permute-start.10 = (bf16[160,1024]{1,0:T(8,128)(2,1)}, bf16[160,1024]{1,0:T(8,128)(2,1)S(1)}, u32[]{:S(2)}, u32[]{:S(2)}) collective-permute-start(bf16[160,1024]{1,0:T(8,128)(2,1)} %collective-permute-done.8.refs_3_), channel_id=1, source_target_pairs={{2,0},{0,4},{4,8},{8,12},{12,14},{14,10},{10,6},{6,2},{3,1},{1,5},... | collective-permute-start | bytes 983048 | tf_op jit(solution)/shard_map/ppermute | solution.py:231
  23.1 0.0 collective-permute-done.9.refs_4_
  23.1 0.5 collective-permute-start.11
  23.6 0.0 collective-permute-done.2.attn_other
  23.6 0.0 collective-permute-done.3.w_other
  23.6 0.0 copy-done.3
  23.6 0.0 copy-start.15
  23.6 0.0 copy-start.17
  23.6 3.7 %shard_map.93 = (bf16[256,1280]{1,0:T(8,128)(2,1)S(1)}, bf16[128,1280]{1,0:T(8,128)(2,1)}) custom-call(s32[1]{0:T(128)} %bitcast.1.core, bf16[256,1280]{1,0:T(8,128)(2,1)S(1)} %copy-done.3, bf16[256,640]{1,0:T(8,128)(2,1)} %shard_map.92.attn_own, bf16[256,640]{1,0:T(8,128)(2,1)} %collective-permute-done.2.attn_other, bf16[640,1280]{1,0:T(8,128)(2,1)S(1)} %copy-done, ...), custom_call_target="tpu_custom_call" | custom-call | flops 20000000000 | bytes 5570564 | tf_op jit(solution)/shard_map/pallas_call | solution.py:43
  27.4 0.8 %copy-done.12 = bf16[256,1280]{1,0:T(8,128)(2,1)} copy-done((bf16[256,1280]{1,0:T(8,128)(2,1)}, bf16[256,1280]{1,0:T(8,128)(2,1)S(1)}, u32[]{:S(2)}) %copy-start.12) | copy-done | bytes 655384
  28.2 3.5 %collective-permute-start.4 = (bf16[128,1280]{1,0:T(8,128)(2,1)}, bf16[128,1280]{1,0:T(8,128)(2,1)S(1)}, u32[]{:S(2)}, u32[]{:S(2)}) collective-permute-start(bf16[128,1280]{1,0:T(8,128)(2,1)} %get-tuple-element.8), channel_id=1, source_target_pairs={{0,2},{2,4},{4,6},{6,8},{8,10},{10,12},{12,14},{1,3},{3,5},{5,7},{... | collective-permute-start | bytes 983048 | tf_op jit(solution)/shard_map/ppermute | solution.py:188
  31.7 0.0 collective-permute-done.back2
  31.7 0.0 copy-done.15
  31.7 0.1 broadcast_select_fusion
  31.8 1.6 %collective-permute-start.1 = (bf16[272,512]{1,0:T(8,128)(2,1)S(1)}, bf16[272,512]{1,0:T(8,128)(2,1)S(1)}, u32[]{:S(2)}, u32[]{:S(2)}) collective-permute-start(bf16[272,512]{1,0:T(8,128)(2,1)S(1)} %broadcast_select_fusion), channel_id=1, source_target_pairs={{0,2},{2,0},{4,6},{6,4},{8,10},{10,8},{12,14},{14,12},{1,3},{3,1},... | collective-permute-start | bytes 835592 | tf_op jit(solution)/shard_map/ppermute | solution.py:192
  33.4 0.0 copy-done.17
  33.4 0.1 stack.47.place
  33.5 0.6 %collective-permute-done.10.refs_5_ = bf16[160,1024]{1,0:T(8,128)(2,1)S(1)} collective-permute-done((bf16[160,1024]{1,0:T(8,128)(2,1)}, bf16[160,1024]{1,0:T(8,128)(2,1)S(1)}, u32[]{:S(2)}, u32[]{:S(2)}) %collective-permute-start.10) | collective-permute-done | bytes 327712 | tf_op jit(solution)/shard_map/ppermute | solution.py:231
  34.1 2.4 %collective-permute-start.12 = (bf16[80,1024]{1,0:T(8,128)(2,1)S(1)}, bf16[80,1024]{1,0:T(8,128)(2,1)S(1)}, u32[]{:S(2)}, u32[]{:S(2)}) collective-permute-start(bf16[80,1024]{1,0:T(8,128)(2,1)S(1)} %slice.8), channel_id=1, source_target_pairs={{2,0},{0,4},{4,8},{8,12},{12,14},{14,10},{10,6},{6,2},{3,1},{1,5},... | collective-permute-start | bytes 491528 | tf_op jit(solution)/shard_map/ppermute | solution.py:231
  36.5 0.0 collective-permute-done.11.refs_6_
  36.5 0.0 copy-start.6
  36.5 0.0 copy-start.8
  36.5 0.0 copy-start.10
  36.5 0.0 copy-start.11
  36.6 0.0 copy-start.13
  36.6 0.1 collective-permute-start.13
  36.6 3.5 %collective-permute-done.4.before_mine = bf16[128,1280]{1,0:T(8,128)(2,1)S(1)} collective-permute-done((bf16[128,1280]{1,0:T(8,128)(2,1)}, bf16[128,1280]{1,0:T(8,128)(2,1)S(1)}, u32[]{:S(2)}, u32[]{:S(2)}) %collective-permute-start.4) | collective-permute-done | bytes 327712 | tf_op jit(solution)/shard_map/ppermute | solution.py:188
  40.1 0.0 collective-permute-start.5
  40.1 5.2 %collective-permute-done.1.back1 = bf16[272,512]{1,0:T(8,128)(2,1)S(1)} collective-permute-done((bf16[272,512]{1,0:T(8,128)(2,1)S(1)}, bf16[272,512]{1,0:T(8,128)(2,1)S(1)}, u32[]{:S(2)}, u32[]{:S(2)}) %collective-permute-start.1) | collective-permute-done | bytes 278560 | tf_op jit(solution)/shard_map/ppermute | solution.py:192
  45.3 0.0 copy-done.1
  45.3 2.6 %shard_map.91.self_out = f32[128,4096]{1,0:T(8,128)S(1)} custom-call(s32[1]{0:T(128)} %bitcast.seq, bf16[128,4096]{1,0:T(8,128)(2,1)S(1)} %copy-done.1, bf16[272,512]{1,0:T(8,128)(2,1)S(1)} %pad_maximum_fusion.own, bf16[272,512]{1,0:T(8,128)(2,1)S(1)} %collective-permute-done.1.back1, bf16[272,512]{1,0:T(8,128)(2,1)S(1)} %collective-permute-done.back2), custom_call_target="tpu_custom_call" | custom-call | flops 20000000000 | bytes 3981316 | tf_op jit(solution)/shard_map/pallas_call | solution.py:43
  47.9 0.0 collective-permute-done.12.refs_7_
  47.9 0.0 collective-permute-done.13.refs_8_
  47.9 0.0 collective-permute-done.5.before_other
  48.0 0.1 broadcast_in_dim.4
  48.0 0.0 copy-done.6
  48.0 0.0 copy-done.8
  48.0 0.0 copy-done.10
  48.0 0.0 copy-done.11
  48.0 0.0 copy-done.13
  48.1 6.5 %shard_map.95 = bf16[128,4096]{1,0:T(8,128)(2,1)} custom-call(s32[11]{0:T(128)S(1)} %stack.47.place, bf16[128,4096]{1,0:T(8,128)(2,1)S(1)} %copy-done.1, f32[128,4096]{1,0:T(8,128)S(1)} %shard_map.91.self_out, s32[2,128]{1,0:T(2,128)S(1)} %bitcast.15, f32[1,4096]{1,0:T(1,128)S(1)} %bitcast.14, bf16[256,1280]{1,0:T(8,128)(2,1)S(1)} %copy-done.13, ...), custom_call_target="tpu_custom_call" | custom-call | flops 20000000000 | bytes 8143916 | tf_op jit(solution)/shard_map/pallas_call | solution.py:43
  (15 shorter events, 0.1 us)
Async XLA Ops:
  0.0 4.9 %copy-start = (bf16[640,1280]{1,0:T(8,128)(2,1)S(1)}, bf16[640,1280]{1,0:T(8,128)(2,1)}, u32[]{:S(2)}) copy-start(bf16[640,1280]{1,0:T(8,128)(2,1)} %w_own.1) | copy-start | bytes 4915204
  0.0 14.6 %copy-start.2 = (bf16[3,256,640]{2,1,0:T(8,128)(2,1)S(1)}, bf16[3,256,640]{2,1,0:T(8,128)(2,1)}, u32[]{:S(2)}) copy-start(bf16[3,256,640]{2,1,0:T(8,128)(2,1)} %qkv.1) | copy-start | bytes 2949124
  0.0 1.1 %copy-start.4 = (bf16[160,2,512]{2,1,0:T(2,128)(2,1)S(1)}, bf16[160,2,512]{2,1,0:T(2,128)(2,1)}, u32[]{:S(2)}) copy-start(bf16[160,2,512]{2,1,0:T(2,128)(2,1)} %w.1) | copy-start | bytes 983044
  1.8 14.7 %copy-start.5 = (bf16[160,1024]{1,0:T(8,128)(2,1)}, bf16[160,1024]{1,0:T(8,128)(2,1)S(1)}, u32[]{:S(2)}) copy-start(bf16[160,1024]{1,0:T(8,128)(2,1)S(1)} %shard_map.94.refs_0_) | copy-start | bytes 983044
  1.8 14.7 %copy-start.16 = (s32[128]{0:T(128)S(1)}, s32[128]{0:T(128)}, u32[]{:S(2)}) copy-start(s32[128]{0:T(128)} %param.11) | copy-start | bytes 1540
  1.8 14.8 %copy-start.14 = (bf16[2,128,512]{2,1,0:T(8,128)(2,1)S(1)}, bf16[2,128,512]{2,1,0:T(8,128)(2,1)}, u32[]{:S(2)}) copy-start(bf16[2,128,512]{2,1,0:T(8,128)(2,1)} %param.10) | copy-start | bytes 786436
  1.9 21.8 %copy-start.3 = (bf16[256,1280]{1,0:T(8,128)(2,1)S(1)}, bf16[256,1280]{1,0:T(8,128)(2,1)}, u32[]{:S(2)}) copy-start(bf16[256,1280]{1,0:T(8,128)(2,1)} %hidden.1) | copy-start | bytes 1966084
  1.9 10.7 %collective-permute-start.6 = (bf16[160,1024]{1,0:T(8,128)(2,1)S(1)}, bf16[160,1024]{1,0:T(8,128)(2,1)S(1)}, u32[]{:S(2)}, u32[]{:S(2)}) collective-permute-start(bf16[160,1024]{1,0:T(8,128)(2,1)S(1)} %shard_map.94.refs_0_), channel_id=1, source_target_pairs={{2,0},{0,4},{4,8},{8,12},{12,14},{14,10},{10,6},{6,2},{3,1},{1,5},... | collective-permute-start | bytes 983048 | tf_op jit(solution)/shard_map/ppermute | solution.py:231
  4.9 9.5 %collective-permute-start.7 = (bf16[160,1024]{1,0:T(8,128)(2,1)S(1)}, bf16[160,1024]{1,0:T(8,128)(2,1)S(1)}, u32[]{:S(2)}, u32[]{:S(2)}) collective-permute-start(bf16[160,1024]{1,0:T(8,128)(2,1)S(1)} %shard_map.94.refs_0_), channel_id=1, source_target_pairs={{0,2},{4,0},{8,4},{12,8},{14,12},{10,14},{6,10},{2,6},{1,3},{5,1},... | collective-permute-start | bytes 983048 | tf_op jit(solution)/shard_map/ppermute | solution.py:231
  4.9 18.7 %collective-permute-start.3 = (bf16[640,1280]{1,0:T(8,128)(2,1)S(1)}, bf16[640,1280]{1,0:T(8,128)(2,1)}, u32[]{:S(2)}, u32[]{:S(2)}) collective-permute-start(bf16[640,1280]{1,0:T(8,128)(2,1)S(1)} %copy-done), channel_id=1, source_target_pairs={{0,1},{1,0},{2,3},{3,2},{4,5},{5,4},{6,7},{7,6},{8,9},{9,8},{10,11... | collective-permute-start | bytes 4915208 | tf_op jit(solution)/shard_map/ppermute | solution.py:192
  12.6 3.9 %copy-start.7 = (bf16[160,1024]{1,0:T(8,128)(2,1)}, bf16[160,1024]{1,0:T(8,128)(2,1)S(1)}, u32[]{:S(2)}) copy-start(bf16[160,1024]{1,0:T(8,128)(2,1)S(1)} %collective-permute-done.6.refs_1_) | copy-start | bytes 983044
  12.6 9.0 %collective-permute-start.8 = (bf16[160,1024]{1,0:T(8,128)(2,1)S(1)}, bf16[160,1024]{1,0:T(8,128)(2,1)}, u32[]{:S(2)}, u32[]{:S(2)}) collective-permute-start(bf16[160,1024]{1,0:T(8,128)(2,1)S(1)} %collective-permute-done.6.refs_1_), channel_id=1, source_target_pairs={{2,0},{0,4},{4,8},{8,12},{12,14},{14,10},{10,6},{6,2},{3,1},{1,5},... | collective-permute-start | bytes 983048 | tf_op jit(solution)/shard_map/ppermute | solution.py:231
  14.4 2.1 %copy-start.9 = (bf16[160,1024]{1,0:T(8,128)(2,1)}, bf16[160,1024]{1,0:T(8,128)(2,1)S(1)}, u32[]{:S(2)}) copy-start(bf16[160,1024]{1,0:T(8,128)(2,1)S(1)} %collective-permute-done.7.refs_2_) | copy-start | bytes 983044
  14.4 8.7 %collective-permute-start.9 = (bf16[160,1024]{1,0:T(8,128)(2,1)S(1)}, bf16[160,1024]{1,0:T(8,128)(2,1)}, u32[]{:S(2)}, u32[]{:S(2)}) collective-permute-start(bf16[160,1024]{1,0:T(8,128)(2,1)S(1)} %collective-permute-done.7.refs_2_), channel_id=1, source_target_pairs={{0,2},{4,0},{8,4},{12,8},{14,12},{10,14},{6,10},{2,6},{1,3},{5,1},... | collective-permute-start | bytes 983048 | tf_op jit(solution)/shard_map/ppermute | solution.py:231
  16.5 7.1 %collective-permute-start.2 = (bf16[256,640]{1,0:T(8,128)(2,1)}, bf16[256,640]{1,0:T(8,128)(2,1)}, u32[]{:S(2)}, u32[]{:S(2)}) collective-permute-start(bf16[256,640]{1,0:T(8,128)(2,1)} %shard_map.92.attn_own), channel_id=1, source_target_pairs={{0,1},{1,0},{2,3},{3,2},{4,5},{5,4},{6,7},{7,6},{8,9},{9,8},{10,11... | collective-permute-start | bytes 983048 | tf_op jit(solution)/shard_map/ppermute | solution.py:192
  16.6 15.1 %collective-permute-start = (bf16[272,512]{1,0:T(8,128)(2,1)S(1)}, bf16[272,512]{1,0:T(8,128)(2,1)S(1)}, u32[]{:S(2)}, u32[]{:S(2)}) collective-permute-start(bf16[272,512]{1,0:T(8,128)(2,1)S(1)} %pad_maximum_fusion.own), channel_id=1, source_target_pairs={{0,4},{2,6},{4,8},{6,10},{8,12},{10,14},{1,5},{3,7},{5,9},{7,11},{... | collective-permute-start | bytes 835592 | tf_op jit(solution)/shard_map/ppermute | solution.py:188
  21.6 12.5 %collective-permute-start.10 = (bf16[160,1024]{1,0:T(8,128)(2,1)}, bf16[160,1024]{1,0:T(8,128)(2,1)S(1)}, u32[]{:S(2)}, u32[]{:S(2)}) collective-permute-start(bf16[160,1024]{1,0:T(8,128)(2,1)} %collective-permute-done.8.refs_3_), channel_id=1, source_target_pairs={{2,0},{0,4},{4,8},{8,12},{12,14},{14,10},{10,6},{6,2},{3,1},{1,5},... | collective-permute-start | bytes 983048 | tf_op jit(solution)/shard_map/ppermute | solution.py:231
  23.1 13.4 %collective-permute-start.11 = (bf16[160,1024]{1,0:T(8,128)(2,1)}, bf16[160,1024]{1,0:T(8,128)(2,1)S(1)}, u32[]{:S(2)}, u32[]{:S(2)}) collective-permute-start(bf16[160,1024]{1,0:T(8,128)(2,1)} %collective-permute-done.9.refs_4_), channel_id=1, source_target_pairs={{0,2},{4,0},{8,4},{12,8},{14,12},{10,14},{6,10},{2,6},{1,3},{5,1},... | collective-permute-start | bytes 983048 | tf_op jit(solution)/shard_map/ppermute | solution.py:231
  23.6 8.1 %copy-start.15 = (bf16[2,128,512]{2,1,0:T(8,128)(2,1)S(1)}, bf16[2,128,512]{2,1,0:T(8,128)(2,1)}, u32[]{:S(2)}) copy-start(bf16[2,128,512]{2,1,0:T(8,128)(2,1)} %param.10) | copy-start | bytes 786436
  23.6 9.8 %copy-start.17 = (f32[32]{0:T(128)S(1)}, f32[32]{0:T(128)}, u32[]{:S(2)}) copy-start(f32[32]{0:T(128)} %param.17) | copy-start | bytes 388
  27.4 0.8 %copy-start.12 = (bf16[256,1280]{1,0:T(8,128)(2,1)}, bf16[256,1280]{1,0:T(8,128)(2,1)S(1)}, u32[]{:S(2)}) copy-start(bf16[256,1280]{1,0:T(8,128)(2,1)S(1)} %get-tuple-element.7.norm_own) | copy-start | bytes 1966084
  28.2 17.1 %copy-start.1 = (bf16[128,4096]{1,0:T(8,128)(2,1)S(1)}, bf16[128,4096]{1,0:T(8,128)(2,1)}, u32[]{:S(2)}) copy-start(bf16[128,4096]{1,0:T(8,128)(2,1)} %q.3) | copy-start | bytes 3145732
  28.2 11.9 %collective-permute-start.4 = (bf16[128,1280]{1,0:T(8,128)(2,1)}, bf16[128,1280]{1,0:T(8,128)(2,1)S(1)}, u32[]{:S(2)}, u32[]{:S(2)}) collective-permute-start(bf16[128,1280]{1,0:T(8,128)(2,1)} %get-tuple-element.8), channel_id=1, source_target_pairs={{0,2},{2,4},{4,6},{6,8},{8,10},{10,12},{12,14},{1,3},{3,5},{5,7},{... | collective-permute-start | bytes 983048 | tf_op jit(solution)/shard_map/ppermute | solution.py:188
  31.8 13.5 %collective-permute-start.1 = (bf16[272,512]{1,0:T(8,128)(2,1)S(1)}, bf16[272,512]{1,0:T(8,128)(2,1)S(1)}, u32[]{:S(2)}, u32[]{:S(2)}) collective-permute-start(bf16[272,512]{1,0:T(8,128)(2,1)S(1)} %broadcast_select_fusion), channel_id=1, source_target_pairs={{0,2},{2,0},{4,6},{6,4},{8,10},{10,8},{12,14},{14,12},{1,3},{3,1},... | collective-permute-start | bytes 835592 | tf_op jit(solution)/shard_map/ppermute | solution.py:192
  34.1 13.9 %collective-permute-start.12 = (bf16[80,1024]{1,0:T(8,128)(2,1)S(1)}, bf16[80,1024]{1,0:T(8,128)(2,1)S(1)}, u32[]{:S(2)}, u32[]{:S(2)}) collective-permute-start(bf16[80,1024]{1,0:T(8,128)(2,1)S(1)} %slice.8), channel_id=1, source_target_pairs={{2,0},{0,4},{4,8},{8,12},{12,14},{14,10},{10,6},{6,2},{3,1},{1,5},... | collective-permute-start | bytes 491528 | tf_op jit(solution)/shard_map/ppermute | solution.py:231
  36.5 11.5 %copy-start.6 = (bf16[160,1024]{1,0:T(8,128)(2,1)S(1)}, bf16[160,1024]{1,0:T(8,128)(2,1)}, u32[]{:S(2)}) copy-start(bf16[160,1024]{1,0:T(8,128)(2,1)} %copy-done.5) | copy-start | bytes 983044
  36.5 11.5 %copy-start.8 = (bf16[160,1024]{1,0:T(8,128)(2,1)S(1)}, bf16[160,1024]{1,0:T(8,128)(2,1)}, u32[]{:S(2)}) copy-start(bf16[160,1024]{1,0:T(8,128)(2,1)} %copy-done.7) | copy-start | bytes 983044
  36.5 11.5 %copy-start.10 = (bf16[160,1024]{1,0:T(8,128)(2,1)S(1)}, bf16[160,1024]{1,0:T(8,128)(2,1)}, u32[]{:S(2)}) copy-start(bf16[160,1024]{1,0:T(8,128)(2,1)} %copy-done.9) | copy-start | bytes 983044
  36.5 11.5 %copy-start.11 = (s32[128,2]{0,1:T(2,128)S(1)}, s32[128,2]{0,1:T(2,128)}, u32[]{:S(2)}) copy-start(s32[128,2]{0,1:T(2,128)} %param.12) | copy-start | bytes 3076
  36.6 11.5 %copy-start.13 = (bf16[256,1280]{1,0:T(8,128)(2,1)S(1)}, bf16[256,1280]{1,0:T(8,128)(2,1)}, u32[]{:S(2)}) copy-start(bf16[256,1280]{1,0:T(8,128)(2,1)} %copy-done.12) | copy-start | bytes 1966084
  36.6 11.4 %collective-permute-start.13 = (bf16[80,1024]{1,0:T(8,128)(2,1)S(1)}, bf16[80,1024]{1,0:T(8,128)(2,1)S(1)}, u32[]{:S(2)}, u32[]{:S(2)}) collective-permute-start(bf16[80,1024]{1,0:T(8,128)(2,1)S(1)} %slice.9), channel_id=1, source_target_pairs={{0,2},{4,0},{8,4},{12,8},{14,12},{10,14},{6,10},{2,6},{1,3},{5,1},... | collective-permute-start | bytes 491528 | tf_op jit(solution)/shard_map/ppermute | solution.py:231
  40.1 7.8 %collective-permute-start.5 = (bf16[128,1280]{1,0:T(8,128)(2,1)S(1)}, bf16[128,1280]{1,0:T(8,128)(2,1)S(1)}, u32[]{:S(2)}, u32[]{:S(2)}) collective-permute-start(bf16[128,1280]{1,0:T(8,128)(2,1)S(1)} %collective-permute-done.4.before_mine), channel_id=1, source_target_pairs={{0,1},{1,0},{2,3},{3,2},{4,5},{5,4},{6,7},{7,6},{8,9},{9,8},{10,11... | collective-permute-start | bytes 983048 | tf_op jit(solution)/shard_map/ppermute | solution.py:192

commit v4 on v3

--- a/solution.py
+++ b/solution.py
@@ -35,16 +35,18 @@
     return jnp.sum(jnp.where(at, row, 0.0), axis=1, keepdims=True)
 
 
-def call(kernel, out_shape, args, smem=0, scratch=()):
+def call(kernel, out_shape, args, smem=0, hbm=0, scratch=()):
     many = isinstance(out_shape, (tuple, list))
     vmem = pl.BlockSpec(memory_space=pltpu.VMEM)
+    anywhere = pl.BlockSpec(memory_space=pl.ANY)
     outs = out_shape if many else (out_shape,)
     moved = sum(math.prod(a.shape) * jnp.dtype(a.dtype).itemsize for a in (*args, *outs))
     return pl.pallas_call(
         kernel,
         out_shape=out_shape,
-        in_specs=[pl.BlockSpec(memory_space=pltpu.SMEM)] * smem + [vmem] * (len(args) - smem),
-        out_specs=[vmem] * len(out_shape) if many else vmem,
+        in_specs=[pl.BlockSpec(memory_space=pltpu.SMEM)] * smem + [anywhere] * hbm
+        + [vmem] * (len(args) - smem - hbm),
+        out_specs=[vmem] * len(out_shape) if many else anywhere if hbm else vmem,
         scratch_shapes=list(scratch),
         compiler_params=pltpu.CompilerParams(vmem_limit_bytes=VMEM_LIMIT),
         cost_estimate=pl.CostEstimate(flops=PLANNED_FLOPS, bytes_accessed=moved, transcendentals=0),
@@ -131,23 +133,43 @@
             out[:, j * HEAD_SIZE : (j + 1) * HEAD_SIZE] = o[i * rows : (i + 1) * rows]
 
 
-def cross_kernel(pieces, place, q, self_out, span, gate, norm_own, before_mine, before_other, *refs):
-    weights, out, w, kv = refs[:pieces], refs[pieces], refs[pieces + 1], refs[pieces + 2]
+def image_kernel(pieces, late, place, norm_own, before_mine, before_other, *refs):
+    weights, refs = refs[:pieces], refs[pieces:]
+    total, w = refs[0], refs[-1]
+    for i, piece in enumerate(weights):
+        n = piece.shape[0]
+        w[pl.ds(pl.multiple_of(place[3 + i], ID_ROWS), n), :] = piece[...]
+    first, mine, other = place[1] == 0, before_mine[...], before_other[...]
+    norms = [jnp.where(first, mine, other), jnp.where(first, other, mine), norm_own[...]]
+    norms = jnp.concatenate(norms, axis=0)
+    if late:
+        w[pl.ds(pl.multiple_of(place[2], ID_ROWS), late), :] = jnp.zeros((late, w.shape[1]), BF16)
+        shape = (w.shape[0], late)
+        picks = lax.broadcasted_iota(jnp.int32, shape, 0) == (
+            lax.broadcasted_iota(jnp.int32, shape, 1) + place[2]
+        )
+        refs[1][...] = dot_n(norms, jnp.where(picks, 1.0, 0.0).astype(BF16)).astype(BF16)
+    total[...] = dot_n(norms, w[...])
+
+
+def cross_kernel(seq, q_all, self_all, span, gate, total, *refs):
+    late, (out_all, kv, q, self_out, out, sems) = refs[:-6], refs[-6:]
     rows = q.shape[0]
-    tile = norm_own.shape[0]
-    kv_cols = w.shape[1] // 2
+    tile = total.shape[0] // 2
+    kv_cols = total.shape[1] // 2
     groups = kv_cols // HEAD_SIZE
     ratio = q.shape[1] // HEAD_SIZE // groups
     scale = LOG2E / math.sqrt(HEAD_SIZE)
-    for i, piece in enumerate(weights):
-        n = piece.shape[0]
-        start = place[2 + i]
-        w[pl.ds(pl.multiple_of(start, ID_ROWS), n), :] = piece[...]
-    first, mine, other = place[1] == 0, before_mine[...], before_other[...]
-    norms = [jnp.where(first, mine, other), jnp.where(first, other, mine), norm_own[...]]
-    norms = jnp.concatenate(norms, axis=0)
-    kv[...] = dot_n(norms, w[...]).astype(BF16)
-    this = place[0].astype(F32)
+    fetch_q = pltpu.make_async_copy(q_all, q, sems.at[0])
+    fetch_self = pltpu.make_async_copy(self_all, self_out, sems.at[1])
+    fetch_q.start()
+    fetch_self.start()
+    if late:
+        rest = jnp.concatenate([block[...] for block in late[1:]], axis=0)
+        kv[...] = (total[...] + dot_n(late[0][...], rest)).astype(BF16)
+    else:
+        kv[...] = total[...].astype(BF16)
+    this = seq[0].astype(F32)
     low = column_of(span[0:1, :].astype(F32))
     high = column_of(span[1:2, :].astype(F32))
     see_own = (low <= this) & (this < high)
@@ -161,6 +183,9 @@
         axis=1,
     )
     ones = jnp.ones((2 * tile, HEAD_SIZE), BF16)
+    fetch_q.wait()
+    fetch_self.wait()
+    stores = []
     for g in range(groups):
         keys = kv[:, g * HEAD_SIZE : (g + 1) * HEAD_SIZE]
         values = kv[:, kv_cols + g * HEAD_SIZE : kv_cols + (g + 1) * HEAD_SIZE]
@@ -172,15 +197,11 @@
             o = dot_n(p, values)
             o = o[:, :HEAD_SIZE] * (1.0 / o[:, HEAD_SIZE:])
             out[:, at] = (self_out[:, at] + gate[:, at] * present * o).astype(BF16)
-
-
-def mark_kernel(x, out):
-    out[...] = x[...]
-
-
-def marker(*done):
-    x = after(jnp.zeros((8, LANES), F32), *done)
-    return call(mark_kernel, jax.ShapeDtypeStruct(x.shape, F32), (x,))
+        whole = slice(g * ratio * HEAD_SIZE, (g + 1) * ratio * HEAD_SIZE)
+        stores.append(pltpu.make_async_copy(out.at[:, whole], out_all.at[:, whole], sems.at[2 + g]))
+        stores[-1].start()
+    for store in stores:
+        store.wait()
 
 
 def shifted(block, axis, distance):
@@ -190,10 +211,6 @@
 
 def flipped(block, axis, bits):
     return lax.ppermute(block, axis, [(i, i ^ bits) for i in range(lax.axis_size(axis))])
-
-
-def after(x, *done):
-    return lax.optimization_barrier((x, *done))[0]
 
 
 def per_device(
@@ -265,12 +282,6 @@
     back1 = flipped(jnp.where(even, text, back2), "seq", 1)
     before_mine = shifted(norm_half, "seq", 1)
     before_other = other_core(before_mine)
-    self_out = call(
-        self_kernel,
-        sds(text_query_rows.shape, F32),
-        (seq.reshape(1), text_query_rows, text, back1, back2),
-        smem=1,
-    )
     if rings:
         up, down = [block for block in (step3[0], step3[-1])]
         step4 = around([(0, up[:half]), (1, down[-half:])])
@@ -282,30 +293,42 @@
             for i, block in enumerate(step):
                 first = at(place + (k if i % 2 else n - k)) + i // 2 * (rows // chunks)
                 pieces += [(block, first)]
-        pieces += [(step4[0], at(place + n // 2)), (step4[1], at(place + n // 2) + half)]
+        late, late_at = list(step4), at(place + n // 2)
     else:
         pieces = [(lax.all_gather(w, "seq", axis=0, tiled=True), 0)]
+        late, late_at = [], 0
 
     gate = jnp.repeat(jnp.tanh(cross_gate), HEAD_SIZE)[None, :]
-    place = jnp.stack([seq, core] + [jnp.asarray(p[1], jnp.int32) for p in pieces])
+    place = jnp.stack([seq, core] + [jnp.asarray(p, jnp.int32) for p in (late_at, *[p[1] for p in pieces])])
+    image = [sds((2 * tile_rows, 2 * kv_cols), F32)]
+    if late:
+        image.append(sds((2 * tile_rows, rows), BF16))
+    image = list(call(
+        functools.partial(image_kernel, len(pieces), rows if late else 0),
+        tuple(image),
+        (place, norm, before_mine, before_other, *[p[0] for p in pieces]),
+        smem=1,
+        scratch=(pltpu.VMEM((width, 2 * kv_cols), BF16),),
+    ))
+    turn, image[0] = lax.optimization_barrier((seq.reshape(1), image[0]))
+    self_out = call(
+        self_kernel,
+        sds(text_query_rows.shape, F32),
+        (turn, text_query_rows, text, back1, back2),
+        smem=1,
+    )
     return call(
-        functools.partial(cross_kernel, len(pieces)),
+        cross_kernel,
         sds(text_query_rows.shape, BF16),
-        (
-            place,
-            text_query_rows,
-            self_out,
-            tile_span.T,
-            gate,
-            norm,
-            before_mine,
-            before_other,
-            *[p[0] for p in pieces],
-        ),
+        (seq.reshape(1), text_query_rows, self_out, tile_span.T, gate, *image, *late),
         smem=1,
+        hbm=2,
         scratch=(
-            pltpu.VMEM((width, 2 * kv_cols), BF16),
             pltpu.VMEM((2 * tile_rows, 2 * kv_cols), BF16),
+            pltpu.VMEM(text_query_rows.shape, BF16),
+            pltpu.VMEM(text_query_rows.shape, F32),
+            pltpu.VMEM(text_query_rows.shape, BF16),
+            pltpu.SemaphoreType.DMA((2 + kv_heads,)),
         ),
     )
 

time: 55.1 us -> 54.9 us (level)
  waiting for transfers between devices: 18.1 us -> 10.5 us
  starting transfers between devices: 18.5 us -> 24.5 us
  local copies, waits for them, and re-layouts: 2.23 us -> 3.27 us
    ppermute x4, waiting for transfers between devices: 5.2 us -> 0.01 us  [flipped(): lax.ppermute(block, axis, [(i, i ^ bits) for i in range(lax.axis_size(axi...]
    ppermute x4, starting transfers between devices: 1.67 us -> 5.56 us  [flipped(): lax.ppermute(block, axis, [(i, i ^ bits) for i in range(lax.axis_size(axi...]
    ppermute x8, waiting for transfers between devices: 9.35 us -> 5.57 us  [around(): lax.ppermute(block, 'seq', ways[way])]
    ppermute x8, starting transfers between devices: 9.62 us -> 11.7 us  [around(): lax.ppermute(block, 'seq', ways[way])]
    ppermute x2, waiting for transfers between devices: 3.51 us -> 4.88 us  [shifted(): lax.ppermute(block, axis, [(i, i + distance) for i in range(n - distance)])]
    unnamed x36 -> x22, local copies, waits for them, and re-layouts: 2.04 us -> 3.07 us
    pallas_call x5 -> x6, Pallas kernels: 15.4 us -> 15.9 us  [call(): pl.pallas_call(kernel, out_shape=out_shape, in_specs=[pl.BlockSpec(memory...]
  transfers between devices with their start and end apart: 14 -> 14, of which waited for: 5 -> 3; matrix products, arithmetic and copies ran while one was open for 0% -> 0% of each run, Pallas kernels for 15% -> 19%
where the time goes in v4:
time: 54.9 us; the launch traced here: 54.6 us
  starting transfers between devices  24.5 us (45%)
  Pallas kernels  15.9 us (29%)
  waiting for transfers between devices  10.5 us (19%)
  local copies, waits for them, and re-layouts  3.27 us (6%)
    pallas_call x6, Pallas kernels, call(): pl.pallas_call(kernel, out_shape=out_shape, in_specs=[pl.BlockSpec(memory...  15.9 us
    ppermute x8, starting transfers between devices, around(): lax.ppermute(block, 'seq', ways[way])  11.7 us
    ppermute x2, starting transfers between devices, shifted(): lax.ppermute(block, axis, [(i, i + distance) for i in range(n - distance)])  7.27 us
    ppermute x8, waiting for transfers between devices, around(): lax.ppermute(block, 'seq', ways[way])  5.57 us
    ppermute x4, starting transfers between devices, flipped(): lax.ppermute(block, axis, [(i, i ^ bits) for i in range(lax.axis_size(axi...  5.56 us
    ppermute x2, waiting for transfers between devices, shifted(): lax.ppermute(block, axis, [(i, i + distance) for i in range(n - distance)])  4.88 us
    unnamed x22, local copies, waits for them, and re-layouts  3.07 us
  transfers between devices with their start and end apart: 14, of which 3 were waited for; matrix products, arithmetic and copies ran while one was open for 0% of the time, Pallas kernels for 19%

profile of v4, /device:TPU:0, one launch (start us, length us, event | category | flops | bytes accessed | tf_op | source)
XLA Modules:
  0.0 54.6 jit_solution(5135397988542532783)
XLA Ops:
  0.0 0.0 copy-start
  0.0 0.0 copy-start.2
  0.0 0.0 copy-start.4
  0.0 1.1 %copy-done.4 = bf16[160,2,512]{2,1,0:T(2,128)(2,1)S(1)} copy-done((bf16[160,2,512]{2,1,0:T(2,128)(2,1)S(1)}, bf16[160,2,512]{2,1,0:T(2,128)(2,1)}, u32[]{:S(2)}) %copy-start.4) | copy-done | bytes 327704
  1.1 1.4 %shard_map.93.refs_0_ = bf16[160,1024]{1,0:T(8,128)(2,1)} custom-call(bf16[160,2,512]{2,1,0:T(2,128)(2,1)S(1)} %copy-done.4), custom_call_target="tpu_custom_call" | custom-call | flops 20000000000 | bytes 655360 | tf_op jit(solution)/shard_map/pallas_call | solution.py:44
  2.5 3.0 %collective-permute-start.4 = (bf16[160,1024]{1,0:T(8,128)(2,1)}, bf16[160,1024]{1,0:T(8,128)(2,1)}, u32[]{:S(2)}, u32[]{:S(2)}) collective-permute-start(bf16[160,1024]{1,0:T(8,128)(2,1)} %shard_map.93.refs_0_), channel_id=1, source_target_pairs={{2,0},{0,4},{4,8},{8,12},{12,14},{14,10},{10,6},{6,2},{3,1},{1,5},... | collective-permute-start | bytes 983048 | tf_op jit(solution)/shard_map/ppermute | solution.py:248
  5.6 0.0 collective-permute-start.5
  5.6 0.0 copy-done
  5.6 0.0 collective-permute-start.1
  5.6 0.0 copy-done.2
  5.6 1.9 %shard_map.91.attn_own = bf16[256,640]{1,0:T(8,128)(2,1)} custom-call(bf16[3,256,640]{2,1,0:T(8,128)(2,1)S(1)} %copy-done.2), custom_call_target="tpu_custom_call" | custom-call | flops 20000000000 | bytes 1310720 | tf_op jit(solution)/shard_map/pallas_call | solution.py:44
  7.5 0.5 collective-permute-start
  8.0 5.5 %collective-permute-done.4.refs_1_ = bf16[160,1024]{1,0:T(8,128)(2,1)} collective-permute-done((bf16[160,1024]{1,0:T(8,128)(2,1)}, bf16[160,1024]{1,0:T(8,128)(2,1)}, u32[]{:S(2)}, u32[]{:S(2)}) %collective-permute-start.4) | collective-permute-done | bytes 327712 | tf_op jit(solution)/shard_map/ppermute | solution.py:248
  13.5 1.8 %collective-permute-start.6 = (bf16[160,1024]{1,0:T(8,128)(2,1)}, bf16[160,1024]{1,0:T(8,128)(2,1)}, u32[]{:S(2)}, u32[]{:S(2)}) collective-permute-start(bf16[160,1024]{1,0:T(8,128)(2,1)} %collective-permute-done.4.refs_1_), channel_id=1, source_target_pairs={{2,0},{0,4},{4,8},{8,12},{12,14},{14,10},{10,6},{6,2},{3,1},{1,5},... | collective-permute-start | bytes 983048 | tf_op jit(solution)/shard_map/ppermute | solution.py:248
  15.3 0.0 collective-permute-done.5.refs_2_
  15.3 0.2 collective-permute-start.7
  15.5 0.0 collective-permute-done.attn_other
  15.5 0.0 collective-permute-done.1.w_other
  15.5 0.0 copy-start.3
  15.6 1.1 %copy-done.3 = bf16[256,1280]{1,0:T(8,128)(2,1)S(1)} copy-done((bf16[256,1280]{1,0:T(8,128)(2,1)S(1)}, bf16[256,1280]{1,0:T(8,128)(2,1)}, u32[]{:S(2)}) %copy-start.3) | copy-done | bytes 655384
  16.6 0.0 copy-start.9
  16.6 0.0 copy-start.8
  16.6 0.0 copy-start.10
  16.6 2.4 %shard_map.92 = (bf16[256,1280]{1,0:T(8,128)(2,1)S(1)}, bf16[128,1280]{1,0:T(8,128)(2,1)S(1)}) custom-call(s32[1]{0:T(128)} %bitcast.1.core, bf16[256,1280]{1,0:T(8,128)(2,1)S(1)} %copy-done.3, bf16[256,640]{1,0:T(8,128)(2,1)} %shard_map.91.attn_own, bf16[256,640]{1,0:T(8,128)(2,1)} %collective-permute-done.attn_other, bf16[640,1280]{1,0:T(8,128)(2,1)S(1)} %copy-done, ...), custom_call_target="tpu_custom_call" | custom-call | flops 20000000000 | bytes 5570564 | tf_op jit(solution)/shard_map/pallas_call | solution.py:44
  19.1 0.0 copy-start.6
  19.1 0.8 %copy-done.6 = bf16[256,1280]{1,0:T(8,128)(2,1)} copy-done((bf16[256,1280]{1,0:T(8,128)(2,1)}, bf16[256,1280]{1,0:T(8,128)(2,1)S(1)}, u32[]{:S(2)}) %copy-start.6) | copy-done | bytes 655384
  19.9 0.0 copy-start.7
  19.9 3.8 %collective-permute-start.2 = (bf16[128,1280]{1,0:T(8,128)(2,1)S(1)}, bf16[128,1280]{1,0:T(8,128)(2,1)S(1)}, u32[]{:S(2)}, u32[]{:S(2)}) collective-permute-start(bf16[128,1280]{1,0:T(8,128)(2,1)S(1)} %get-tuple-element.12), channel_id=1, source_target_pairs={{0,2},{2,4},{4,6},{6,8},{8,10},{10,12},{12,14},{1,3},{3,5},{5,7},{... | collective-permute-start | bytes 983048 | tf_op jit(solution)/shard_map/ppermute | solution.py:209
  23.7 0.0 copy-done.9
  23.8 0.0 copy-done.8
  23.8 3.5 %collective-permute-start.10 = (bf16[272,512]{1,0:T(8,128)(2,1)S(1)}, bf16[272,512]{1,0:T(8,128)(2,1)S(1)}, u32[]{:S(2)}, u32[]{:S(2)}) collective-permute-start(bf16[272,512]{1,0:T(8,128)(2,1)S(1)} %pad_maximum_fusion.own), channel_id=1, source_target_pairs={{0,4},{2,6},{4,8},{6,10},{8,12},{10,14},{1,5},{3,7},{5,9},{7,11},{... | collective-permute-start | bytes 835592 | tf_op jit(solution)/shard_map/ppermute | solution.py:209
  27.3 0.0 collective-permute-done.6.refs_3_
  27.3 1.6 %collective-permute-start.8 = (bf16[160,1024]{1,0:T(8,128)(2,1)}, bf16[160,1024]{1,0:T(8,128)(2,1)S(1)}, u32[]{:S(2)}, u32[]{:S(2)}) collective-permute-start(bf16[160,1024]{1,0:T(8,128)(2,1)} %collective-permute-done.6.refs_3_), channel_id=1, source_target_pairs={{2,0},{0,4},{4,8},{8,12},{12,14},{14,10},{10,6},{6,2},{3,1},{1,5},... | collective-permute-start | bytes 983048 | tf_op jit(solution)/shard_map/ppermute | solution.py:248
  28.9 0.0 collective-permute-done.7.refs_4_
  28.9 0.5 collective-permute-start.9
  29.4 1.7 %collective-permute-done.2.before_mine = bf16[128,1280]{1,0:T(8,128)(2,1)S(1)} collective-permute-done((bf16[128,1280]{1,0:T(8,128)(2,1)S(1)}, bf16[128,1280]{1,0:T(8,128)(2,1)S(1)}, u32[]{:S(2)}, u32[]{:S(2)}) %collective-permute-start.2) | collective-permute-done | bytes 327712 | tf_op jit(solution)/shard_map/ppermute | solution.py:209
  31.1 0.0 collective-permute-start.3
  31.1 0.0 copy-done.10
  31.1 0.1 stack.40.place
  31.2 3.2 %collective-permute-done.10.back2 = bf16[272,512]{1,0:T(8,128)(2,1)S(1)} collective-permute-done((bf16[272,512]{1,0:T(8,128)(2,1)S(1)}, bf16[272,512]{1,0:T(8,128)(2,1)S(1)}, u32[]{:S(2)}, u32[]{:S(2)}) %collective-permute-start.10) | collective-permute-done | bytes 278560 | tf_op jit(solution)/shard_map/ppermute | solution.py:209
  34.4 0.1 broadcast_select_fusion
  34.5 5.1 %collective-permute-start.11 = (bf16[272,512]{1,0:T(8,128)(2,1)S(1)}, bf16[272,512]{1,0:T(8,128)(2,1)S(1)}, u32[]{:S(2)}, u32[]{:S(2)}) collective-permute-start(bf16[272,512]{1,0:T(8,128)(2,1)S(1)} %broadcast_select_fusion), channel_id=1, source_target_pairs={{0,2},{2,0},{4,6},{6,4},{8,10},{10,8},{12,14},{14,12},{1,3},{3,1},... | collective-permute-start | bytes 835592 | tf_op jit(solution)/shard_map/ppermute | solution.py:213
  39.5 0.0 collective-permute-done.8.refs_5_
  39.5 2.5 %collective-permute-start.12 = (bf16[80,1024]{1,0:T(8,128)(2,1)S(1)}, bf16[80,1024]{1,0:T(8,128)(2,1)S(1)}, u32[]{:S(2)}, u32[]{:S(2)}) collective-permute-start(bf16[80,1024]{1,0:T(8,128)(2,1)S(1)} %slice.8), channel_id=1, source_target_pairs={{2,0},{0,4},{4,8},{8,12},{12,14},{14,10},{10,6},{6,2},{3,1},{1,5},... | collective-permute-start | bytes 491528 | tf_op jit(solution)/shard_map/ppermute | solution.py:248
  42.1 0.0 collective-permute-done.9.refs_6_
  42.1 2.0 %collective-permute-start.13 = (bf16[80,1024]{1,0:T(8,128)(2,1)S(1)}, bf16[80,1024]{1,0:T(8,128)(2,1)S(1)}, u32[]{:S(2)}, u32[]{:S(2)}) collective-permute-start(bf16[80,1024]{1,0:T(8,128)(2,1)S(1)} %slice.9), channel_id=1, source_target_pairs={{0,2},{4,0},{8,4},{12,8},{14,12},{10,14},{6,10},{2,6},{1,3},{5,1},... | collective-permute-start | bytes 491528 | tf_op jit(solution)/shard_map/ppermute | solution.py:248
  44.1 0.0 collective-permute-done.3.before_other
  44.1 0.0 copy-done.7
  44.1 0.0 copy-start.1
  44.1 3.5 %shard_map.94 = (f32[512,1024]{1,0:T(8,128)S(1)}, bf16[512,160]{1,0:T(8,128)(2,1)S(1)}) custom-call(s32[10]{0:T(128)S(1)} %stack.40.place, bf16[256,1280]{1,0:T(8,128)(2,1)S(1)} %copy-done.7, bf16[128,1280]{1,0:T(8,128)(2,1)S(1)} %collective-permute-done.2.before_mine, bf16[128,1280]{1,0:T(8,128)(2,1)S(1)} %collective-permute-done.3.before_other, ...), custom_call_target="tpu_custom_call" | custom-call | flops 20000000000 | bytes 5865512 | tf_op jit(solution)/shard_map/pallas_call | solution.py:44
  47.6 0.0 copy-start.5
  47.7 0.0 collective-permute-done.11.back1
  47.7 0.0 copy-done.1
  47.7 2.6 %shard_map.95.self_all = f32[128,4096]{1,0:T(8,128)S(1)} custom-call(s32[1]{0:T(128)} %bitcast.seq, bf16[128,4096]{1,0:T(8,128)(2,1)S(1)} %copy-done.1, bf16[272,512]{1,0:T(8,128)(2,1)S(1)} %pad_maximum_fusion.own, bf16[272,512]{1,0:T(8,128)(2,1)S(1)} %collective-permute-done.11.back1, bf16[272,512]{1,0:T(8,128)(2,1)S(1)} %collective-permute-done.10.back2), custom_call_target="tpu_custom_call" | custom-call | flops 20000000000 | bytes 3981316 | tf_op jit(solution)/shard_map/pallas_call | solution.py:44
  50.3 0.0 collective-permute-done.12.refs_1_
  50.3 0.0 collective-permute-done.13.refs_2_
  50.3 0.1 broadcast_in_dim.4
  50.4 0.0 copy-done.5
  50.4 4.1 %shard_map.96 = bf16[128,4096]{1,0:T(8,128)(2,1)} custom-call(s32[1]{0:T(128)} %bitcast.seq, bf16[128,4096]{1,0:T(8,128)(2,1)S(1)} %copy-done.1, f32[128,4096]{1,0:T(8,128)S(1)} %shard_map.95.self_all, s32[2,128]{1,0:T(2,128)S(1)} %bitcast.14, f32[1,4096]{1,0:T(1,128)S(1)} %bitcast.13, f32[512,1024]{1,0:T(8,128)S(1)} %get-tuple-element.15.total, ...), custom_call_target="tpu_custom_call" | custom-call | flops 20000000000 | bytes 6800388 | tf_op jit(solution)/shard_map/pallas_call | solution.py:44
  (7 shorter events, 0.1 us)
Async XLA Ops:
  0.0 5.6 %copy-start = (bf16[640,1280]{1,0:T(8,128)(2,1)S(1)}, bf16[640,1280]{1,0:T(8,128)(2,1)}, u32[]{:S(2)}) copy-start(bf16[640,1280]{1,0:T(8,128)(2,1)} %w_own.1) | copy-start | bytes 4915204
  0.0 5.6 %copy-start.2 = (bf16[3,256,640]{2,1,0:T(8,128)(2,1)S(1)}, bf16[3,256,640]{2,1,0:T(8,128)(2,1)}, u32[]{:S(2)}) copy-start(bf16[3,256,640]{2,1,0:T(8,128)(2,1)} %qkv.1) | copy-start | bytes 2949124
  0.0 1.1 %copy-start.4 = (bf16[160,2,512]{2,1,0:T(2,128)(2,1)S(1)}, bf16[160,2,512]{2,1,0:T(2,128)(2,1)}, u32[]{:S(2)}) copy-start(bf16[160,2,512]{2,1,0:T(2,128)(2,1)} %w.1) | copy-start | bytes 983044
  2.5 11.0 %collective-permute-start.4 = (bf16[160,1024]{1,0:T(8,128)(2,1)}, bf16[160,1024]{1,0:T(8,128)(2,1)}, u32[]{:S(2)}, u32[]{:S(2)}) collective-permute-start(bf16[160,1024]{1,0:T(8,128)(2,1)} %shard_map.93.refs_0_), channel_id=1, source_target_pairs={{2,0},{0,4},{4,8},{8,12},{12,14},{14,10},{10,6},{6,2},{3,1},{1,5},... | collective-permute-start | bytes 983048 | tf_op jit(solution)/shard_map/ppermute | solution.py:248
  5.6 9.8 %collective-permute-start.5 = (bf16[160,1024]{1,0:T(8,128)(2,1)}, bf16[160,1024]{1,0:T(8,128)(2,1)}, u32[]{:S(2)}, u32[]{:S(2)}) collective-permute-start(bf16[160,1024]{1,0:T(8,128)(2,1)} %shard_map.93.refs_0_), channel_id=1, source_target_pairs={{0,2},{4,0},{8,4},{12,8},{14,12},{10,14},{6,10},{2,6},{1,3},{5,1},... | collective-permute-start | bytes 983048 | tf_op jit(solution)/shard_map/ppermute | solution.py:248
  5.6 10.0 %collective-permute-start.1 = (bf16[640,1280]{1,0:T(8,128)(2,1)S(1)}, bf16[640,1280]{1,0:T(8,128)(2,1)S(1)}, u32[]{:S(2)}, u32[]{:S(2)}) collective-permute-start(bf16[640,1280]{1,0:T(8,128)(2,1)S(1)} %copy-done), channel_id=1, source_target_pairs={{0,1},{1,0},{2,3},{3,2},{4,5},{5,4},{6,7},{7,6},{8,9},{9,8},{10,11... | collective-permute-start | bytes 4915208 | tf_op jit(solution)/shard_map/ppermute | solution.py:213
  7.5 8.1 %collective-permute-start = (bf16[256,640]{1,0:T(8,128)(2,1)}, bf16[256,640]{1,0:T(8,128)(2,1)}, u32[]{:S(2)}, u32[]{:S(2)}) collective-permute-start(bf16[256,640]{1,0:T(8,128)(2,1)} %shard_map.91.attn_own), channel_id=1, source_target_pairs={{0,1},{1,0},{2,3},{3,2},{4,5},{5,4},{6,7},{7,6},{8,9},{9,8},{10,11... | collective-permute-start | bytes 983048 | tf_op jit(solution)/shard_map/ppermute | solution.py:213
  13.5 13.8 %collective-permute-start.6 = (bf16[160,1024]{1,0:T(8,128)(2,1)}, bf16[160,1024]{1,0:T(8,128)(2,1)}, u32[]{:S(2)}, u32[]{:S(2)}) collective-permute-start(bf16[160,1024]{1,0:T(8,128)(2,1)} %collective-permute-done.4.refs_1_), channel_id=1, source_target_pairs={{2,0},{0,4},{4,8},{8,12},{12,14},{14,10},{10,6},{6,2},{3,1},{1,5},... | collective-permute-start | bytes 983048 | tf_op jit(solution)/shard_map/ppermute | solution.py:248
  15.3 13.6 %collective-permute-start.7 = (bf16[160,1024]{1,0:T(8,128)(2,1)}, bf16[160,1024]{1,0:T(8,128)(2,1)}, u32[]{:S(2)}, u32[]{:S(2)}) collective-permute-start(bf16[160,1024]{1,0:T(8,128)(2,1)} %collective-permute-done.5.refs_2_), channel_id=1, source_target_pairs={{0,2},{4,0},{8,4},{12,8},{14,12},{10,14},{6,10},{2,6},{1,3},{5,1},... | collective-permute-start | bytes 983048 | tf_op jit(solution)/shard_map/ppermute | solution.py:248
  15.5 1.1 %copy-start.3 = (bf16[256,1280]{1,0:T(8,128)(2,1)S(1)}, bf16[256,1280]{1,0:T(8,128)(2,1)}, u32[]{:S(2)}) copy-start(bf16[256,1280]{1,0:T(8,128)(2,1)} %hidden.1) | copy-start | bytes 1966084
  16.6 7.1 %copy-start.9 = (s32[128]{0:T(128)S(1)}, s32[128]{0:T(128)}, u32[]{:S(2)}) copy-start(s32[128]{0:T(128)} %param.11) | copy-start | bytes 1540
  16.6 7.1 %copy-start.8 = (bf16[2,128,512]{2,1,0:T(8,128)(2,1)S(1)}, bf16[2,128,512]{2,1,0:T(8,128)(2,1)}, u32[]{:S(2)}) copy-start(bf16[2,128,512]{2,1,0:T(8,128)(2,1)} %param.10) | copy-start | bytes 786436
  16.6 14.5 %copy-start.10 = (f32[32]{0:T(128)S(1)}, f32[32]{0:T(128)}, u32[]{:S(2)}) copy-start(f32[32]{0:T(128)} %param.17) | copy-start | bytes 388
  19.1 0.8 %copy-start.6 = (bf16[256,1280]{1,0:T(8,128)(2,1)}, bf16[256,1280]{1,0:T(8,128)(2,1)S(1)}, u32[]{:S(2)}) copy-start(bf16[256,1280]{1,0:T(8,128)(2,1)S(1)} %get-tuple-element.11.norm_own) | copy-start | bytes 1966084
  19.9 24.2 %copy-start.7 = (bf16[256,1280]{1,0:T(8,128)(2,1)S(1)}, bf16[256,1280]{1,0:T(8,128)(2,1)}, u32[]{:S(2)}) copy-start(bf16[256,1280]{1,0:T(8,128)(2,1)} %copy-done.6) | copy-start | bytes 1966084
  19.9 11.2 %collective-permute-start.2 = (bf16[128,1280]{1,0:T(8,128)(2,1)S(1)}, bf16[128,1280]{1,0:T(8,128)(2,1)S(1)}, u32[]{:S(2)}, u32[]{:S(2)}) collective-permute-start(bf16[128,1280]{1,0:T(8,128)(2,1)S(1)} %get-tuple-element.12), channel_id=1, source_target_pairs={{0,2},{2,4},{4,6},{6,8},{8,10},{10,12},{12,14},{1,3},{3,5},{5,7},{... | collective-permute-start | bytes 983048 | tf_op jit(solution)/shard_map/ppermute | solution.py:209
  23.8 10.6 %collective-permute-start.10 = (bf16[272,512]{1,0:T(8,128)(2,1)S(1)}, bf16[272,512]{1,0:T(8,128)(2,1)S(1)}, u32[]{:S(2)}, u32[]{:S(2)}) collective-permute-start(bf16[272,512]{1,0:T(8,128)(2,1)S(1)} %pad_maximum_fusion.own), channel_id=1, source_target_pairs={{0,4},{2,6},{4,8},{6,10},{8,12},{10,14},{1,5},{3,7},{5,9},{7,11},{... | collective-permute-start | bytes 835592 | tf_op jit(solution)/shard_map/ppermute | solution.py:209
  27.3 12.2 %collective-permute-start.8 = (bf16[160,1024]{1,0:T(8,128)(2,1)}, bf16[160,1024]{1,0:T(8,128)(2,1)S(1)}, u32[]{:S(2)}, u32[]{:S(2)}) collective-permute-start(bf16[160,1024]{1,0:T(8,128)(2,1)} %collective-permute-done.6.refs_3_), channel_id=1, source_target_pairs={{2,0},{0,4},{4,8},{8,12},{12,14},{14,10},{10,6},{6,2},{3,1},{1,5},... | collective-permute-start | bytes 983048 | tf_op jit(solution)/shard_map/ppermute | solution.py:248
  28.9 13.1 %collective-permute-start.9 = (bf16[160,1024]{1,0:T(8,128)(2,1)}, bf16[160,1024]{1,0:T(8,128)(2,1)S(1)}, u32[]{:S(2)}, u32[]{:S(2)}) collective-permute-start(bf16[160,1024]{1,0:T(8,128)(2,1)} %collective-permute-done.7.refs_4_), channel_id=1, source_target_pairs={{0,2},{4,0},{8,4},{12,8},{14,12},{10,14},{6,10},{2,6},{1,3},{5,1},... | collective-permute-start | bytes 983048 | tf_op jit(solution)/shard_map/ppermute | solution.py:248
  31.1 13.0 %collective-permute-start.3 = (bf16[128,1280]{1,0:T(8,128)(2,1)S(1)}, bf16[128,1280]{1,0:T(8,128)(2,1)S(1)}, u32[]{:S(2)}, u32[]{:S(2)}) collective-permute-start(bf16[128,1280]{1,0:T(8,128)(2,1)S(1)} %collective-permute-done.2.before_mine), channel_id=1, source_target_pairs={{0,1},{1,0},{2,3},{3,2},{4,5},{5,4},{6,7},{7,6},{8,9},{9,8},{10,11... | collective-permute-start | bytes 983048 | tf_op jit(solution)/shard_map/ppermute | solution.py:213
  34.5 13.2 %collective-permute-start.11 = (bf16[272,512]{1,0:T(8,128)(2,1)S(1)}, bf16[272,512]{1,0:T(8,128)(2,1)S(1)}, u32[]{:S(2)}, u32[]{:S(2)}) collective-permute-start(bf16[272,512]{1,0:T(8,128)(2,1)S(1)} %broadcast_select_fusion), channel_id=1, source_target_pairs={{0,2},{2,0},{4,6},{6,4},{8,10},{10,8},{12,14},{14,12},{1,3},{3,1},... | collective-permute-start | bytes 835592 | tf_op jit(solution)/shard_map/ppermute | solution.py:213
  39.5 10.7 %collective-permute-start.12 = (bf16[80,1024]{1,0:T(8,128)(2,1)S(1)}, bf16[80,1024]{1,0:T(8,128)(2,1)S(1)}, u32[]{:S(2)}, u32[]{:S(2)}) collective-permute-start(bf16[80,1024]{1,0:T(8,128)(2,1)S(1)} %slice.8), channel_id=1, source_target_pairs={{2,0},{0,4},{4,8},{8,12},{12,14},{14,10},{10,6},{6,2},{3,1},{1,5},... | collective-permute-start | bytes 491528 | tf_op jit(solution)/shard_map/ppermute | solution.py:248
  42.1 8.2 %collective-permute-start.13 = (bf16[80,1024]{1,0:T(8,128)(2,1)S(1)}, bf16[80,1024]{1,0:T(8,128)(2,1)S(1)}, u32[]{:S(2)}, u32[]{:S(2)}) collective-permute-start(bf16[80,1024]{1,0:T(8,128)(2,1)S(1)} %slice.9), channel_id=1, source_target_pairs={{0,2},{4,0},{8,4},{12,8},{14,12},{10,14},{6,10},{2,6},{1,3},{5,1},... | collective-permute-start | bytes 491528 | tf_op jit(solution)/shard_map/ppermute | solution.py:248
  44.1 3.5 %copy-start.1 = (bf16[128,4096]{1,0:T(8,128)(2,1)S(1)}, bf16[128,4096]{1,0:T(8,128)(2,1)}, u32[]{:S(2)}) copy-start(bf16[128,4096]{1,0:T(8,128)(2,1)} %q_all.1) | copy-start | bytes 3145732
  47.6 2.7 %copy-start.5 = (s32[128,2]{0,1:T(2,128)S(1)}, s32[128,2]{0,1:T(2,128)}, u32[]{:S(2)}) copy-start(s32[128,2]{0,1:T(2,128)} %param.12) | copy-start | bytes 3076

commit v5 on v4

--- a/solution.py
+++ b/solution.py
@@ -35,7 +35,7 @@
     return jnp.sum(jnp.where(at, row, 0.0), axis=1, keepdims=True)
 
 
-def call(kernel, out_shape, args, smem=0, hbm=0, scratch=()):
+def call(kernel, out_shape, args, smem=0, stored=False, scratch=()):
     many = isinstance(out_shape, (tuple, list))
     vmem = pl.BlockSpec(memory_space=pltpu.VMEM)
     anywhere = pl.BlockSpec(memory_space=pl.ANY)
@@ -44,9 +44,8 @@
     return pl.pallas_call(
         kernel,
         out_shape=out_shape,
-        in_specs=[pl.BlockSpec(memory_space=pltpu.SMEM)] * smem + [anywhere] * hbm
-        + [vmem] * (len(args) - smem - hbm),
-        out_specs=[vmem] * len(out_shape) if many else anywhere if hbm else vmem,
+        in_specs=[pl.BlockSpec(memory_space=pltpu.SMEM)] * smem + [vmem] * (len(args) - smem),
+        out_specs=[vmem] * len(out_shape) if many else anywhere if stored else vmem,
         scratch_shapes=list(scratch),
         compiler_params=pltpu.CompilerParams(vmem_limit_bytes=VMEM_LIMIT),
         cost_estimate=pl.CostEstimate(flops=PLANNED_FLOPS, bytes_accessed=moved, transcendentals=0),
@@ -152,18 +151,14 @@
     total[...] = dot_n(norms, w[...])
 
 
-def cross_kernel(seq, q_all, self_all, span, gate, total, *refs):
-    late, (out_all, kv, q, self_out, out, sems) = refs[:-6], refs[-6:]
+def cross_kernel(seq, q, self_out, span, gate, total, *refs):
+    late, (out_all, kv, out, sems) = refs[:-4], refs[-4:]
     rows = q.shape[0]
     tile = total.shape[0] // 2
     kv_cols = total.shape[1] // 2
     groups = kv_cols // HEAD_SIZE
     ratio = q.shape[1] // HEAD_SIZE // groups
     scale = LOG2E / math.sqrt(HEAD_SIZE)
-    fetch_q = pltpu.make_async_copy(q_all, q, sems.at[0])
-    fetch_self = pltpu.make_async_copy(self_all, self_out, sems.at[1])
-    fetch_q.start()
-    fetch_self.start()
     if late:
         rest = jnp.concatenate([block[...] for block in late[1:]], axis=0)
         kv[...] = (total[...] + dot_n(late[0][...], rest)).astype(BF16)
@@ -183,8 +178,6 @@
         axis=1,
     )
     ones = jnp.ones((2 * tile, HEAD_SIZE), BF16)
-    fetch_q.wait()
-    fetch_self.wait()
     stores = []
     for g in range(groups):
         keys = kv[:, g * HEAD_SIZE : (g + 1) * HEAD_SIZE]
@@ -198,7 +191,7 @@
             o = o[:, :HEAD_SIZE] * (1.0 / o[:, HEAD_SIZE:])
             out[:, at] = (self_out[:, at] + gate[:, at] * present * o).astype(BF16)
         whole = slice(g * ratio * HEAD_SIZE, (g + 1) * ratio * HEAD_SIZE)
-        stores.append(pltpu.make_async_copy(out.at[:, whole], out_all.at[:, whole], sems.at[2 + g]))
+        stores.append(pltpu.make_async_copy(out.at[:, whole], out_all.at[:, whole], sems.at[g]))
         stores[-1].start()
     for store in stores:
         store.wait()
@@ -322,13 +315,11 @@
         sds(text_query_rows.shape, BF16),
         (seq.reshape(1), text_query_rows, self_out, tile_span.T, gate, *image, *late),
         smem=1,
-        hbm=2,
+        stored=True,
         scratch=(
             pltpu.VMEM((2 * tile_rows, 2 * kv_cols), BF16),
             pltpu.VMEM(text_query_rows.shape, BF16),
-            pltpu.VMEM(text_query_rows.shape, F32),
-            pltpu.VMEM(text_query_rows.shape, BF16),
-            pltpu.SemaphoreType.DMA((2 + kv_heads,)),
+            pltpu.SemaphoreType.DMA((kv_heads,)),
         ),
     )
 

time: 54.9 us -> 54.3 us (0.989)
  no operation moved by 1% of the time
where the time goes in v5:
time: 54.3 us; the launch traced here: 54 us
  starting transfers between devices  24.4 us (45%)
  Pallas kernels  15.7 us (29%)
  waiting for transfers between devices  10.5 us (19%)
  local copies, waits for them, and re-layouts  3.27 us (6%)
    pallas_call x6, Pallas kernels, call(): pl.pallas_call(kernel, out_shape=out_shape, in_specs=[pl.BlockSpec(memory...  15.7 us
    ppermute x8, starting transfers between devices, around(): lax.ppermute(block, 'seq', ways[way])  11.5 us
    ppermute x2, starting transfers between devices, shifted(): lax.ppermute(block, axis, [(i, i + distance) for i in range(n - distance)])  7.27 us
    ppermute x8, waiting for transfers between devices, around(): lax.ppermute(block, 'seq', ways[way])  5.57 us
    ppermute x4, starting transfers between devices, flipped(): lax.ppermute(block, axis, [(i, i ^ bits) for i in range(lax.axis_size(axi...  5.56 us
    ppermute x2, waiting for transfers between devices, shifted(): lax.ppermute(block, axis, [(i, i + distance) for i in range(n - distance)])  4.88 us
    unnamed x22, local copies, waits for them, and re-layouts  3.07 us
  transfers between devices with their start and end apart: 14, of which 3 were waited for; matrix products, arithmetic and copies ran while one was open for 0% of the time, Pallas kernels for 19%

profile of v5, /device:TPU:0, one launch (start us, length us, event | category | flops | bytes accessed | tf_op | source)
XLA Modules:
  0.0 54.0 jit_solution(7991988584211652233)
XLA Ops:
  0.0 0.0 copy-start
  0.0 0.0 copy-start.2
  0.0 0.0 copy-start.4
  0.0 1.1 %copy-done.4 = bf16[160,2,512]{2,1,0:T(2,128)(2,1)S(1)} copy-done((bf16[160,2,512]{2,1,0:T(2,128)(2,1)S(1)}, bf16[160,2,512]{2,1,0:T(2,128)(2,1)}, u32[]{:S(2)}) %copy-start.4) | copy-done | bytes 327704
  1.1 1.4 %shard_map.93.refs_0_ = bf16[160,1024]{1,0:T(8,128)(2,1)} custom-call(bf16[160,2,512]{2,1,0:T(2,128)(2,1)S(1)} %copy-done.4), custom_call_target="tpu_custom_call" | custom-call | flops 20000000000 | bytes 655360 | tf_op jit(solution)/shard_map/pallas_call | solution.py:44
  2.5 3.0 %collective-permute-start.4 = (bf16[160,1024]{1,0:T(8,128)(2,1)}, bf16[160,1024]{1,0:T(8,128)(2,1)}, u32[]{:S(2)}, u32[]{:S(2)}) collective-permute-start(bf16[160,1024]{1,0:T(8,128)(2,1)} %shard_map.93.refs_0_), channel_id=1, source_target_pairs={{2,0},{0,4},{4,8},{8,12},{12,14},{14,10},{10,6},{6,2},{3,1},{1,5},... | collective-permute-start | bytes 983048 | tf_op jit(solution)/shard_map/ppermute | solution.py:241
  5.6 0.0 collective-permute-start.5
  5.6 0.0 copy-done
  5.6 0.0 collective-permute-start.1
  5.6 0.0 copy-done.2
  5.6 1.9 %shard_map.91.attn_own = bf16[256,640]{1,0:T(8,128)(2,1)} custom-call(bf16[3,256,640]{2,1,0:T(8,128)(2,1)S(1)} %copy-done.2), custom_call_target="tpu_custom_call" | custom-call | flops 20000000000 | bytes 1310720 | tf_op jit(solution)/shard_map/pallas_call | solution.py:44
  7.5 0.5 collective-permute-start
  8.0 5.5 %collective-permute-done.4.refs_1_ = bf16[160,1024]{1,0:T(8,128)(2,1)} collective-permute-done((bf16[160,1024]{1,0:T(8,128)(2,1)}, bf16[160,1024]{1,0:T(8,128)(2,1)}, u32[]{:S(2)}, u32[]{:S(2)}) %collective-permute-start.4) | collective-permute-done | bytes 327712 | tf_op jit(solution)/shard_map/ppermute | solution.py:241
  13.5 1.8 %collective-permute-start.6 = (bf16[160,1024]{1,0:T(8,128)(2,1)}, bf16[160,1024]{1,0:T(8,128)(2,1)}, u32[]{:S(2)}, u32[]{:S(2)}) collective-permute-start(bf16[160,1024]{1,0:T(8,128)(2,1)} %collective-permute-done.4.refs_1_), channel_id=1, source_target_pairs={{2,0},{0,4},{4,8},{8,12},{12,14},{14,10},{10,6},{6,2},{3,1},{1,5},... | collective-permute-start | bytes 983048 | tf_op jit(solution)/shard_map/ppermute | solution.py:241
  15.3 0.0 collective-permute-done.5.refs_2_
  15.3 0.2 collective-permute-start.7
  15.5 0.0 collective-permute-done.attn_other
  15.5 0.0 collective-permute-done.1.w_other
  15.5 0.0 copy-start.3
  15.6 1.1 %copy-done.3 = bf16[256,1280]{1,0:T(8,128)(2,1)S(1)} copy-done((bf16[256,1280]{1,0:T(8,128)(2,1)S(1)}, bf16[256,1280]{1,0:T(8,128)(2,1)}, u32[]{:S(2)}) %copy-start.3) | copy-done | bytes 655384
  16.6 0.0 copy-start.9
  16.6 0.0 copy-start.8
  16.6 0.0 copy-start.10
  16.6 2.4 %shard_map.92 = (bf16[256,1280]{1,0:T(8,128)(2,1)S(1)}, bf16[128,1280]{1,0:T(8,128)(2,1)S(1)}) custom-call(s32[1]{0:T(128)} %bitcast.1.core, bf16[256,1280]{1,0:T(8,128)(2,1)S(1)} %copy-done.3, bf16[256,640]{1,0:T(8,128)(2,1)} %shard_map.91.attn_own, bf16[256,640]{1,0:T(8,128)(2,1)} %collective-permute-done.attn_other, bf16[640,1280]{1,0:T(8,128)(2,1)S(1)} %copy-done, ...), custom_call_target="tpu_custom_call" | custom-call | flops 20000000000 | bytes 5570564 | tf_op jit(solution)/shard_map/pallas_call | solution.py:44
  19.1 0.0 copy-start.6
  19.1 0.8 %copy-done.6 = bf16[256,1280]{1,0:T(8,128)(2,1)} copy-done((bf16[256,1280]{1,0:T(8,128)(2,1)}, bf16[256,1280]{1,0:T(8,128)(2,1)S(1)}, u32[]{:S(2)}) %copy-start.6) | copy-done | bytes 655384
  19.9 0.0 copy-start.7
  19.9 3.8 %collective-permute-start.2 = (bf16[128,1280]{1,0:T(8,128)(2,1)S(1)}, bf16[128,1280]{1,0:T(8,128)(2,1)S(1)}, u32[]{:S(2)}, u32[]{:S(2)}) collective-permute-start(bf16[128,1280]{1,0:T(8,128)(2,1)S(1)} %get-tuple-element.12), channel_id=1, source_target_pairs={{0,2},{2,4},{4,6},{6,8},{8,10},{10,12},{12,14},{1,3},{3,5},{5,7},{... | collective-permute-start | bytes 983048 | tf_op jit(solution)/shard_map/ppermute | solution.py:202
  23.7 0.0 copy-done.9
  23.8 0.0 copy-done.8
  23.8 3.5 %collective-permute-start.10 = (bf16[272,512]{1,0:T(8,128)(2,1)S(1)}, bf16[272,512]{1,0:T(8,128)(2,1)S(1)}, u32[]{:S(2)}, u32[]{:S(2)}) collective-permute-start(bf16[272,512]{1,0:T(8,128)(2,1)S(1)} %pad_maximum_fusion.own), channel_id=1, source_target_pairs={{0,4},{2,6},{4,8},{6,10},{8,12},{10,14},{1,5},{3,7},{5,9},{7,11},{... | collective-permute-start | bytes 835592 | tf_op jit(solution)/shard_map/ppermute | solution.py:202
  27.3 0.0 collective-permute-done.6.refs_3_
  27.3 1.6 %collective-permute-start.8 = (bf16[160,1024]{1,0:T(8,128)(2,1)}, bf16[160,1024]{1,0:T(8,128)(2,1)S(1)}, u32[]{:S(2)}, u32[]{:S(2)}) collective-permute-start(bf16[160,1024]{1,0:T(8,128)(2,1)} %collective-permute-done.6.refs_3_), channel_id=1, source_target_pairs={{2,0},{0,4},{4,8},{8,12},{12,14},{14,10},{10,6},{6,2},{3,1},{1,5},... | collective-permute-start | bytes 983048 | tf_op jit(solution)/shard_map/ppermute | solution.py:241
  28.9 0.0 collective-permute-done.7.refs_4_
  28.9 0.5 collective-permute-start.9
  29.4 1.7 %collective-permute-done.2.before_mine = bf16[128,1280]{1,0:T(8,128)(2,1)S(1)} collective-permute-done((bf16[128,1280]{1,0:T(8,128)(2,1)S(1)}, bf16[128,1280]{1,0:T(8,128)(2,1)S(1)}, u32[]{:S(2)}, u32[]{:S(2)}) %collective-permute-start.2) | collective-permute-done | bytes 327712 | tf_op jit(solution)/shard_map/ppermute | solution.py:202
  31.1 0.0 collective-permute-start.3
  31.1 0.0 copy-done.10
  31.1 0.1 stack.40.place
  31.2 3.2 %collective-permute-done.10.back2 = bf16[272,512]{1,0:T(8,128)(2,1)S(1)} collective-permute-done((bf16[272,512]{1,0:T(8,128)(2,1)S(1)}, bf16[272,512]{1,0:T(8,128)(2,1)S(1)}, u32[]{:S(2)}, u32[]{:S(2)}) %collective-permute-start.10) | collective-permute-done | bytes 278560 | tf_op jit(solution)/shard_map/ppermute | solution.py:202
  34.4 0.1 broadcast_select_fusion
  34.5 5.1 %collective-permute-start.11 = (bf16[272,512]{1,0:T(8,128)(2,1)S(1)}, bf16[272,512]{1,0:T(8,128)(2,1)S(1)}, u32[]{:S(2)}, u32[]{:S(2)}) collective-permute-start(bf16[272,512]{1,0:T(8,128)(2,1)S(1)} %broadcast_select_fusion), channel_id=1, source_target_pairs={{0,2},{2,0},{4,6},{6,4},{8,10},{10,8},{12,14},{14,12},{1,3},{3,1},... | collective-permute-start | bytes 835592 | tf_op jit(solution)/shard_map/ppermute | solution.py:206
  39.5 0.0 collective-permute-done.8.refs_5_
  39.5 2.5 %collective-permute-start.12 = (bf16[80,1024]{1,0:T(8,128)(2,1)S(1)}, bf16[80,1024]{1,0:T(8,128)(2,1)S(1)}, u32[]{:S(2)}, u32[]{:S(2)}) collective-permute-start(bf16[80,1024]{1,0:T(8,128)(2,1)S(1)} %slice.8), channel_id=1, source_target_pairs={{2,0},{0,4},{4,8},{8,12},{12,14},{14,10},{10,6},{6,2},{3,1},{1,5},... | collective-permute-start | bytes 491528 | tf_op jit(solution)/shard_map/ppermute | solution.py:241
  42.1 0.0 collective-permute-done.9.refs_6_
  42.1 1.9 %collective-permute-start.13 = (bf16[80,1024]{1,0:T(8,128)(2,1)S(1)}, bf16[80,1024]{1,0:T(8,128)(2,1)S(1)}, u32[]{:S(2)}, u32[]{:S(2)}) collective-permute-start(bf16[80,1024]{1,0:T(8,128)(2,1)S(1)} %slice.9), channel_id=1, source_target_pairs={{0,2},{4,0},{8,4},{12,8},{14,12},{10,14},{6,10},{2,6},{1,3},{5,1},... | collective-permute-start | bytes 491528 | tf_op jit(solution)/shard_map/ppermute | solution.py:241
  43.9 0.0 collective-permute-done.3.before_other
  43.9 0.0 copy-done.7
  43.9 0.0 copy-start.1
  43.9 3.5 %shard_map.94 = (f32[512,1024]{1,0:T(8,128)S(1)}, bf16[512,160]{1,0:T(8,128)(2,1)S(1)}) custom-call(s32[10]{0:T(128)S(1)} %stack.40.place, bf16[256,1280]{1,0:T(8,128)(2,1)S(1)} %copy-done.7, bf16[128,1280]{1,0:T(8,128)(2,1)S(1)} %collective-permute-done.2.before_mine, bf16[128,1280]{1,0:T(8,128)(2,1)S(1)} %collective-permute-done.3.before_other, ...), custom_call_target="tpu_custom_call" | custom-call | flops 20000000000 | bytes 5865512 | tf_op jit(solution)/shard_map/pallas_call | solution.py:44
  47.5 0.0 copy-start.5
  47.5 0.0 collective-permute-done.11.back1
  47.5 0.0 copy-done.1
  47.5 2.6 %shard_map.95.self_out = f32[128,4096]{1,0:T(8,128)S(1)} custom-call(s32[1]{0:T(128)} %bitcast.seq, bf16[128,4096]{1,0:T(8,128)(2,1)S(1)} %copy-done.1, bf16[272,512]{1,0:T(8,128)(2,1)S(1)} %pad_maximum_fusion.own, bf16[272,512]{1,0:T(8,128)(2,1)S(1)} %collective-permute-done.11.back1, bf16[272,512]{1,0:T(8,128)(2,1)S(1)} %collective-permute-done.10.back2), custom_call_target="tpu_custom_call" | custom-call | flops 20000000000 | bytes 3981316 | tf_op jit(solution)/shard_map/pallas_call | solution.py:44
  50.1 0.0 collective-permute-done.12.refs_1_
  50.1 0.0 collective-permute-done.13.refs_2_
  50.1 0.1 broadcast_in_dim.4
  50.2 0.0 copy-done.5
  50.2 3.8 %shard_map.96 = bf16[128,4096]{1,0:T(8,128)(2,1)} custom-call(s32[1]{0:T(128)} %bitcast.seq, bf16[128,4096]{1,0:T(8,128)(2,1)S(1)} %copy-done.1, f32[128,4096]{1,0:T(8,128)S(1)} %shard_map.95.self_out, s32[2,128]{1,0:T(2,128)S(1)} %bitcast.14, f32[1,4096]{1,0:T(1,128)S(1)} %bitcast.13, f32[512,1024]{1,0:T(8,128)S(1)} %get-tuple-element.15.total, ...), custom_call_target="tpu_custom_call" | custom-call | flops 20000000000 | bytes 6800388 | tf_op jit(solution)/shard_map/pallas_call | solution.py:44
  (7 shorter events, 0.1 us)
Async XLA Ops:
  0.0 5.6 %copy-start = (bf16[640,1280]{1,0:T(8,128)(2,1)S(1)}, bf16[640,1280]{1,0:T(8,128)(2,1)}, u32[]{:S(2)}) copy-start(bf16[640,1280]{1,0:T(8,128)(2,1)} %w_own.1) | copy-start | bytes 4915204
  0.0 5.6 %copy-start.2 = (bf16[3,256,640]{2,1,0:T(8,128)(2,1)S(1)}, bf16[3,256,640]{2,1,0:T(8,128)(2,1)}, u32[]{:S(2)}) copy-start(bf16[3,256,640]{2,1,0:T(8,128)(2,1)} %qkv.1) | copy-start | bytes 2949124
  0.0 1.1 %copy-start.4 = (bf16[160,2,512]{2,1,0:T(2,128)(2,1)S(1)}, bf16[160,2,512]{2,1,0:T(2,128)(2,1)}, u32[]{:S(2)}) copy-start(bf16[160,2,512]{2,1,0:T(2,128)(2,1)} %w.1) | copy-start | bytes 983044
  2.5 11.0 %collective-permute-start.4 = (bf16[160,1024]{1,0:T(8,128)(2,1)}, bf16[160,1024]{1,0:T(8,128)(2,1)}, u32[]{:S(2)}, u32[]{:S(2)}) collective-permute-start(bf16[160,1024]{1,0:T(8,128)(2,1)} %shard_map.93.refs_0_), channel_id=1, source_target_pairs={{2,0},{0,4},{4,8},{8,12},{12,14},{14,10},{10,6},{6,2},{3,1},{1,5},... | collective-permute-start | bytes 983048 | tf_op jit(solution)/shard_map/ppermute | solution.py:241
  5.6 9.8 %collective-permute-start.5 = (bf16[160,1024]{1,0:T(8,128)(2,1)}, bf16[160,1024]{1,0:T(8,128)(2,1)}, u32[]{:S(2)}, u32[]{:S(2)}) collective-permute-start(bf16[160,1024]{1,0:T(8,128)(2,1)} %shard_map.93.refs_0_), channel_id=1, source_target_pairs={{0,2},{4,0},{8,4},{12,8},{14,12},{10,14},{6,10},{2,6},{1,3},{5,1},... | collective-permute-start | bytes 983048 | tf_op jit(solution)/shard_map/ppermute | solution.py:241
  5.6 10.0 %collective-permute-start.1 = (bf16[640,1280]{1,0:T(8,128)(2,1)S(1)}, bf16[640,1280]{1,0:T(8,128)(2,1)S(1)}, u32[]{:S(2)}, u32[]{:S(2)}) collective-permute-start(bf16[640,1280]{1,0:T(8,128)(2,1)S(1)} %copy-done), channel_id=1, source_target_pairs={{0,1},{1,0},{2,3},{3,2},{4,5},{5,4},{6,7},{7,6},{8,9},{9,8},{10,11... | collective-permute-start | bytes 4915208 | tf_op jit(solution)/shard_map/ppermute | solution.py:206
  7.5 8.1 %collective-permute-start = (bf16[256,640]{1,0:T(8,128)(2,1)}, bf16[256,640]{1,0:T(8,128)(2,1)}, u32[]{:S(2)}, u32[]{:S(2)}) collective-permute-start(bf16[256,640]{1,0:T(8,128)(2,1)} %shard_map.91.attn_own), channel_id=1, source_target_pairs={{0,1},{1,0},{2,3},{3,2},{4,5},{5,4},{6,7},{7,6},{8,9},{9,8},{10,11... | collective-permute-start | bytes 983048 | tf_op jit(solution)/shard_map/ppermute | solution.py:206
  13.5 13.8 %collective-permute-start.6 = (bf16[160,1024]{1,0:T(8,128)(2,1)}, bf16[160,1024]{1,0:T(8,128)(2,1)}, u32[]{:S(2)}, u32[]{:S(2)}) collective-permute-start(bf16[160,1024]{1,0:T(8,128)(2,1)} %collective-permute-done.4.refs_1_), channel_id=1, source_target_pairs={{2,0},{0,4},{4,8},{8,12},{12,14},{14,10},{10,6},{6,2},{3,1},{1,5},... | collective-permute-start | bytes 983048 | tf_op jit(solution)/shard_map/ppermute | solution.py:241
  15.3 13.6 %collective-permute-start.7 = (bf16[160,1024]{1,0:T(8,128)(2,1)}, bf16[160,1024]{1,0:T(8,128)(2,1)}, u32[]{:S(2)}, u32[]{:S(2)}) collective-permute-start(bf16[160,1024]{1,0:T(8,128)(2,1)} %collective-permute-done.5.refs_2_), channel_id=1, source_target_pairs={{0,2},{4,0},{8,4},{12,8},{14,12},{10,14},{6,10},{2,6},{1,3},{5,1},... | collective-permute-start | bytes 983048 | tf_op jit(solution)/shard_map/ppermute | solution.py:241
  15.5 1.1 %copy-start.3 = (bf16[256,1280]{1,0:T(8,128)(2,1)S(1)}, bf16[256,1280]{1,0:T(8,128)(2,1)}, u32[]{:S(2)}) copy-start(bf16[256,1280]{1,0:T(8,128)(2,1)} %hidden.1) | copy-start | bytes 1966084
  16.6 7.1 %copy-start.9 = (s32[128]{0:T(128)S(1)}, s32[128]{0:T(128)}, u32[]{:S(2)}) copy-start(s32[128]{0:T(128)} %param.11) | copy-start | bytes 1540
  16.6 7.1 %copy-start.8 = (bf16[2,128,512]{2,1,0:T(8,128)(2,1)S(1)}, bf16[2,128,512]{2,1,0:T(8,128)(2,1)}, u32[]{:S(2)}) copy-start(bf16[2,128,512]{2,1,0:T(8,128)(2,1)} %param.10) | copy-start | bytes 786436
  16.6 14.5 %copy-start.10 = (f32[32]{0:T(128)S(1)}, f32[32]{0:T(128)}, u32[]{:S(2)}) copy-start(f32[32]{0:T(128)} %param.17) | copy-start | bytes 388
  19.1 0.8 %copy-start.6 = (bf16[256,1280]{1,0:T(8,128)(2,1)}, bf16[256,1280]{1,0:T(8,128)(2,1)S(1)}, u32[]{:S(2)}) copy-start(bf16[256,1280]{1,0:T(8,128)(2,1)S(1)} %get-tuple-element.11.norm_own) | copy-start | bytes 1966084
  19.9 24.0 %copy-start.7 = (bf16[256,1280]{1,0:T(8,128)(2,1)S(1)}, bf16[256,1280]{1,0:T(8,128)(2,1)}, u32[]{:S(2)}) copy-start(bf16[256,1280]{1,0:T(8,128)(2,1)} %copy-done.6) | copy-start | bytes 1966084
  19.9 11.2 %collective-permute-start.2 = (bf16[128,1280]{1,0:T(8,128)(2,1)S(1)}, bf16[128,1280]{1,0:T(8,128)(2,1)S(1)}, u32[]{:S(2)}, u32[]{:S(2)}) collective-permute-start(bf16[128,1280]{1,0:T(8,128)(2,1)S(1)} %get-tuple-element.12), channel_id=1, source_target_pairs={{0,2},{2,4},{4,6},{6,8},{8,10},{10,12},{12,14},{1,3},{3,5},{5,7},{... | collective-permute-start | bytes 983048 | tf_op jit(solution)/shard_map/ppermute | solution.py:202
  23.8 10.6 %collective-permute-start.10 = (bf16[272,512]{1,0:T(8,128)(2,1)S(1)}, bf16[272,512]{1,0:T(8,128)(2,1)S(1)}, u32[]{:S(2)}, u32[]{:S(2)}) collective-permute-start(bf16[272,512]{1,0:T(8,128)(2,1)S(1)} %pad_maximum_fusion.own), channel_id=1, source_target_pairs={{0,4},{2,6},{4,8},{6,10},{8,12},{10,14},{1,5},{3,7},{5,9},{7,11},{... | collective-permute-start | bytes 835592 | tf_op jit(solution)/shard_map/ppermute | solution.py:202
  27.3 12.2 %collective-permute-start.8 = (bf16[160,1024]{1,0:T(8,128)(2,1)}, bf16[160,1024]{1,0:T(8,128)(2,1)S(1)}, u32[]{:S(2)}, u32[]{:S(2)}) collective-permute-start(bf16[160,1024]{1,0:T(8,128)(2,1)} %collective-permute-done.6.refs_3_), channel_id=1, source_target_pairs={{2,0},{0,4},{4,8},{8,12},{12,14},{14,10},{10,6},{6,2},{3,1},{1,5},... | collective-permute-start | bytes 983048 | tf_op jit(solution)/shard_map/ppermute | solution.py:241
  28.9 13.1 %collective-permute-start.9 = (bf16[160,1024]{1,0:T(8,128)(2,1)}, bf16[160,1024]{1,0:T(8,128)(2,1)S(1)}, u32[]{:S(2)}, u32[]{:S(2)}) collective-permute-start(bf16[160,1024]{1,0:T(8,128)(2,1)} %collective-permute-done.7.refs_4_), channel_id=1, source_target_pairs={{0,2},{4,0},{8,4},{12,8},{14,12},{10,14},{6,10},{2,6},{1,3},{5,1},... | collective-permute-start | bytes 983048 | tf_op jit(solution)/shard_map/ppermute | solution.py:241
  31.1 12.8 %collective-permute-start.3 = (bf16[128,1280]{1,0:T(8,128)(2,1)S(1)}, bf16[128,1280]{1,0:T(8,128)(2,1)S(1)}, u32[]{:S(2)}, u32[]{:S(2)}) collective-permute-start(bf16[128,1280]{1,0:T(8,128)(2,1)S(1)} %collective-permute-done.2.before_mine), channel_id=1, source_target_pairs={{0,1},{1,0},{2,3},{3,2},{4,5},{5,4},{6,7},{7,6},{8,9},{9,8},{10,11... | collective-permute-start | bytes 983048 | tf_op jit(solution)/shard_map/ppermute | solution.py:206
  34.5 13.0 %collective-permute-start.11 = (bf16[272,512]{1,0:T(8,128)(2,1)S(1)}, bf16[272,512]{1,0:T(8,128)(2,1)S(1)}, u32[]{:S(2)}, u32[]{:S(2)}) collective-permute-start(bf16[272,512]{1,0:T(8,128)(2,1)S(1)} %broadcast_select_fusion), channel_id=1, source_target_pairs={{0,2},{2,0},{4,6},{6,4},{8,10},{10,8},{12,14},{14,12},{1,3},{3,1},... | collective-permute-start | bytes 835592 | tf_op jit(solution)/shard_map/ppermute | solution.py:206
  39.5 10.6 %collective-permute-start.12 = (bf16[80,1024]{1,0:T(8,128)(2,1)S(1)}, bf16[80,1024]{1,0:T(8,128)(2,1)S(1)}, u32[]{:S(2)}, u32[]{:S(2)}) collective-permute-start(bf16[80,1024]{1,0:T(8,128)(2,1)S(1)} %slice.8), channel_id=1, source_target_pairs={{2,0},{0,4},{4,8},{8,12},{12,14},{14,10},{10,6},{6,2},{3,1},{1,5},... | collective-permute-start | bytes 491528 | tf_op jit(solution)/shard_map/ppermute | solution.py:241
  42.1 8.0 %collective-permute-start.13 = (bf16[80,1024]{1,0:T(8,128)(2,1)S(1)}, bf16[80,1024]{1,0:T(8,128)(2,1)S(1)}, u32[]{:S(2)}, u32[]{:S(2)}) collective-permute-start(bf16[80,1024]{1,0:T(8,128)(2,1)S(1)} %slice.9), channel_id=1, source_target_pairs={{0,2},{4,0},{8,4},{12,8},{14,12},{10,14},{6,10},{2,6},{1,3},{5,1},... | collective-permute-start | bytes 491528 | tf_op jit(solution)/shard_map/ppermute | solution.py:241
  43.9 3.5 %copy-start.1 = (bf16[128,4096]{1,0:T(8,128)(2,1)S(1)}, bf16[128,4096]{1,0:T(8,128)(2,1)}, u32[]{:S(2)}) copy-start(bf16[128,4096]{1,0:T(8,128)(2,1)} %q.3) | copy-start | bytes 3145732
  47.5 2.7 %copy-start.5 = (s32[128,2]{0,1:T(2,128)S(1)}, s32[128,2]{0,1:T(2,128)}, u32[]{:S(2)}) copy-start(s32[128,2]{0,1:T(2,128)} %param.12) | copy-start | bytes 3076

commit v6 on v5

--- a/solution.py
+++ b/solution.py
@@ -94,13 +94,6 @@
     half[...] = out[pl.ds(pl.multiple_of(core[0] * n, n), n), :]
 
 
-def stacked_queries(q, group, ratio):
-    first = group * ratio * HEAD_SIZE
-    return jnp.concatenate(
-        [q[:, first + i * HEAD_SIZE : first + (i + 1) * HEAD_SIZE] for i in range(ratio)], axis=0
-    )
-
-
 def self_kernel(seq, q, own, back1, back2, out):
     rows = q.shape[0]
     groups = own.shape[1] // HEAD_SIZE
@@ -117,19 +110,18 @@
         (ids[2] == own_ids) & (k <= t),
     ]
     bias = jnp.concatenate([jnp.where(m, 0.0, NEG) for m in ok], axis=1)
-    bias = jnp.concatenate([bias] * ratio, axis=0)
     ones = jnp.ones((len(blocks) * rows, HEAD_SIZE), BF16)
     for g in range(groups):
         cols = slice(g * HEAD_SIZE, (g + 1) * HEAD_SIZE)
         keys = jnp.concatenate([b[0:rows, cols] for b in blocks], axis=0)
         values = jnp.concatenate([b[rows : 2 * rows, cols] for b in blocks], axis=0)
-        s = dot_t(stacked_queries(q, g, ratio), keys) + bias
-        p = jnp.exp2((s - jnp.max(s, axis=1, keepdims=True)) * scale).astype(BF16)
-        o = dot_n(p, jnp.concatenate([values, ones], axis=1))
-        o = o[:, :HEAD_SIZE] * (1.0 / o[:, HEAD_SIZE:])
+        values = jnp.concatenate([values, ones], axis=1)
         for i in range(ratio):
-            j = g * ratio + i
-            out[:, j * HEAD_SIZE : (j + 1) * HEAD_SIZE] = o[i * rows : (i + 1) * rows]
+            at = slice((g * ratio + i) * HEAD_SIZE, (g * ratio + i + 1) * HEAD_SIZE)
+            s = dot_t(q[:, at], keys) + bias
+            p = jnp.exp2((s - jnp.max(s, axis=1, keepdims=True)) * scale).astype(BF16)
+            o = dot_n(p, values)
+            out[:, at] = o[:, :HEAD_SIZE] * (1.0 / o[:, HEAD_SIZE:])
 
 
 def image_kernel(pieces, late, place, norm_own, before_mine, before_other, *refs):

time: 54.3 us -> 54.5 us (level)
  transfers between devices with their start and end apart: 14 -> 14, of which waited for: 3 -> 3; matrix products, arithmetic and copies ran while one was open for 0% -> 0% of each run, Pallas kernels for 19% -> 20%
where the time goes in v6:
time: 54.5 us; the launch traced here: 54.2 us
  starting transfers between devices  24.4 us (45%)
  Pallas kernels  15.9 us (29%)
  waiting for transfers between devices  10.5 us (19%)
  local copies, waits for them, and re-layouts  3.27 us (6%)
    pallas_call x6, Pallas kernels, call(): pl.pallas_call(kernel, out_shape=out_shape, in_specs=[pl.BlockSpec(memory...  15.9 us
    ppermute x8, starting transfers between devices, around(): lax.ppermute(block, 'seq', ways[way])  11.5 us
    ppermute x2, starting transfers between devices, shifted(): lax.ppermute(block, axis, [(i, i + distance) for i in range(n - distance)])  7.27 us
    ppermute x8, waiting for transfers between devices, around(): lax.ppermute(block, 'seq', ways[way])  5.57 us
    ppermute x4, starting transfers between devices, flipped(): lax.ppermute(block, axis, [(i, i ^ bits) for i in range(lax.axis_size(axi...  5.56 us
    ppermute x2, waiting for transfers between devices, shifted(): lax.ppermute(block, axis, [(i, i + distance) for i in range(n - distance)])  4.88 us
    unnamed x22, local copies, waits for them, and re-layouts  3.07 us
  transfers between devices with their start and end apart: 14, of which 3 were waited for; matrix products, arithmetic and copies ran while one was open for 0% of the time, Pallas kernels for 20%

profile of v6, /device:TPU:0, one launch (start us, length us, event | category | flops | bytes accessed | tf_op | source)
XLA Modules:
  0.0 54.2 jit_solution(11301835116821007104)
XLA Ops:
  0.0 0.0 copy-start
  0.0 0.0 copy-start.2
  0.0 0.0 copy-start.4
  0.0 1.1 %copy-done.4 = bf16[160,2,512]{2,1,0:T(2,128)(2,1)S(1)} copy-done((bf16[160,2,512]{2,1,0:T(2,128)(2,1)S(1)}, bf16[160,2,512]{2,1,0:T(2,128)(2,1)}, u32[]{:S(2)}) %copy-start.4) | copy-done | bytes 327704
  1.1 1.4 %shard_map.93.refs_0_ = bf16[160,1024]{1,0:T(8,128)(2,1)} custom-call(bf16[160,2,512]{2,1,0:T(2,128)(2,1)S(1)} %copy-done.4), custom_call_target="tpu_custom_call" | custom-call | flops 20000000000 | bytes 655360 | tf_op jit(solution)/shard_map/pallas_call | solution.py:44
  2.5 3.0 %collective-permute-start.4 = (bf16[160,1024]{1,0:T(8,128)(2,1)}, bf16[160,1024]{1,0:T(8,128)(2,1)}, u32[]{:S(2)}, u32[]{:S(2)}) collective-permute-start(bf16[160,1024]{1,0:T(8,128)(2,1)} %shard_map.93.refs_0_), channel_id=1, source_target_pairs={{2,0},{0,4},{4,8},{8,12},{12,14},{14,10},{10,6},{6,2},{3,1},{1,5},... | collective-permute-start | bytes 983048 | tf_op jit(solution)/shard_map/ppermute | solution.py:233
  5.6 0.0 collective-permute-start.5
  5.6 0.0 copy-done
  5.6 0.0 collective-permute-start.1
  5.6 0.0 copy-done.2
  5.6 1.9 %shard_map.91.attn_own = bf16[256,640]{1,0:T(8,128)(2,1)} custom-call(bf16[3,256,640]{2,1,0:T(8,128)(2,1)S(1)} %copy-done.2), custom_call_target="tpu_custom_call" | custom-call | flops 20000000000 | bytes 1310720 | tf_op jit(solution)/shard_map/pallas_call | solution.py:44
  7.5 0.5 collective-permute-start
  8.0 5.5 %collective-permute-done.4.refs_1_ = bf16[160,1024]{1,0:T(8,128)(2,1)} collective-permute-done((bf16[160,1024]{1,0:T(8,128)(2,1)}, bf16[160,1024]{1,0:T(8,128)(2,1)}, u32[]{:S(2)}, u32[]{:S(2)}) %collective-permute-start.4) | collective-permute-done | bytes 327712 | tf_op jit(solution)/shard_map/ppermute | solution.py:233
  13.5 1.8 %collective-permute-start.6 = (bf16[160,1024]{1,0:T(8,128)(2,1)}, bf16[160,1024]{1,0:T(8,128)(2,1)}, u32[]{:S(2)}, u32[]{:S(2)}) collective-permute-start(bf16[160,1024]{1,0:T(8,128)(2,1)} %collective-permute-done.4.refs_1_), channel_id=1, source_target_pairs={{2,0},{0,4},{4,8},{8,12},{12,14},{14,10},{10,6},{6,2},{3,1},{1,5},... | collective-permute-start | bytes 983048 | tf_op jit(solution)/shard_map/ppermute | solution.py:233
  15.3 0.0 collective-permute-done.5.refs_2_
  15.3 0.2 collective-permute-start.7
  15.5 0.0 collective-permute-done.attn_other
  15.5 0.0 collective-permute-done.1.w_other
  15.5 0.0 copy-start.3
  15.6 1.1 %copy-done.3 = bf16[256,1280]{1,0:T(8,128)(2,1)S(1)} copy-done((bf16[256,1280]{1,0:T(8,128)(2,1)S(1)}, bf16[256,1280]{1,0:T(8,128)(2,1)}, u32[]{:S(2)}) %copy-start.3) | copy-done | bytes 655384
  16.6 0.0 copy-start.9
  16.6 0.0 copy-start.8
  16.6 0.0 copy-start.10
  16.6 2.4 %shard_map.92 = (bf16[256,1280]{1,0:T(8,128)(2,1)S(1)}, bf16[128,1280]{1,0:T(8,128)(2,1)S(1)}) custom-call(s32[1]{0:T(128)} %bitcast.1.core, bf16[256,1280]{1,0:T(8,128)(2,1)S(1)} %copy-done.3, bf16[256,640]{1,0:T(8,128)(2,1)} %shard_map.91.attn_own, bf16[256,640]{1,0:T(8,128)(2,1)} %collective-permute-done.attn_other, bf16[640,1280]{1,0:T(8,128)(2,1)S(1)} %copy-done, ...), custom_call_target="tpu_custom_call" | custom-call | flops 20000000000 | bytes 5570564 | tf_op jit(solution)/shard_map/pallas_call | solution.py:44
  19.1 0.0 copy-start.6
  19.1 0.8 %copy-done.6 = bf16[256,1280]{1,0:T(8,128)(2,1)} copy-done((bf16[256,1280]{1,0:T(8,128)(2,1)}, bf16[256,1280]{1,0:T(8,128)(2,1)S(1)}, u32[]{:S(2)}) %copy-start.6) | copy-done | bytes 655384
  19.9 0.0 copy-start.7
  19.9 3.8 %collective-permute-start.2 = (bf16[128,1280]{1,0:T(8,128)(2,1)S(1)}, bf16[128,1280]{1,0:T(8,128)(2,1)S(1)}, u32[]{:S(2)}, u32[]{:S(2)}) collective-permute-start(bf16[128,1280]{1,0:T(8,128)(2,1)S(1)} %get-tuple-element.12), channel_id=1, source_target_pairs={{0,2},{2,4},{4,6},{6,8},{8,10},{10,12},{12,14},{1,3},{3,5},{5,7},{... | collective-permute-start | bytes 983048 | tf_op jit(solution)/shard_map/ppermute | solution.py:194
  23.7 0.0 copy-done.9
  23.8 0.0 copy-done.8
  23.8 3.5 %collective-permute-start.10 = (bf16[272,512]{1,0:T(8,128)(2,1)S(1)}, bf16[272,512]{1,0:T(8,128)(2,1)S(1)}, u32[]{:S(2)}, u32[]{:S(2)}) collective-permute-start(bf16[272,512]{1,0:T(8,128)(2,1)S(1)} %pad_maximum_fusion.own), channel_id=1, source_target_pairs={{0,4},{2,6},{4,8},{6,10},{8,12},{10,14},{1,5},{3,7},{5,9},{7,11},{... | collective-permute-start | bytes 835592 | tf_op jit(solution)/shard_map/ppermute | solution.py:194
  27.3 0.0 collective-permute-done.6.refs_3_
  27.3 1.6 %collective-permute-start.8 = (bf16[160,1024]{1,0:T(8,128)(2,1)}, bf16[160,1024]{1,0:T(8,128)(2,1)S(1)}, u32[]{:S(2)}, u32[]{:S(2)}) collective-permute-start(bf16[160,1024]{1,0:T(8,128)(2,1)} %collective-permute-done.6.refs_3_), channel_id=1, source_target_pairs={{2,0},{0,4},{4,8},{8,12},{12,14},{14,10},{10,6},{6,2},{3,1},{1,5},... | collective-permute-start | bytes 983048 | tf_op jit(solution)/shard_map/ppermute | solution.py:233
  28.9 0.0 collective-permute-done.7.refs_4_
  28.9 0.5 collective-permute-start.9
  29.4 1.7 %collective-permute-done.2.before_mine = bf16[128,1280]{1,0:T(8,128)(2,1)S(1)} collective-permute-done((bf16[128,1280]{1,0:T(8,128)(2,1)S(1)}, bf16[128,1280]{1,0:T(8,128)(2,1)S(1)}, u32[]{:S(2)}, u32[]{:S(2)}) %collective-permute-start.2) | collective-permute-done | bytes 327712 | tf_op jit(solution)/shard_map/ppermute | solution.py:194
  31.1 0.0 collective-permute-start.3
  31.1 0.0 copy-done.10
  31.1 0.1 stack.40.place
  31.2 3.2 %collective-permute-done.10.back2 = bf16[272,512]{1,0:T(8,128)(2,1)S(1)} collective-permute-done((bf16[272,512]{1,0:T(8,128)(2,1)S(1)}, bf16[272,512]{1,0:T(8,128)(2,1)S(1)}, u32[]{:S(2)}, u32[]{:S(2)}) %collective-permute-start.10) | collective-permute-done | bytes 278560 | tf_op jit(solution)/shard_map/ppermute | solution.py:194
  34.4 0.1 broadcast_select_fusion
  34.5 5.1 %collective-permute-start.11 = (bf16[272,512]{1,0:T(8,128)(2,1)S(1)}, bf16[272,512]{1,0:T(8,128)(2,1)S(1)}, u32[]{:S(2)}, u32[]{:S(2)}) collective-permute-start(bf16[272,512]{1,0:T(8,128)(2,1)S(1)} %broadcast_select_fusion), channel_id=1, source_target_pairs={{0,2},{2,0},{4,6},{6,4},{8,10},{10,8},{12,14},{14,12},{1,3},{3,1},... | collective-permute-start | bytes 835592 | tf_op jit(solution)/shard_map/ppermute | solution.py:198
  39.5 0.0 collective-permute-done.8.refs_5_
  39.5 2.5 %collective-permute-start.12 = (bf16[80,1024]{1,0:T(8,128)(2,1)S(1)}, bf16[80,1024]{1,0:T(8,128)(2,1)S(1)}, u32[]{:S(2)}, u32[]{:S(2)}) collective-permute-start(bf16[80,1024]{1,0:T(8,128)(2,1)S(1)} %slice.8), channel_id=1, source_target_pairs={{2,0},{0,4},{4,8},{8,12},{12,14},{14,10},{10,6},{6,2},{3,1},{1,5},... | collective-permute-start | bytes 491528 | tf_op jit(solution)/shard_map/ppermute | solution.py:233
  42.1 0.0 collective-permute-done.9.refs_6_
  42.1 1.9 %collective-permute-start.13 = (bf16[80,1024]{1,0:T(8,128)(2,1)S(1)}, bf16[80,1024]{1,0:T(8,128)(2,1)S(1)}, u32[]{:S(2)}, u32[]{:S(2)}) collective-permute-start(bf16[80,1024]{1,0:T(8,128)(2,1)S(1)} %slice.9), channel_id=1, source_target_pairs={{0,2},{4,0},{8,4},{12,8},{14,12},{10,14},{6,10},{2,6},{1,3},{5,1},... | collective-permute-start | bytes 491528 | tf_op jit(solution)/shard_map/ppermute | solution.py:233
  43.9 0.0 collective-permute-done.3.before_other
  43.9 0.0 copy-done.7
  43.9 0.0 copy-start.1
  43.9 3.5 %shard_map.94 = (f32[512,1024]{1,0:T(8,128)S(1)}, bf16[512,160]{1,0:T(8,128)(2,1)S(1)}) custom-call(s32[10]{0:T(128)S(1)} %stack.40.place, bf16[256,1280]{1,0:T(8,128)(2,1)S(1)} %copy-done.7, bf16[128,1280]{1,0:T(8,128)(2,1)S(1)} %collective-permute-done.2.before_mine, bf16[128,1280]{1,0:T(8,128)(2,1)S(1)} %collective-permute-done.3.before_other, ...), custom_call_target="tpu_custom_call" | custom-call | flops 20000000000 | bytes 5865512 | tf_op jit(solution)/shard_map/pallas_call | solution.py:44
  47.5 0.0 copy-start.5
  47.5 0.0 collective-permute-done.11.back1
  47.5 0.0 copy-done.1
  47.5 2.8 %shard_map.95.self_out = f32[128,4096]{1,0:T(8,128)S(1)} custom-call(s32[1]{0:T(128)} %bitcast.seq, bf16[128,4096]{1,0:T(8,128)(2,1)S(1)} %copy-done.1, bf16[272,512]{1,0:T(8,128)(2,1)S(1)} %pad_maximum_fusion.own, bf16[272,512]{1,0:T(8,128)(2,1)S(1)} %collective-permute-done.11.back1, bf16[272,512]{1,0:T(8,128)(2,1)S(1)} %collective-permute-done.10.back2), custom_call_target="tpu_custom_call" | custom-call | flops 20000000000 | bytes 3981316 | tf_op jit(solution)/shard_map/pallas_call | solution.py:44
  50.3 0.0 collective-permute-done.12.refs_1_
  50.3 0.0 collective-permute-done.13.refs_2_
  50.3 0.1 broadcast_in_dim.4
  50.4 0.0 copy-done.5
  50.4 3.8 %shard_map.96 = bf16[128,4096]{1,0:T(8,128)(2,1)} custom-call(s32[1]{0:T(128)} %bitcast.seq, bf16[128,4096]{1,0:T(8,128)(2,1)S(1)} %copy-done.1, f32[128,4096]{1,0:T(8,128)S(1)} %shard_map.95.self_out, s32[2,128]{1,0:T(2,128)S(1)} %bitcast.14, f32[1,4096]{1,0:T(1,128)S(1)} %bitcast.13, f32[512,1024]{1,0:T(8,128)S(1)} %get-tuple-element.15.total, ...), custom_call_target="tpu_custom_call" | custom-call | flops 20000000000 | bytes 6800388 | tf_op jit(solution)/shard_map/pallas_call | solution.py:44
  (7 shorter events, 0.1 us)
Async XLA Ops:
  0.0 5.6 %copy-start = (bf16[640,1280]{1,0:T(8,128)(2,1)S(1)}, bf16[640,1280]{1,0:T(8,128)(2,1)}, u32[]{:S(2)}) copy-start(bf16[640,1280]{1,0:T(8,128)(2,1)} %w_own.1) | copy-start | bytes 4915204
  0.0 5.6 %copy-start.2 = (bf16[3,256,640]{2,1,0:T(8,128)(2,1)S(1)}, bf16[3,256,640]{2,1,0:T(8,128)(2,1)}, u32[]{:S(2)}) copy-start(bf16[3,256,640]{2,1,0:T(8,128)(2,1)} %qkv.1) | copy-start | bytes 2949124
  0.0 1.1 %copy-start.4 = (bf16[160,2,512]{2,1,0:T(2,128)(2,1)S(1)}, bf16[160,2,512]{2,1,0:T(2,128)(2,1)}, u32[]{:S(2)}) copy-start(bf16[160,2,512]{2,1,0:T(2,128)(2,1)} %w.1) | copy-start | bytes 983044
  2.5 11.0 %collective-permute-start.4 = (bf16[160,1024]{1,0:T(8,128)(2,1)}, bf16[160,1024]{1,0:T(8,128)(2,1)}, u32[]{:S(2)}, u32[]{:S(2)}) collective-permute-start(bf16[160,1024]{1,0:T(8,128)(2,1)} %shard_map.93.refs_0_), channel_id=1, source_target_pairs={{2,0},{0,4},{4,8},{8,12},{12,14},{14,10},{10,6},{6,2},{3,1},{1,5},... | collective-permute-start | bytes 983048 | tf_op jit(solution)/shard_map/ppermute | solution.py:233
  5.6 9.8 %collective-permute-start.5 = (bf16[160,1024]{1,0:T(8,128)(2,1)}, bf16[160,1024]{1,0:T(8,128)(2,1)}, u32[]{:S(2)}, u32[]{:S(2)}) collective-permute-start(bf16[160,1024]{1,0:T(8,128)(2,1)} %shard_map.93.refs_0_), channel_id=1, source_target_pairs={{0,2},{4,0},{8,4},{12,8},{14,12},{10,14},{6,10},{2,6},{1,3},{5,1},... | collective-permute-start | bytes 983048 | tf_op jit(solution)/shard_map/ppermute | solution.py:233
  5.6 10.0 %collective-permute-start.1 = (bf16[640,1280]{1,0:T(8,128)(2,1)S(1)}, bf16[640,1280]{1,0:T(8,128)(2,1)S(1)}, u32[]{:S(2)}, u32[]{:S(2)}) collective-permute-start(bf16[640,1280]{1,0:T(8,128)(2,1)S(1)} %copy-done), channel_id=1, source_target_pairs={{0,1},{1,0},{2,3},{3,2},{4,5},{5,4},{6,7},{7,6},{8,9},{9,8},{10,11... | collective-permute-start | bytes 4915208 | tf_op jit(solution)/shard_map/ppermute | solution.py:198
  7.5 8.1 %collective-permute-start = (bf16[256,640]{1,0:T(8,128)(2,1)}, bf16[256,640]{1,0:T(8,128)(2,1)}, u32[]{:S(2)}, u32[]{:S(2)}) collective-permute-start(bf16[256,640]{1,0:T(8,128)(2,1)} %shard_map.91.attn_own), channel_id=1, source_target_pairs={{0,1},{1,0},{2,3},{3,2},{4,5},{5,4},{6,7},{7,6},{8,9},{9,8},{10,11... | collective-permute-start | bytes 983048 | tf_op jit(solution)/shard_map/ppermute | solution.py:198
  13.5 13.8 %collective-permute-start.6 = (bf16[160,1024]{1,0:T(8,128)(2,1)}, bf16[160,1024]{1,0:T(8,128)(2,1)}, u32[]{:S(2)}, u32[]{:S(2)}) collective-permute-start(bf16[160,1024]{1,0:T(8,128)(2,1)} %collective-permute-done.4.refs_1_), channel_id=1, source_target_pairs={{2,0},{0,4},{4,8},{8,12},{12,14},{14,10},{10,6},{6,2},{3,1},{1,5},... | collective-permute-start | bytes 983048 | tf_op jit(solution)/shard_map/ppermute | solution.py:233
  15.3 13.6 %collective-permute-start.7 = (bf16[160,1024]{1,0:T(8,128)(2,1)}, bf16[160,1024]{1,0:T(8,128)(2,1)}, u32[]{:S(2)}, u32[]{:S(2)}) collective-permute-start(bf16[160,1024]{1,0:T(8,128)(2,1)} %collective-permute-done.5.refs_2_), channel_id=1, source_target_pairs={{0,2},{4,0},{8,4},{12,8},{14,12},{10,14},{6,10},{2,6},{1,3},{5,1},... | collective-permute-start | bytes 983048 | tf_op jit(solution)/shard_map/ppermute | solution.py:233
  15.5 1.1 %copy-start.3 = (bf16[256,1280]{1,0:T(8,128)(2,1)S(1)}, bf16[256,1280]{1,0:T(8,128)(2,1)}, u32[]{:S(2)}) copy-start(bf16[256,1280]{1,0:T(8,128)(2,1)} %hidden.1) | copy-start | bytes 1966084
  16.6 7.1 %copy-start.9 = (s32[128]{0:T(128)S(1)}, s32[128]{0:T(128)}, u32[]{:S(2)}) copy-start(s32[128]{0:T(128)} %param.11) | copy-start | bytes 1540
  16.6 7.1 %copy-start.8 = (bf16[2,128,512]{2,1,0:T(8,128)(2,1)S(1)}, bf16[2,128,512]{2,1,0:T(8,128)(2,1)}, u32[]{:S(2)}) copy-start(bf16[2,128,512]{2,1,0:T(8,128)(2,1)} %param.10) | copy-start | bytes 786436
  16.6 14.5 %copy-start.10 = (f32[32]{0:T(128)S(1)}, f32[32]{0:T(128)}, u32[]{:S(2)}) copy-start(f32[32]{0:T(128)} %param.17) | copy-start | bytes 388
  19.1 0.8 %copy-start.6 = (bf16[256,1280]{1,0:T(8,128)(2,1)}, bf16[256,1280]{1,0:T(8,128)(2,1)S(1)}, u32[]{:S(2)}) copy-start(bf16[256,1280]{1,0:T(8,128)(2,1)S(1)} %get-tuple-element.11.norm_own) | copy-start | bytes 1966084
  19.9 24.0 %copy-start.7 = (bf16[256,1280]{1,0:T(8,128)(2,1)S(1)}, bf16[256,1280]{1,0:T(8,128)(2,1)}, u32[]{:S(2)}) copy-start(bf16[256,1280]{1,0:T(8,128)(2,1)} %copy-done.6) | copy-start | bytes 1966084
  19.9 11.2 %collective-permute-start.2 = (bf16[128,1280]{1,0:T(8,128)(2,1)S(1)}, bf16[128,1280]{1,0:T(8,128)(2,1)S(1)}, u32[]{:S(2)}, u32[]{:S(2)}) collective-permute-start(bf16[128,1280]{1,0:T(8,128)(2,1)S(1)} %get-tuple-element.12), channel_id=1, source_target_pairs={{0,2},{2,4},{4,6},{6,8},{8,10},{10,12},{12,14},{1,3},{3,5},{5,7},{... | collective-permute-start | bytes 983048 | tf_op jit(solution)/shard_map/ppermute | solution.py:194
  23.8 10.6 %collective-permute-start.10 = (bf16[272,512]{1,0:T(8,128)(2,1)S(1)}, bf16[272,512]{1,0:T(8,128)(2,1)S(1)}, u32[]{:S(2)}, u32[]{:S(2)}) collective-permute-start(bf16[272,512]{1,0:T(8,128)(2,1)S(1)} %pad_maximum_fusion.own), channel_id=1, source_target_pairs={{0,4},{2,6},{4,8},{6,10},{8,12},{10,14},{1,5},{3,7},{5,9},{7,11},{... | collective-permute-start | bytes 835592 | tf_op jit(solution)/shard_map/ppermute | solution.py:194
  27.3 12.2 %collective-permute-start.8 = (bf16[160,1024]{1,0:T(8,128)(2,1)}, bf16[160,1024]{1,0:T(8,128)(2,1)S(1)}, u32[]{:S(2)}, u32[]{:S(2)}) collective-permute-start(bf16[160,1024]{1,0:T(8,128)(2,1)} %collective-permute-done.6.refs_3_), channel_id=1, source_target_pairs={{2,0},{0,4},{4,8},{8,12},{12,14},{14,10},{10,6},{6,2},{3,1},{1,5},... | collective-permute-start | bytes 983048 | tf_op jit(solution)/shard_map/ppermute | solution.py:233
  28.9 13.1 %collective-permute-start.9 = (bf16[160,1024]{1,0:T(8,128)(2,1)}, bf16[160,1024]{1,0:T(8,128)(2,1)S(1)}, u32[]{:S(2)}, u32[]{:S(2)}) collective-permute-start(bf16[160,1024]{1,0:T(8,128)(2,1)} %collective-permute-done.7.refs_4_), channel_id=1, source_target_pairs={{0,2},{4,0},{8,4},{12,8},{14,12},{10,14},{6,10},{2,6},{1,3},{5,1},... | collective-permute-start | bytes 983048 | tf_op jit(solution)/shard_map/ppermute | solution.py:233
  31.1 12.8 %collective-permute-start.3 = (bf16[128,1280]{1,0:T(8,128)(2,1)S(1)}, bf16[128,1280]{1,0:T(8,128)(2,1)S(1)}, u32[]{:S(2)}, u32[]{:S(2)}) collective-permute-start(bf16[128,1280]{1,0:T(8,128)(2,1)S(1)} %collective-permute-done.2.before_mine), channel_id=1, source_target_pairs={{0,1},{1,0},{2,3},{3,2},{4,5},{5,4},{6,7},{7,6},{8,9},{9,8},{10,11... | collective-permute-start | bytes 983048 | tf_op jit(solution)/shard_map/ppermute | solution.py:198
  34.5 13.0 %collective-permute-start.11 = (bf16[272,512]{1,0:T(8,128)(2,1)S(1)}, bf16[272,512]{1,0:T(8,128)(2,1)S(1)}, u32[]{:S(2)}, u32[]{:S(2)}) collective-permute-start(bf16[272,512]{1,0:T(8,128)(2,1)S(1)} %broadcast_select_fusion), channel_id=1, source_target_pairs={{0,2},{2,0},{4,6},{6,4},{8,10},{10,8},{12,14},{14,12},{1,3},{3,1},... | collective-permute-start | bytes 835592 | tf_op jit(solution)/shard_map/ppermute | solution.py:198
  39.5 10.8 %collective-permute-start.12 = (bf16[80,1024]{1,0:T(8,128)(2,1)S(1)}, bf16[80,1024]{1,0:T(8,128)(2,1)S(1)}, u32[]{:S(2)}, u32[]{:S(2)}) collective-permute-start(bf16[80,1024]{1,0:T(8,128)(2,1)S(1)} %slice.8), channel_id=1, source_target_pairs={{2,0},{0,4},{4,8},{8,12},{12,14},{14,10},{10,6},{6,2},{3,1},{1,5},... | collective-permute-start | bytes 491528 | tf_op jit(solution)/shard_map/ppermute | solution.py:233
  42.1 8.2 %collective-permute-start.13 = (bf16[80,1024]{1,0:T(8,128)(2,1)S(1)}, bf16[80,1024]{1,0:T(8,128)(2,1)S(1)}, u32[]{:S(2)}, u32[]{:S(2)}) collective-permute-start(bf16[80,1024]{1,0:T(8,128)(2,1)S(1)} %slice.9), channel_id=1, source_target_pairs={{0,2},{4,0},{8,4},{12,8},{14,12},{10,14},{6,10},{2,6},{1,3},{5,1},... | collective-permute-start | bytes 491528 | tf_op jit(solution)/shard_map/ppermute | solution.py:233
  43.9 3.5 %copy-start.1 = (bf16[128,4096]{1,0:T(8,128)(2,1)S(1)}, bf16[128,4096]{1,0:T(8,128)(2,1)}, u32[]{:S(2)}) copy-start(bf16[128,4096]{1,0:T(8,128)(2,1)} %q.3) | copy-start | bytes 3145732
  47.5 2.9 %copy-start.5 = (s32[128,2]{0,1:T(2,128)S(1)}, s32[128,2]{0,1:T(2,128)}, u32[]{:S(2)}) copy-start(s32[128,2]{0,1:T(2,128)} %param.12) | copy-start | bytes 3076

commit v7 on v6

--- a/solution.py
+++ b/solution.py
@@ -18,7 +18,7 @@
 F32 = jnp.float32
 BF16 = jnp.bfloat16
 PLANNED_FLOPS = 20000000000
-VMEM_LIMIT = 40 * 1024 * 1024
+VMEM_LIMIT = 32 * 1024 * 1024
 
 
 def dot_t(a, b):

time: 54.5 us -> 54.5 us (level)
  no operation moved by 1% of the time
where the time goes in v7:
time: 54.5 us; the launch traced here: 54.2 us
  starting transfers between devices  24.4 us (45%)
  Pallas kernels  15.9 us (29%)
  waiting for transfers between devices  10.5 us (19%)
  local copies, waits for them, and re-layouts  3.27 us (6%)
    pallas_call x6, Pallas kernels, call(): pl.pallas_call(kernel, out_shape=out_shape, in_specs=[pl.BlockSpec(memory...  15.9 us
    ppermute x8, starting transfers between devices, around(): lax.ppermute(block, 'seq', ways[way])  11.5 us
    ppermute x2, starting transfers between devices, shifted(): lax.ppermute(block, axis, [(i, i + distance) for i in range(n - distance)])  7.27 us
    ppermute x8, waiting for transfers between devices, around(): lax.ppermute(block, 'seq', ways[way])  5.57 us
    ppermute x4, starting transfers between devices, flipped(): lax.ppermute(block, axis, [(i, i ^ bits) for i in range(lax.axis_size(axi...  5.56 us
    ppermute x2, waiting for transfers between devices, shifted(): lax.ppermute(block, axis, [(i, i + distance) for i in range(n - distance)])  4.88 us
    unnamed x22, local copies, waits for them, and re-layouts  3.07 us
  transfers between devices with their start and end apart: 14, of which 3 were waited for; matrix products, arithmetic and copies ran while one was open for 0% of the time, Pallas kernels for 20%

profile of v7, /device:TPU:0, one launch (start us, length us, event | category | flops | bytes accessed | tf_op | source)
XLA Modules:
  0.0 54.2 jit_solution(17086519428606152655)
XLA Ops:
  0.0 0.0 copy-start
  0.0 0.0 copy-start.2
  0.0 0.0 copy-start.4
  0.0 1.1 %copy-done.4 = bf16[160,2,512]{2,1,0:T(2,128)(2,1)S(1)} copy-done((bf16[160,2,512]{2,1,0:T(2,128)(2,1)S(1)}, bf16[160,2,512]{2,1,0:T(2,128)(2,1)}, u32[]{:S(2)}) %copy-start.4) | copy-done | bytes 327704
  1.1 1.4 %shard_map.93.refs_0_ = bf16[160,1024]{1,0:T(8,128)(2,1)} custom-call(bf16[160,2,512]{2,1,0:T(2,128)(2,1)S(1)} %copy-done.4), custom_call_target="tpu_custom_call" | custom-call | flops 20000000000 | bytes 655360 | tf_op jit(solution)/shard_map/pallas_call | solution.py:44
  2.5 3.0 %collective-permute-start.4 = (bf16[160,1024]{1,0:T(8,128)(2,1)}, bf16[160,1024]{1,0:T(8,128)(2,1)}, u32[]{:S(2)}, u32[]{:S(2)}) collective-permute-start(bf16[160,1024]{1,0:T(8,128)(2,1)} %shard_map.93.refs_0_), channel_id=1, source_target_pairs={{2,0},{0,4},{4,8},{8,12},{12,14},{14,10},{10,6},{6,2},{3,1},{1,5},... | collective-permute-start | bytes 983048 | tf_op jit(solution)/shard_map/ppermute | solution.py:233
  5.6 0.0 collective-permute-start.5
  5.6 0.0 copy-done
  5.6 0.0 collective-permute-start.1
  5.6 0.0 copy-done.2
  5.6 1.9 %shard_map.91.attn_own = bf16[256,640]{1,0:T(8,128)(2,1)} custom-call(bf16[3,256,640]{2,1,0:T(8,128)(2,1)S(1)} %copy-done.2), custom_call_target="tpu_custom_call" | custom-call | flops 20000000000 | bytes 1310720 | tf_op jit(solution)/shard_map/pallas_call | solution.py:44
  7.5 0.5 collective-permute-start
  8.0 5.5 %collective-permute-done.4.refs_1_ = bf16[160,1024]{1,0:T(8,128)(2,1)} collective-permute-done((bf16[160,1024]{1,0:T(8,128)(2,1)}, bf16[160,1024]{1,0:T(8,128)(2,1)}, u32[]{:S(2)}, u32[]{:S(2)}) %collective-permute-start.4) | collective-permute-done | bytes 327712 | tf_op jit(solution)/shard_map/ppermute | solution.py:233
  13.5 1.8 %collective-permute-start.6 = (bf16[160,1024]{1,0:T(8,128)(2,1)}, bf16[160,1024]{1,0:T(8,128)(2,1)}, u32[]{:S(2)}, u32[]{:S(2)}) collective-permute-start(bf16[160,1024]{1,0:T(8,128)(2,1)} %collective-permute-done.4.refs_1_), channel_id=1, source_target_pairs={{2,0},{0,4},{4,8},{8,12},{12,14},{14,10},{10,6},{6,2},{3,1},{1,5},... | collective-permute-start | bytes 983048 | tf_op jit(solution)/shard_map/ppermute | solution.py:233
  15.3 0.0 collective-permute-done.5.refs_2_
  15.3 0.2 collective-permute-start.7
  15.5 0.0 collective-permute-done.attn_other
  15.5 0.0 collective-permute-done.1.w_other
  15.5 0.0 copy-start.3
  15.6 1.1 %copy-done.3 = bf16[256,1280]{1,0:T(8,128)(2,1)S(1)} copy-done((bf16[256,1280]{1,0:T(8,128)(2,1)S(1)}, bf16[256,1280]{1,0:T(8,128)(2,1)}, u32[]{:S(2)}) %copy-start.3) | copy-done | bytes 655384
  16.6 0.0 copy-start.9
  16.6 0.0 copy-start.8
  16.6 0.0 copy-start.10
  16.6 2.4 %shard_map.92 = (bf16[256,1280]{1,0:T(8,128)(2,1)S(1)}, bf16[128,1280]{1,0:T(8,128)(2,1)S(1)}) custom-call(s32[1]{0:T(128)} %bitcast.1.core, bf16[256,1280]{1,0:T(8,128)(2,1)S(1)} %copy-done.3, bf16[256,640]{1,0:T(8,128)(2,1)} %shard_map.91.attn_own, bf16[256,640]{1,0:T(8,128)(2,1)} %collective-permute-done.attn_other, bf16[640,1280]{1,0:T(8,128)(2,1)S(1)} %copy-done, ...), custom_call_target="tpu_custom_call" | custom-call | flops 20000000000 | bytes 5570564 | tf_op jit(solution)/shard_map/pallas_call | solution.py:44
  19.1 0.0 copy-start.6
  19.1 0.8 %copy-done.6 = bf16[256,1280]{1,0:T(8,128)(2,1)} copy-done((bf16[256,1280]{1,0:T(8,128)(2,1)}, bf16[256,1280]{1,0:T(8,128)(2,1)S(1)}, u32[]{:S(2)}) %copy-start.6) | copy-done | bytes 655384
  19.9 0.0 copy-start.7
  19.9 3.8 %collective-permute-start.2 = (bf16[128,1280]{1,0:T(8,128)(2,1)S(1)}, bf16[128,1280]{1,0:T(8,128)(2,1)S(1)}, u32[]{:S(2)}, u32[]{:S(2)}) collective-permute-start(bf16[128,1280]{1,0:T(8,128)(2,1)S(1)} %get-tuple-element.12), channel_id=1, source_target_pairs={{0,2},{2,4},{4,6},{6,8},{8,10},{10,12},{12,14},{1,3},{3,5},{5,7},{... | collective-permute-start | bytes 983048 | tf_op jit(solution)/shard_map/ppermute | solution.py:194
  23.7 0.0 copy-done.9
  23.8 0.0 copy-done.8
  23.8 3.5 %collective-permute-start.10 = (bf16[272,512]{1,0:T(8,128)(2,1)S(1)}, bf16[272,512]{1,0:T(8,128)(2,1)S(1)}, u32[]{:S(2)}, u32[]{:S(2)}) collective-permute-start(bf16[272,512]{1,0:T(8,128)(2,1)S(1)} %pad_maximum_fusion.own), channel_id=1, source_target_pairs={{0,4},{2,6},{4,8},{6,10},{8,12},{10,14},{1,5},{3,7},{5,9},{7,11},{... | collective-permute-start | bytes 835592 | tf_op jit(solution)/shard_map/ppermute | solution.py:194
  27.3 0.0 collective-permute-done.6.refs_3_
  27.3 1.6 %collective-permute-start.8 = (bf16[160,1024]{1,0:T(8,128)(2,1)}, bf16[160,1024]{1,0:T(8,128)(2,1)S(1)}, u32[]{:S(2)}, u32[]{:S(2)}) collective-permute-start(bf16[160,1024]{1,0:T(8,128)(2,1)} %collective-permute-done.6.refs_3_), channel_id=1, source_target_pairs={{2,0},{0,4},{4,8},{8,12},{12,14},{14,10},{10,6},{6,2},{3,1},{1,5},... | collective-permute-start | bytes 983048 | tf_op jit(solution)/shard_map/ppermute | solution.py:233
  28.9 0.0 collective-permute-done.7.refs_4_
  28.9 0.5 collective-permute-start.9
  29.4 1.7 %collective-permute-done.2.before_mine = bf16[128,1280]{1,0:T(8,128)(2,1)S(1)} collective-permute-done((bf16[128,1280]{1,0:T(8,128)(2,1)S(1)}, bf16[128,1280]{1,0:T(8,128)(2,1)S(1)}, u32[]{:S(2)}, u32[]{:S(2)}) %collective-permute-start.2) | collective-permute-done | bytes 327712 | tf_op jit(solution)/shard_map/ppermute | solution.py:194
  31.1 0.0 collective-permute-start.3
  31.1 0.0 copy-done.10
  31.1 0.1 stack.40.place
  31.2 3.2 %collective-permute-done.10.back2 = bf16[272,512]{1,0:T(8,128)(2,1)S(1)} collective-permute-done((bf16[272,512]{1,0:T(8,128)(2,1)S(1)}, bf16[272,512]{1,0:T(8,128)(2,1)S(1)}, u32[]{:S(2)}, u32[]{:S(2)}) %collective-permute-start.10) | collective-permute-done | bytes 278560 | tf_op jit(solution)/shard_map/ppermute | solution.py:194
  34.4 0.1 broadcast_select_fusion
  34.5 5.1 %collective-permute-start.11 = (bf16[272,512]{1,0:T(8,128)(2,1)S(1)}, bf16[272,512]{1,0:T(8,128)(2,1)S(1)}, u32[]{:S(2)}, u32[]{:S(2)}) collective-permute-start(bf16[272,512]{1,0:T(8,128)(2,1)S(1)} %broadcast_select_fusion), channel_id=1, source_target_pairs={{0,2},{2,0},{4,6},{6,4},{8,10},{10,8},{12,14},{14,12},{1,3},{3,1},... | collective-permute-start | bytes 835592 | tf_op jit(solution)/shard_map/ppermute | solution.py:198
  39.5 0.0 collective-permute-done.8.refs_5_
  39.5 2.5 %collective-permute-start.12 = (bf16[80,1024]{1,0:T(8,128)(2,1)S(1)}, bf16[80,1024]{1,0:T(8,128)(2,1)S(1)}, u32[]{:S(2)}, u32[]{:S(2)}) collective-permute-start(bf16[80,1024]{1,0:T(8,128)(2,1)S(1)} %slice.8), channel_id=1, source_target_pairs={{2,0},{0,4},{4,8},{8,12},{12,14},{14,10},{10,6},{6,2},{3,1},{1,5},... | collective-permute-start | bytes 491528 | tf_op jit(solution)/shard_map/ppermute | solution.py:233
  42.1 0.0 collective-permute-done.9.refs_6_
  42.1 1.9 %collective-permute-start.13 = (bf16[80,1024]{1,0:T(8,128)(2,1)S(1)}, bf16[80,1024]{1,0:T(8,128)(2,1)S(1)}, u32[]{:S(2)}, u32[]{:S(2)}) collective-permute-start(bf16[80,1024]{1,0:T(8,128)(2,1)S(1)} %slice.9), channel_id=1, source_target_pairs={{0,2},{4,0},{8,4},{12,8},{14,12},{10,14},{6,10},{2,6},{1,3},{5,1},... | collective-permute-start | bytes 491528 | tf_op jit(solution)/shard_map/ppermute | solution.py:233
  43.9 0.0 collective-permute-done.3.before_other
  43.9 0.0 copy-done.7
  43.9 0.0 copy-start.1
  43.9 3.5 %shard_map.94 = (f32[512,1024]{1,0:T(8,128)S(1)}, bf16[512,160]{1,0:T(8,128)(2,1)S(1)}) custom-call(s32[10]{0:T(128)S(1)} %stack.40.place, bf16[256,1280]{1,0:T(8,128)(2,1)S(1)} %copy-done.7, bf16[128,1280]{1,0:T(8,128)(2,1)S(1)} %collective-permute-done.2.before_mine, bf16[128,1280]{1,0:T(8,128)(2,1)S(1)} %collective-permute-done.3.before_other, ...), custom_call_target="tpu_custom_call" | custom-call | flops 20000000000 | bytes 5865512 | tf_op jit(solution)/shard_map/pallas_call | solution.py:44
  47.5 0.0 copy-start.5
  47.5 0.0 collective-permute-done.11.back1
  47.5 0.0 copy-done.1
  47.5 2.8 %shard_map.95.self_out = f32[128,4096]{1,0:T(8,128)S(1)} custom-call(s32[1]{0:T(128)} %bitcast.seq, bf16[128,4096]{1,0:T(8,128)(2,1)S(1)} %copy-done.1, bf16[272,512]{1,0:T(8,128)(2,1)S(1)} %pad_maximum_fusion.own, bf16[272,512]{1,0:T(8,128)(2,1)S(1)} %collective-permute-done.11.back1, bf16[272,512]{1,0:T(8,128)(2,1)S(1)} %collective-permute-done.10.back2), custom_call_target="tpu_custom_call" | custom-call | flops 20000000000 | bytes 3981316 | tf_op jit(solution)/shard_map/pallas_call | solution.py:44
  50.3 0.0 collective-permute-done.12.refs_1_
  50.3 0.0 collective-permute-done.13.refs_2_
  50.3 0.1 broadcast_in_dim.4
  50.4 0.0 copy-done.5
  50.4 3.8 %shard_map.96 = bf16[128,4096]{1,0:T(8,128)(2,1)} custom-call(s32[1]{0:T(128)} %bitcast.seq, bf16[128,4096]{1,0:T(8,128)(2,1)S(1)} %copy-done.1, f32[128,4096]{1,0:T(8,128)S(1)} %shard_map.95.self_out, s32[2,128]{1,0:T(2,128)S(1)} %bitcast.14, f32[1,4096]{1,0:T(1,128)S(1)} %bitcast.13, f32[512,1024]{1,0:T(8,128)S(1)} %get-tuple-element.15.total, ...), custom_call_target="tpu_custom_call" | custom-call | flops 20000000000 | bytes 6800388 | tf_op jit(solution)/shard_map/pallas_call | solution.py:44
  (7 shorter events, 0.1 us)
Async XLA Ops:
  0.0 5.6 %copy-start = (bf16[640,1280]{1,0:T(8,128)(2,1)S(1)}, bf16[640,1280]{1,0:T(8,128)(2,1)}, u32[]{:S(2)}) copy-start(bf16[640,1280]{1,0:T(8,128)(2,1)} %w_own.1) | copy-start | bytes 4915204
  0.0 5.6 %copy-start.2 = (bf16[3,256,640]{2,1,0:T(8,128)(2,1)S(1)}, bf16[3,256,640]{2,1,0:T(8,128)(2,1)}, u32[]{:S(2)}) copy-start(bf16[3,256,640]{2,1,0:T(8,128)(2,1)} %qkv.1) | copy-start | bytes 2949124
  0.0 1.1 %copy-start.4 = (bf16[160,2,512]{2,1,0:T(2,128)(2,1)S(1)}, bf16[160,2,512]{2,1,0:T(2,128)(2,1)}, u32[]{:S(2)}) copy-start(bf16[160,2,512]{2,1,0:T(2,128)(2,1)} %w.1) | copy-start | bytes 983044
  2.5 11.0 %collective-permute-start.4 = (bf16[160,1024]{1,0:T(8,128)(2,1)}, bf16[160,1024]{1,0:T(8,128)(2,1)}, u32[]{:S(2)}, u32[]{:S(2)}) collective-permute-start(bf16[160,1024]{1,0:T(8,128)(2,1)} %shard_map.93.refs_0_), channel_id=1, source_target_pairs={{2,0},{0,4},{4,8},{8,12},{12,14},{14,10},{10,6},{6,2},{3,1},{1,5},... | collective-permute-start | bytes 983048 | tf_op jit(solution)/shard_map/ppermute | solution.py:233
  5.6 9.8 %collective-permute-start.5 = (bf16[160,1024]{1,0:T(8,128)(2,1)}, bf16[160,1024]{1,0:T(8,128)(2,1)}, u32[]{:S(2)}, u32[]{:S(2)}) collective-permute-start(bf16[160,1024]{1,0:T(8,128)(2,1)} %shard_map.93.refs_0_), channel_id=1, source_target_pairs={{0,2},{4,0},{8,4},{12,8},{14,12},{10,14},{6,10},{2,6},{1,3},{5,1},... | collective-permute-start | bytes 983048 | tf_op jit(solution)/shard_map/ppermute | solution.py:233
  5.6 10.0 %collective-permute-start.1 = (bf16[640,1280]{1,0:T(8,128)(2,1)S(1)}, bf16[640,1280]{1,0:T(8,128)(2,1)S(1)}, u32[]{:S(2)}, u32[]{:S(2)}) collective-permute-start(bf16[640,1280]{1,0:T(8,128)(2,1)S(1)} %copy-done), channel_id=1, source_target_pairs={{0,1},{1,0},{2,3},{3,2},{4,5},{5,4},{6,7},{7,6},{8,9},{9,8},{10,11... | collective-permute-start | bytes 4915208 | tf_op jit(solution)/shard_map/ppermute | solution.py:198
  7.5 8.1 %collective-permute-start = (bf16[256,640]{1,0:T(8,128)(2,1)}, bf16[256,640]{1,0:T(8,128)(2,1)}, u32[]{:S(2)}, u32[]{:S(2)}) collective-permute-start(bf16[256,640]{1,0:T(8,128)(2,1)} %shard_map.91.attn_own), channel_id=1, source_target_pairs={{0,1},{1,0},{2,3},{3,2},{4,5},{5,4},{6,7},{7,6},{8,9},{9,8},{10,11... | collective-permute-start | bytes 983048 | tf_op jit(solution)/shard_map/ppermute | solution.py:198
  13.5 13.8 %collective-permute-start.6 = (bf16[160,1024]{1,0:T(8,128)(2,1)}, bf16[160,1024]{1,0:T(8,128)(2,1)}, u32[]{:S(2)}, u32[]{:S(2)}) collective-permute-start(bf16[160,1024]{1,0:T(8,128)(2,1)} %collective-permute-done.4.refs_1_), channel_id=1, source_target_pairs={{2,0},{0,4},{4,8},{8,12},{12,14},{14,10},{10,6},{6,2},{3,1},{1,5},... | collective-permute-start | bytes 983048 | tf_op jit(solution)/shard_map/ppermute | solution.py:233
  15.3 13.6 %collective-permute-start.7 = (bf16[160,1024]{1,0:T(8,128)(2,1)}, bf16[160,1024]{1,0:T(8,128)(2,1)}, u32[]{:S(2)}, u32[]{:S(2)}) collective-permute-start(bf16[160,1024]{1,0:T(8,128)(2,1)} %collective-permute-done.5.refs_2_), channel_id=1, source_target_pairs={{0,2},{4,0},{8,4},{12,8},{14,12},{10,14},{6,10},{2,6},{1,3},{5,1},... | collective-permute-start | bytes 983048 | tf_op jit(solution)/shard_map/ppermute | solution.py:233
  15.5 1.1 %copy-start.3 = (bf16[256,1280]{1,0:T(8,128)(2,1)S(1)}, bf16[256,1280]{1,0:T(8,128)(2,1)}, u32[]{:S(2)}) copy-start(bf16[256,1280]{1,0:T(8,128)(2,1)} %hidden.1) | copy-start | bytes 1966084
  16.6 7.1 %copy-start.9 = (s32[128]{0:T(128)S(1)}, s32[128]{0:T(128)}, u32[]{:S(2)}) copy-start(s32[128]{0:T(128)} %param.11) | copy-start | bytes 1540
  16.6 7.1 %copy-start.8 = (bf16[2,128,512]{2,1,0:T(8,128)(2,1)S(1)}, bf16[2,128,512]{2,1,0:T(8,128)(2,1)}, u32[]{:S(2)}) copy-start(bf16[2,128,512]{2,1,0:T(8,128)(2,1)} %param.10) | copy-start | bytes 786436
  16.6 14.5 %copy-start.10 = (f32[32]{0:T(128)S(1)}, f32[32]{0:T(128)}, u32[]{:S(2)}) copy-start(f32[32]{0:T(128)} %param.17) | copy-start | bytes 388
  19.1 0.8 %copy-start.6 = (bf16[256,1280]{1,0:T(8,128)(2,1)}, bf16[256,1280]{1,0:T(8,128)(2,1)S(1)}, u32[]{:S(2)}) copy-start(bf16[256,1280]{1,0:T(8,128)(2,1)S(1)} %get-tuple-element.11.norm_own) | copy-start | bytes 1966084
  19.9 24.0 %copy-start.7 = (bf16[256,1280]{1,0:T(8,128)(2,1)S(1)}, bf16[256,1280]{1,0:T(8,128)(2,1)}, u32[]{:S(2)}) copy-start(bf16[256,1280]{1,0:T(8,128)(2,1)} %copy-done.6) | copy-start | bytes 1966084
  19.9 11.2 %collective-permute-start.2 = (bf16[128,1280]{1,0:T(8,128)(2,1)S(1)}, bf16[128,1280]{1,0:T(8,128)(2,1)S(1)}, u32[]{:S(2)}, u32[]{:S(2)}) collective-permute-start(bf16[128,1280]{1,0:T(8,128)(2,1)S(1)} %get-tuple-element.12), channel_id=1, source_target_pairs={{0,2},{2,4},{4,6},{6,8},{8,10},{10,12},{12,14},{1,3},{3,5},{5,7},{... | collective-permute-start | bytes 983048 | tf_op jit(solution)/shard_map/ppermute | solution.py:194
  23.8 10.6 %collective-permute-start.10 = (bf16[272,512]{1,0:T(8,128)(2,1)S(1)}, bf16[272,512]{1,0:T(8,128)(2,1)S(1)}, u32[]{:S(2)}, u32[]{:S(2)}) collective-permute-start(bf16[272,512]{1,0:T(8,128)(2,1)S(1)} %pad_maximum_fusion.own), channel_id=1, source_target_pairs={{0,4},{2,6},{4,8},{6,10},{8,12},{10,14},{1,5},{3,7},{5,9},{7,11},{... | collective-permute-start | bytes 835592 | tf_op jit(solution)/shard_map/ppermute | solution.py:194
  27.3 12.2 %collective-permute-start.8 = (bf16[160,1024]{1,0:T(8,128)(2,1)}, bf16[160,1024]{1,0:T(8,128)(2,1)S(1)}, u32[]{:S(2)}, u32[]{:S(2)}) collective-permute-start(bf16[160,1024]{1,0:T(8,128)(2,1)} %collective-permute-done.6.refs_3_), channel_id=1, source_target_pairs={{2,0},{0,4},{4,8},{8,12},{12,14},{14,10},{10,6},{6,2},{3,1},{1,5},... | collective-permute-start | bytes 983048 | tf_op jit(solution)/shard_map/ppermute | solution.py:233
  28.9 13.1 %collective-permute-start.9 = (bf16[160,1024]{1,0:T(8,128)(2,1)}, bf16[160,1024]{1,0:T(8,128)(2,1)S(1)}, u32[]{:S(2)}, u32[]{:S(2)}) collective-permute-start(bf16[160,1024]{1,0:T(8,128)(2,1)} %collective-permute-done.7.refs_4_), channel_id=1, source_target_pairs={{0,2},{4,0},{8,4},{12,8},{14,12},{10,14},{6,10},{2,6},{1,3},{5,1},... | collective-permute-start | bytes 983048 | tf_op jit(solution)/shard_map/ppermute | solution.py:233
  31.1 12.8 %collective-permute-start.3 = (bf16[128,1280]{1,0:T(8,128)(2,1)S(1)}, bf16[128,1280]{1,0:T(8,128)(2,1)S(1)}, u32[]{:S(2)}, u32[]{:S(2)}) collective-permute-start(bf16[128,1280]{1,0:T(8,128)(2,1)S(1)} %collective-permute-done.2.before_mine), channel_id=1, source_target_pairs={{0,1},{1,0},{2,3},{3,2},{4,5},{5,4},{6,7},{7,6},{8,9},{9,8},{10,11... | collective-permute-start | bytes 983048 | tf_op jit(solution)/shard_map/ppermute | solution.py:198
  34.5 13.0 %collective-permute-start.11 = (bf16[272,512]{1,0:T(8,128)(2,1)S(1)}, bf16[272,512]{1,0:T(8,128)(2,1)S(1)}, u32[]{:S(2)}, u32[]{:S(2)}) collective-permute-start(bf16[272,512]{1,0:T(8,128)(2,1)S(1)} %broadcast_select_fusion), channel_id=1, source_target_pairs={{0,2},{2,0},{4,6},{6,4},{8,10},{10,8},{12,14},{14,12},{1,3},{3,1},... | collective-permute-start | bytes 835592 | tf_op jit(solution)/shard_map/ppermute | solution.py:198
  39.5 10.8 %collective-permute-start.12 = (bf16[80,1024]{1,0:T(8,128)(2,1)S(1)}, bf16[80,1024]{1,0:T(8,128)(2,1)S(1)}, u32[]{:S(2)}, u32[]{:S(2)}) collective-permute-start(bf16[80,1024]{1,0:T(8,128)(2,1)S(1)} %slice.8), channel_id=1, source_target_pairs={{2,0},{0,4},{4,8},{8,12},{12,14},{14,10},{10,6},{6,2},{3,1},{1,5},... | collective-permute-start | bytes 491528 | tf_op jit(solution)/shard_map/ppermute | solution.py:233
  42.1 8.2 %collective-permute-start.13 = (bf16[80,1024]{1,0:T(8,128)(2,1)S(1)}, bf16[80,1024]{1,0:T(8,128)(2,1)S(1)}, u32[]{:S(2)}, u32[]{:S(2)}) collective-permute-start(bf16[80,1024]{1,0:T(8,128)(2,1)S(1)} %slice.9), channel_id=1, source_target_pairs={{0,2},{4,0},{8,4},{12,8},{14,12},{10,14},{6,10},{2,6},{1,3},{5,1},... | collective-permute-start | bytes 491528 | tf_op jit(solution)/shard_map/ppermute | solution.py:233
  43.9 3.5 %copy-start.1 = (bf16[128,4096]{1,0:T(8,128)(2,1)S(1)}, bf16[128,4096]{1,0:T(8,128)(2,1)}, u32[]{:S(2)}) copy-start(bf16[128,4096]{1,0:T(8,128)(2,1)} %q.3) | copy-start | bytes 3145732
  47.5 2.9 %copy-start.5 = (s32[128,2]{0,1:T(2,128)S(1)}, s32[128,2]{0,1:T(2,128)}, u32[]{:S(2)}) copy-start(s32[128,2]{0,1:T(2,128)} %param.12) | copy-start | bytes 3076
